TPU v7x, 256 devices: a whole 4x4x8 slice. The times are simulated.
256 devices in a mesh: blk: 32 (over x_lo, z, core), rep: 8 (over x_hi, y).
Axes of the slice: x: 4 (x_hi: 2, x_lo: 2; x = x_hi * 2 + x_lo), y: 4, z: 8, core: 2. Of those that a mesh axis runs over, the one named last changes fastest.
Arguments:
- node_features: bfloat16 [65536, 128], P(('blk', 'rep')), may hold values from -6 to 6
- weight_matrix: bfloat16 [128, 512], replicated, may hold values from -0.5 to 0.5
- bias_vector: float32 [512], replicated, may hold values from -3 to 3
- node_degree: int32 [65536], P(('blk', 'rep')), may hold values from 4 to 64, as said below
- tile_values: bfloat16 [32, 8, 64, 2, 128, 128], P('blk', 'rep'), may hold values from 0 to 1
- tile_row: int32 [32, 8, 64, 2], P('blk', 'rep'), may hold values from 0 to 15
- tile_count: int32 [32, 8, 64], P('blk', 'rep'), may hold values from 1 to 2
- cotangent: bfloat16 [65536, 512], P(('blk', 'rep')), may hold values from -6 to 6
Outputs:
- hidden_out: bfloat16 [65536, 512], P(('blk', 'rep'))
- weight_grad: float32 [128, 512], replicated
- input_grad: bfloat16 [65536, 128], P(('blk', 'rep'))
Inputs may be any that keep to these rules, and one draw needn't show every extreme that they name: `tile_row`: row tile of a slot, within the 2048 rows of its group. `tile_count`: number of live slots of a column tile; slots at or past it are ignored. `node_degree`: degree of a node, one of 4, 16 and 64.
All inputs are finite; a program needn't handle non-finite values.
Results may differ from a plain program's by a relative error of at most 0.0027.
Values may be sent and summed in bfloat16 or wider, within the bound.
No kernel may reach another device: no remote copies, remote signals or barrier semaphores. Data moves between devices by JAX's collectives and lax.ppermute only.
A program may use at most 128 MiB of HBM per device.

v0:
```python
import math

import jax
import jax.numpy as jnp
from jax import lax
from jax.sharding import PartitionSpec as P

exact_mode = lax.Precision.HIGHEST


def gelu_tanh(values):
    return jax.nn.gelu(values, approximate=True)


def alive_mask(slot_rows, live_slots):
    slot_ids = lax.broadcasted_iota(jnp.int32, slot_rows.shape, 1)
    return slot_ids < live_slots[:, None]


def tile_product(tile_block, slot_rows, live_slots, column_part, row_tiles):
    products = jnp.einsum(
        "kscj,kjf->kscf", tile_block, column_part, preferred_element_type=jnp.float32
    )
    alive = alive_mask(slot_rows, live_slots)
    products = jnp.where(alive[:, :, None, None], products, 0.0)
    count, slots, side, col_width = products.shape
    placed = jnp.zeros((row_tiles, side, col_width), jnp.float32)
    placed = placed.at[slot_rows.reshape(-1)].add(products.reshape(count * slots, side, col_width))
    return placed.reshape(row_tiles * side, col_width)


def column_terms(tile_values, tile_row, tile_count, incoming, row_tiles):
    tile_side = tile_values.shape[-1]
    length, col_width = incoming.shape
    tile_total = length // tile_side
    group_len = max(4, tile_total // 8)
    running = jnp.zeros((row_tiles * tile_side, col_width), jnp.float32)
    for offset_tile in range(0, tile_total, group_len):
        span_len = min(group_len, tile_total - offset_tile)
        tile_block = lax.dynamic_slice_in_dim(tile_values, offset_tile, span_len, 0)
        slot_rows = lax.dynamic_slice_in_dim(tile_row, offset_tile, span_len, 0)
        live_slots = lax.dynamic_slice_in_dim(tile_count, offset_tile, span_len, 0)
        column_part = incoming[
            offset_tile * tile_side : (offset_tile + span_len) * tile_side
        ].reshape(span_len, tile_side, col_width)
        running = running + tile_product(tile_block, slot_rows, live_slots, column_part, row_tiles)
    return running


def column_spread(tile_values, tile_row, tile_count, group_grads, span):
    tile_side = tile_values.shape[-1]
    col_width = group_grads.shape[-1]
    row_tiles = group_grads.shape[0] // tile_side
    grouped = group_grads.reshape(row_tiles, tile_side, col_width)
    tile_total = span // tile_side
    group_len = max(4, tile_total // 8)
    pieces_out = []
    for offset_tile in range(0, tile_total, group_len):
        span_len = min(group_len, tile_total - offset_tile)
        tile_block = lax.dynamic_slice_in_dim(tile_values, offset_tile, span_len, 0)
        slot_rows = lax.dynamic_slice_in_dim(tile_row, offset_tile, span_len, 0)
        live_slots = lax.dynamic_slice_in_dim(tile_count, offset_tile, span_len, 0)
        alive = alive_mask(slot_rows, live_slots)
        picked = jnp.where(
            alive[:, :, None, None], grouped[slot_rows], jnp.zeros((), grouped.dtype)
        )
        terms = jnp.einsum(
            "kscj,kscf->kjf", tile_block.astype(jnp.float32), picked, precision=exact_mode
        )
        pieces_out.append(terms.reshape(span_len * tile_side, col_width))
    return jnp.concatenate(pieces_out, 0)


def per_device(
    node_features,
    weight_matrix,
    bias_vector,
    node_degree,
    tile_values,
    tile_row,
    tile_count,
    cotangent,
):
    tile_values = tile_values[0, 0]
    tile_row = tile_row[0, 0]
    tile_count = tile_count[0, 0]
    own_rows = node_features.shape[0]
    tile_side = tile_values.shape[-1]
    replicas = lax.axis_size("rep")
    row_tiles = replicas * own_rows // tile_side
    node_total = own_rows * replicas * lax.axis_size("blk")
    weight_wide = weight_matrix.astype(jnp.float32)
    row_scale = 1.0 / jnp.sqrt(node_degree.astype(jnp.float32))
    scaled_in = (node_features.astype(jnp.float32) * row_scale[:, None]).astype(jnp.bfloat16)
    partial_value = column_terms(
        tile_values,
        tile_row,
        tile_count,
        lax.all_gather(scaled_in, "blk", axis=0, tiled=True),
        row_tiles,
    )
    summed = lax.psum_scatter(partial_value, "rep", scatter_dimension=0, tiled=True)
    mixed = jnp.dot(summed, weight_wide, precision=exact_mode)
    pre_act = row_scale[:, None] * mixed + bias_vector[None, :]
    activated, pullback = jax.vjp(gelu_tanh, pre_act)
    pre_grad = pullback(cotangent.astype(jnp.float32))[0]
    local_grad = jnp.dot(node_features.astype(jnp.float32).T, pre_grad, precision=exact_mode)
    weight_grad = lax.psum(local_grad, ("blk", "rep")) * (1.0 / math.sqrt(node_total))
    back_rows = row_scale[:, None] * pre_grad
    group_grads = lax.all_gather(back_rows, "rep", axis=0, tiled=True)
    returned = lax.psum_scatter(
        column_spread(
            tile_values, tile_row, tile_count, group_grads, own_rows * lax.axis_size("blk")
        ),
        "blk",
        scatter_dimension=0,
        tiled=True,
    )
    input_grad = jnp.dot(row_scale[:, None] * returned, weight_wide.T, precision=exact_mode)
    return (activated.astype(jnp.bfloat16), weight_grad, input_grad.astype(jnp.bfloat16))


def solution(mesh):
    in_specs = (
        P(("blk", "rep"), None),
        P(),
        P(),
        P(("blk", "rep")),
        P("blk", "rep", None, None, None, None),
        P("blk", "rep", None, None),
        P("blk", "rep", None),
        P(("blk", "rep"), None),
    )
    out_specs = (P(("blk", "rep"), None), P(), P(("blk", "rep"), None))
    return jax.shard_map(
        per_device, mesh=mesh, in_specs=in_specs, out_specs=out_specs, check_vma=False
    )
```

profile of v0, /device:TPU:32, one launch (start us, length us, event | category | flops | bytes accessed | tf_op | source)
XLA Modules:
  0.0 680.5 jit_solution(12609042886615589437)
XLA Ops:
  19.2 57.8 %all-gather.3.cloned.1.call-done = bf16[8192,128]{1,0:T(8,128)(2,1)} async-done(((bf16[256,128]{1,0:T(8,128)(2,1)}), bf16[8192,128]{1,0:T(8,128)(2,1)}) %all-gather.3.cloned.1.call-update) | async-done | bytes 2097168 | tf_op jit(solution)/shard_map/all_gather | solution.py:99
  77.0 2.4 fusion.93
  100.4 2.1 scatter_fusion
  102.6 2.6 scatter_fusion.1
  105.4 2.6 scatter_fusion.2
  108.1 1.6 scatter_fusion.3
  109.9 2.6 scatter_fusion.4
  112.7 1.6 scatter_fusion.5
  114.4 2.6 scatter_fusion.6
  117.2 1.6 scatter_fusion.7
  120.0 77.5 %reduce-scatter.3.cloned.1.call-done = f32[256,128]{1,0:T(8,128)} async-done(((f32[2048,128]{1,0:T(8,128)}), f32[256,128]{1,0:T(8,128)}) %reduce-scatter.3.cloned.1.call-update) | async-done | bytes 131088 | tf_op jit(solution)/shard_map/reduce_scatter | solution.py:102
  197.5 2.7 broadcast_multiply_fusion
  203.6 72.4 %all-gather.5.cloned.1.call-done = f32[2048,512]{1,0:T(8,128)} async-done(((f32[256,512]{1,0:T(8,128)}), f32[2048,512]{1,0:T(8,128)}) %all-gather.5.cloned.1.call-update) | async-done | bytes 4194320 | tf_op jit(solution)/shard_map/all_gather | solution.py:110
  276.0 4.9 gather_fusion
  280.9 4.3 fusion.14
  286.7 5.0 gather_fusion.1
  291.7 4.3 fusion.12
  296.0 5.0 gather_fusion.2
  301.1 5.7 fusion.10
  306.8 5.0 gather_fusion.3
  311.8 5.6 fusion.8
  317.4 5.0 gather_fusion.4
  322.4 5.6 fusion.6
  328.1 5.2 gather_fusion.5
  333.3 5.6 fusion.4
  338.9 5.0 gather_fusion.6
  343.9 5.6 fusion.2
  349.5 5.0 gather_fusion.7
  354.5 4.4 fusion
  369.6 159.2 %all-reduce.2.cloned.1.call-done = f32[128,512]{0,1:T(8,128)} async-done(((f32[128,512]{0,1:T(8,128)}), f32[128,512]{0,1:T(8,128)}) %all-reduce.2.cloned.1.call-update) | async-done | bytes 262160 | tf_op jit(solution)/shard_map/psum | solution.py:108
  530.6 141.0 %reduce-scatter.5.cloned.1.call-done = f32[256,512]{1,0:T(8,128)} async-done(((f32[8192,512]{1,0:T(8,128)}), f32[256,512]{1,0:T(8,128)}) %reduce-scatter.5.cloned.1.call-update) | async-done | bytes 524304 | tf_op jit(solution)/shard_map/reduce_scatter | solution.py:111
  671.6 2.1 convolution_convert_fusion
  (155 shorter events, 52.1 us)
Async XLA Ops:
  7.2 190.3 %copy-start = (bf16[128,512]{1,0:T(8,128)(2,1)S(1)}, bf16[128,512]{1,0:T(8,128)(2,1)}, u32[]{:S(2)}) copy-start(bf16[128,512]{1,0:T(8,128)(2,1)} %param.9) | copy-start | bytes 393220
  7.2 69.8 %all-gather.3.cloned.1.call-start = ((), (), s32[]{:S(2)}) async-start(), calls=%async_computation.2 | async-start | bytes 2162688 | tf_op jit(solution)/shard_map/all_gather | solution.py:99
  10.1 187.4 %reduce-scatter.3.cloned.1.call-start = ((), (), s32[]{:S(2)}) async-start(), calls=%async_computation.3 | async-start | bytes 1179648 | tf_op jit(solution)/shard_map/reduce_scatter | solution.py:102
  18.4 62.4 %copy-start.14 = (pred[8,2]{1,0:T(8,128)(4,1)}, pred[8,2]{1,0:T(8,128)(4,1)S(1)}, u32[]{:S(2)}) copy-start(pred[8,2]{1,0:T(8,128)(4,1)S(1)} %get-tuple-element.51) | copy-start | bytes 52
  94.9 5.5 copy-start.25
  97.6 5.0 copy-start.24
  102.5 2.9 copy-start.23
  105.2 2.9 copy-start.22
  105.4 2.7 copy-start.8
  108.0 1.9 copy-start.21
  109.8 2.9 copy-start.20
  109.9 2.7 copy-start.7
  112.5 1.9 copy-start.19
  114.3 2.9 copy-start.18
  114.4 2.8 copy-start.6
  117.1 80.4 %copy-start.17 = (f32[256]{0:T(256)S(1)}, f32[256]{0:T(256)}, u32[]{:S(2)}) copy-start(f32[256]{0:T(256)} %copy-done.16) | copy-start | bytes 3076
  117.1 80.4 %copy-start.27 = (f32[512]{0:T(512)S(1)}, f32[512]{0:T(512)}, u32[]{:S(2)}) copy-start(f32[512]{0:T(512)} %param.10) | copy-start | bytes 6148
  118.8 81.4 %copy-start.9 = (s32[1,1,64,2]{2,3,1,0:T(2,128)S(1)}, s32[1,1,64,2]{2,3,1,0:T(2,128)}, u32[]{:S(2)}) copy-start(s32[1,1,64,2]{2,3,1,0:T(2,128)} %param.13) | copy-start | bytes 1540
  118.8 82.9 %copy-start.10 = (bf16[256,128]{1,0:T(8,128)(2,1)S(1)}, bf16[256,128]{1,0:T(8,128)(2,1)}, u32[]{:S(2)}) copy-start(bf16[256,128]{1,0:T(8,128)(2,1)} %param.8) | copy-start | bytes 196612
  118.8 82.9 %copy-start.26 = (bf16[256,512]{1,0:T(8,128)(2,1)S(1)}, bf16[256,512]{1,0:T(8,128)(2,1)}, u32[]{:S(2)}) copy-start(bf16[256,512]{1,0:T(8,128)(2,1)} %param.15) | copy-start | bytes 786436
  120.0 156.0 %all-gather.5.cloned.1.call-start = ((), (), s32[]{:S(2)}) async-start(), calls=%async_computation.5 | async-start | bytes 4718592 | tf_op jit(solution)/shard_map/all_gather | solution.py:110
  200.2 328.6 %all-reduce.2.cloned.1.call-start = ((), (), s32[]{:S(2)}) async-start(), calls=%async_computation.4 | async-start | bytes 524288 | tf_op jit(solution)/shard_map/psum | solution.py:108
  203.4 468.3 %reduce-scatter.5.cloned.1.call-start = ((), (), s32[]{:S(2)}) async-start(), calls=%async_computation.6 | async-start | bytes 17301504 | tf_op jit(solution)/shard_map/reduce_scatter | solution.py:111
  276.0 4.9 copy-start.15
  286.7 5.0 copy-start.13
  296.0 5.0 copy-start.12
  306.8 5.0 copy-start.11
  354.5 5.9 copy-start.1
  358.9 3.0 copy-start.2
  360.4 3.1 copy-start.3
  361.9 3.1 copy-start.4
  363.5 3.1 copy-start.5
  (1 other events, 0.6 us)
Sparse Core Ops, SparseCore 0:
  10.4 66.5 all-gather.2
  120.1 77.3 reduce-scatter.2
  200.5 75.4 all-gather.4
  282.8 245.9 all-reduce.1
  531.4 140.2 reduce-scatter.4
where the time goes:
time: 691 us; the launch traced here: 681 us
  waiting for transfers between devices  508 us (74%)
  local copies, waits for them, and re-layouts  71 us (10%)
  matrix products  58.7 us (8%)
  other arithmetic  27.8 us (4%)
  between operations  14.6 us (2%)
    psum x1, waiting for transfers between devices, per_device(): lax.psum(local_grad, ('blk', 'rep')) * (1.0 / math.sqrt(node_total))  159 us
    reduce_scatter x1, waiting for transfers between devices, per_device(): lax.psum_scatter(column_spread(tile_values, tile_row, tile_count, group_g...  141 us
    reduce_scatter x1, waiting for transfers between devices, per_device(): lax.psum_scatter(partial_value, 'rep', scatter_dimension=0, tiled=True)  77.5 us
    all_gather x1, waiting for transfers between devices, per_device(): group_grads = lax.all_gather(back_rows, 'rep', axis=0, tiled=True)  72.4 us
    all_gather x1, waiting for transfers between devices, per_device(): lax.all_gather(scaled_in, 'blk', axis=0, tiled=True)  57.8 us
    dot_general x8, matrix products, column_spread(): jnp.einsum('kscj,kscf->kjf', tile_block.astype(jnp.float32), picked, prec...  41.1 us
    gather x8, local copies, waits for them, and re-layouts, column_spread(): grouped[slot_rows]  40.2 us
    scatter-add x8, other arithmetic, tile_product(): placed.at[slot_rows.reshape(-1)]  17.3 us
  transfers between devices with their start and end apart: 5, of which 5 were waited for; matrix products, arithmetic and copies ran while one was open for 16% of the time, Pallas kernels for 0%

commit v1 on v0

v1 whole, which is shorter than its diff:
```python
import functools

import jax
import jax.numpy as jnp
from jax import lax
from jax.experimental import pallas as pl
from jax.experimental.pallas import tpu as pltpu
from jax.sharding import PartitionSpec as P

f32, bf16, f16 = jnp.float32, jnp.bfloat16, jnp.float16

TILE = 128
OWN = 256
BLOCK = OWN + 16
N_X, N_Z, N_C = 2, 8, 2
N_Y = 4
SLOTS = 2
ROW_TILES = 16
VMEM_LIMIT = 40 * 1024 * 1024
DISTANCES = (1, 2, 3)


def blk_index(x, z, c):
    return (x * N_Z + z) * N_C + c


def permute_blk(value, move):
    pairs = []
    for x in range(N_X):
        for z in range(N_Z):
            for c in range(N_C):
                pairs.append((blk_index(x, z, c), blk_index(*move(x, z, c))))
    return lax.ppermute(value, "blk", pairs)


def to_core(x, z, c):
    return x, z, 1 - c


def to_x(x, z, c):
    return 1 - x, z, c


def to_z(distance):
    return lambda x, z, c: (x, (z + distance) % N_Z, c)


def to_z_by_core(distance):
    return lambda x, z, c: (x, (z + (distance if c == 0 else -distance)) % N_Z, c)


def to_z_xor(bit):
    return lambda x, z, c: (x, z ^ bit, c)


def exponent_above(largest):
    return jnp.ceil(jnp.log2(jnp.maximum(largest, 1e-30))) + 1.0


def as_column(row):
    n = row.shape[1]
    diagonal = lax.broadcasted_iota(jnp.int32, (n, n), 0) == lax.broadcasted_iota(
        jnp.int32, (n, n), 1
    )
    return jnp.sum(jnp.where(diagonal, row, 0.0), axis=1, keepdims=True)


def scale_of(degree):
    scale = 1.0 / jnp.sqrt(degree.astype(f32))
    rows = [scale[i : i + 1, :] for i in range(scale.shape[0])]
    return jnp.concatenate(rows, 1), jnp.concatenate([as_column(r) for r in rows], 0)


def split(value):
    high = value.astype(bf16)
    return high, (value - high.astype(f32)).astype(bf16)


def scale_kernel(features_ref, degree_ref, cot_ref, own_ref):
    _, column = scale_of(degree_ref[...])
    scaled = (features_ref[...].astype(f32) * column).astype(bf16)
    own_ref[:OWN, :] = scaled
    cot = jnp.max(jnp.abs(cot_ref[...].astype(f32)))
    feature = jnp.max(jnp.abs(scaled.astype(f32)))
    rows = lax.broadcasted_iota(jnp.int32, (BLOCK - OWN, TILE), 0)
    own_ref[OWN:, :] = jnp.where(rows < 8, cot, feature).astype(bf16)


def forward_kernel(place_ref, rows_ref, count_ref, tiles_ref, *refs):
    pieces, out_ref, acc_ref = refs[:-2], refs[-2], refs[-1]
    x, z, c = place_ref[0], place_ref[1], place_ref[2]
    acc_ref[...] = jnp.zeros_like(acc_ref)
    largest = None
    for ref, blocks in zip(pieces, forward_order(), strict=True):
        for at, (dx, dz, dc) in enumerate(blocks):
            column_block = blk_index(x ^ dx, lax.rem(z + place_ref[3 + dz], N_Z), c ^ dc)
            marks = ref[at, OWN:, :]
            largest = marks if largest is None else jnp.maximum(largest, marks)
            for half in range(OWN // TILE):
                k = column_block * (OWN // TILE) + half
                part = ref[at, half * TILE : (half + 1) * TILE, :]
                product = jnp.dot(tiles_ref[k], part, preferred_element_type=f32)
                for slot in range(SLOTS):
                    row = rows_ref[k * SLOTS + slot]
                    row = jnp.where(slot < count_ref[k], row, ROW_TILES)
                    where = pl.ds(pl.multiple_of(row * TILE, TILE), TILE)
                    acc_ref[where, :] += product[slot * TILE : (slot + 1) * TILE, :]
    marks = exponent_above(largest.astype(f32))
    shrink = 2.0 * jnp.exp2(-marks[8:9, :])
    for r in range(out_ref.shape[0]):
        out_ref[r, :OWN, :] = acc_ref[r * OWN : (r + 1) * OWN, :] * shrink
        out_ref[r, OWN:, :] = marks


def forward_order():
    own = [[(0, 0, 0), (0, 0, 1)], [(1, 0, 0), (1, 0, 1)]]
    for i in (1, 2, 3):
        own.append([(0, i, 0), (0, i, 1)])
        own.append([(1, i, 0), (1, i, 1)])
        own.append([(0, i + 4, 1), (0, i + 4, 0), (1, i + 4, 1), (1, i + 4, 0)])
    own.append([(0, 4, 0)])
    own.append([(1, 4, 0)])
    own.append([(0, 4, 1), (1, 4, 1)])
    return own


def middle_kernel(
    parts_ref,
    weight_ref,
    bias_ref,
    degree_ref,
    features_ref,
    cot_ref,
    hidden_ref,
    back_ref,
    grad_ref,
    factor_ref,
):
    row_scale, column_scale = scale_of(degree_ref[...])
    summed = jnp.zeros((OWN, TILE), f32)
    cot_mark = feature_mark = None
    for r in range(parts_ref.shape[0]):
        cot_r, feature_r = parts_ref[r, OWN : OWN + 1, :], parts_ref[r, OWN + 8 : OWN + 9, :]
        summed += parts_ref[r, :OWN, :] * (0.5 * jnp.exp2(feature_r))
        cot_mark = cot_r if cot_mark is None else jnp.maximum(cot_mark, cot_r)
        feature_mark = feature_r if feature_mark is None else jnp.maximum(feature_mark, feature_r)
    weight = weight_ref[...]
    high, low = split(summed)
    mixed = jnp.dot(high, weight, preferred_element_type=f32)
    mixed += jnp.dot(low, weight, preferred_element_type=f32)
    pre = column_scale * mixed + bias_ref[...]
    root = 0.7978845608028654
    square = pre * pre
    bent = jnp.tanh(root * pre * (1.0 + 0.044715 * square))
    half_up = 0.5 * (1.0 + bent)
    hidden_ref[...] = (pre * half_up).astype(bf16)
    slope = half_up + 0.5 * pre * (1.0 - bent * bent) * (root * (1.0 + 0.134145 * square))
    shrink = jnp.exp2(-cot_mark[:, :1])
    grad = cot_ref[...].astype(f32) * shrink * slope
    high, low = split(grad)
    across = (((1,), (1,)), ((), ()))
    back = lax.dot_general(weight, high, across, preferred_element_type=f32)
    back += lax.dot_general(weight, low, across, preferred_element_type=f32)
    weight_mark = exponent_above(jnp.max(jnp.abs(weight.astype(f32)), axis=(0, 1), keepdims=True))
    back_ref[...] = back * row_scale * (64.0 * jnp.exp2(-weight_mark))
    down = (((0,), (0,)), ((), ()))
    features = features_ref[...]
    local = lax.dot_general(features, high, down, preferred_element_type=f32)
    local += lax.dot_general(features, low, down, preferred_element_type=f32)
    local = local * (16.0 * jnp.exp2(-feature_mark[:, :1]))
    for r in range(grad_ref.shape[0]):
        i, j = r // 2, r % 2
        grad_ref[r] = local[i * 32 : (i + 1) * 32, j * 256 : (j + 1) * 256]
    one = jnp.ones((8, TILE), f32)
    factor_ref[0] = one * (16.0 * jnp.exp2(cot_mark + weight_mark))
    factor_ref[1] = one * (jnp.exp2(cot_mark + feature_mark) / 4096.0)


def backward_kernel(place_ref, rows_ref, count_ref, tiles_ref, back_ref, keep_ref, give_ref, group_ref):
    x, z, c = place_ref[0], place_ref[1], place_ref[2]
    for r in range(ROW_TILES):
        value = back_ref[r // 2, :, (r % 2) * TILE : (r % 2 + 1) * TILE] * (1.0 / 1024.0)
        high, low = split(value)
        group_ref[r, :TILE, :] = high
        group_ref[r, TILE:, :] = low
    group_ref[ROW_TILES] = jnp.zeros(group_ref.shape[1:], bf16)
    for dc, ref in ((1, give_ref), (0, keep_ref)):
        for at, (dx, shift) in enumerate(backward_order()):
            column_block = blk_index(x ^ dx, lax.rem(z + shift, N_Z), c ^ dc)
            for half in range(OWN // TILE):
                k = column_block * (OWN // TILE) + half
                picked = []
                for slot in range(SLOTS):
                    row = rows_ref[k * SLOTS + slot]
                    picked.append(group_ref[jnp.where(slot < count_ref[k], row, ROW_TILES)])
                both = jnp.dot(
                    jnp.concatenate(picked, 1), tiles_ref[k], preferred_element_type=f32
                )
                ref[at, :, half * TILE : (half + 1) * TILE] = both[:TILE] + both[TILE:]


Z_ORDER = (4, 3, 5, 2, 6, 1, 7, 0)


def backward_order():
    return [(dx, shift) for dx in (1, 0) for shift in Z_ORDER]


SMEM = pl.BlockSpec(memory_space=pltpu.SMEM)
VMEM = pl.BlockSpec(memory_space=pltpu.VMEM)


def shape(dims, dtype):
    return jax.ShapeDtypeStruct(dims, dtype)


def call(kernel, outs, smem, vmem, scratch=(), cost=0):
    return pl.pallas_call(
        kernel,
        out_shape=outs,
        in_specs=[SMEM] * smem + [VMEM] * vmem,
        out_specs=jax.tree.map(lambda _: VMEM, outs),
        scratch_shapes=list(scratch),
        compiler_params=pltpu.CompilerParams(vmem_limit_bytes=VMEM_LIMIT),
        cost_estimate=pl.CostEstimate(flops=cost, bytes_accessed=4 << 20, transcendentals=0),
    )


def gather_blocks(own):
    own = own[None]
    pair = jnp.concatenate([own, permute_blk(own, to_core)])
    far = permute_blk(own, to_z_by_core(4))
    near = [permute_blk(pair, to_z_by_core(d)) for d in (3, 2, 1)][::-1]
    pieces = [pair, permute_blk(pair, to_x)]
    for got in near:
        other = permute_blk(got, to_x)
        pieces += [got, other, permute_blk(jnp.concatenate([got, other]), to_core)]
    other = permute_blk(far, to_x)
    pieces += [far, other, permute_blk(jnp.concatenate([far, other]), to_core)]
    return pieces


def scatter_terms(keep, give):
    got = permute_blk(give.astype(f16), to_core)
    chip = keep + got.astype(f32)
    total = None
    for i, shift in enumerate(Z_ORDER):
        term = chip[N_Z + i] + permute_blk(chip[i].astype(f16), to_x).astype(f32)
        if shift:
            term = permute_blk(term.astype(f16), to_z(shift)).astype(f32)
        total = term if total is None else total + term
    return total


def per_device(
    node_features,
    weight_matrix,
    bias_vector,
    node_degree,
    tile_values,
    tile_row,
    tile_count,
    cotangent,
):
    n_out = weight_matrix.shape[1]
    tiles = tile_values.reshape(-1, SLOTS * TILE, TILE)
    rows = tile_row.reshape(-1)
    count = tile_count.reshape(-1)
    degree = node_degree.reshape(OWN // TILE, TILE)
    at = lax.axis_index("blk")
    x, z, c = at // (N_Z * N_C), at // N_C % N_Z, at % N_C
    up = [d % N_Z for d in (0, -1, -2, -3, 4, 1, 2, 3)]
    down = [-d % N_Z for d in up]
    place = jnp.concatenate(
        [jnp.stack([x, z, c]), jnp.where(c == 0, jnp.array(up), jnp.array(down))]
    ).astype(jnp.int32)

    own = call(scale_kernel, shape((BLOCK, TILE), bf16), 0, 3)(node_features, degree, cotangent)
    pieces = gather_blocks(own)
    partial = call(
        forward_kernel,
        shape((8, BLOCK, TILE), f32),
        3,
        1 + len(pieces),
        [pltpu.VMEM(((ROW_TILES + 1) * TILE, TILE), f32)],
        cost=1 << 29,
    )(place, rows, count, tiles, *pieces)
    parts = lax.all_to_all(partial.astype(f16), "rep", 0, 0).astype(f32)
    hidden, back, grad, factor = call(
        middle_kernel,
        (
            shape((OWN, n_out), bf16),
            shape((TILE, OWN), f32),
            shape((8, 32, 256), f32),
            shape((2, 8, TILE), f32),
        ),
        0,
        6,
        cost=1 << 27,
    )(parts, weight_matrix, bias_vector.reshape(1, -1), degree, node_features, cotangent)

    sent = jnp.concatenate([jnp.broadcast_to(back[None], (8, TILE, OWN)), grad], 1).astype(f16)
    got = lax.all_to_all(sent, "rep", 0, 0).astype(f32)
    keep, give = call(
        backward_kernel,
        (shape((16, TILE, OWN), f32), shape((16, TILE, OWN), f32)),
        3,
        2,
        [pltpu.VMEM((ROW_TILES + 1, 2 * TILE, TILE), bf16)],
        cost=1 << 30,
    )(place, rows, count, tiles, got[:, :TILE])
    total = scatter_terms(keep, give)
    row_scale = 1.0 / jnp.sqrt(node_degree.astype(f32))
    input_grad = ((total * row_scale[None, :]).T * factor[0, :1, :]).astype(bf16)

    grad = jnp.sum(got[:, TILE:], 0)
    for move in (to_core, to_x, to_z_xor(1), to_z_xor(2), to_z_xor(4)):
        grad = grad + permute_blk(grad, move)
    whole = lax.all_to_all(jnp.broadcast_to(grad[None], (8, 32, 256)), "rep", 0, 0)
    weight_grad = whole.reshape(4, 2, 32, 256).transpose(0, 2, 1, 3).reshape(TILE, n_out)
    weight_grad = weight_grad * factor[1, 0, 0]
    return hidden, weight_grad, input_grad


def solution(mesh):
    in_specs = (
        P(("blk", "rep"), None),
        P(),
        P(),
        P(("blk", "rep")),
        P("blk", "rep", None, None, None, None),
        P("blk", "rep", None, None),
        P("blk", "rep", None),
        P(("blk", "rep"), None),
    )
    out_specs = (P(("blk", "rep"), None), P(), P(("blk", "rep"), None))
    return jax.shard_map(
        per_device, mesh=mesh, in_specs=in_specs, out_specs=out_specs, check_vma=False
    )
```

time: 691 us -> 140 us (0.20); the launches traced: 681 us -> 139 us
  waiting for transfers between devices: 508 us -> 36.3 us
  local copies, waits for them, and re-layouts: 71 us -> 8.1 us
  matrix products: 58.7 us -> 0 us
  starting transfers between devices: 0.38 us -> 49.4 us
  blocking collectives: 0 us -> 34.6 us
  other arithmetic: 27.8 us -> 2.22 us
  between operations: 14.6 us -> 1.13 us
    reduce_scatter x2 -> x0, waiting for transfers between devices: 218 us -> none  [the longest x1 141 us: per_device(): lax.psum_scatter(column_spread(tile_values, tile_row, tile_count, group_g...]
    psum x1 -> x0, waiting for transfers between devices: 159 us -> none  [per_device(): lax.psum(local_grad, ('blk', 'rep')) * (1.0 / math.sqrt(node_total))]
    all_gather x2 -> x0, waiting for transfers between devices: 130 us -> none  [the longest x1 72.4 us: per_device(): group_grads = lax.all_gather(back_rows, 'rep', axis=0, tiled=True)]
    dot_general x19 -> x0, matrix products: 58.7 us -> none  [the longest x8 41.1 us: column_spread(): jnp.einsum('kscj,kscf->kjf', tile_block.astype(jnp.float32), picked, prec...]
    ppermute x0 -> x35, starting transfers between devices: none -> 46 us  [permute_blk(): return lax.ppermute(value, 'blk', pairs)]
    gather x8 -> x0, local copies, waits for them, and re-layouts: 40.2 us -> none  [column_spread(): grouped[slot_rows]]
    ppermute x0 -> x35, waiting for transfers between devices: none -> 36.3 us  [permute_blk(): return lax.ppermute(value, 'blk', pairs)]
    all_to_all x0 -> x2, blocking collectives: none -> 34.6 us  [the longest x1 19.3 us: per_device(): parts = lax.all_to_all(partial.astype(f16), 'rep', 0, 0).astype(f32)]
  transfers between devices with their start and end apart: 5 -> 36, of which waited for: 5 -> 13; matrix products, arithmetic and copies ran while one was open for 16% -> 3% of each run, Pallas kernels for 0% -> 0%
where the time goes in v1:
time: 140 us; the launch traced here: 139 us
  starting transfers between devices  49.4 us (35%)
  waiting for transfers between devices  36.3 us (26%)
  blocking collectives  34.6 us (25%)
  local copies, waits for them, and re-layouts  8.1 us (6%)
  Pallas kernels  6.82 us (5%)
  other arithmetic  2.22 us (2%)
    ppermute x35, starting transfers between devices, permute_blk(): return lax.ppermute(value, 'blk', pairs)  46 us
    ppermute x35, waiting for transfers between devices, permute_blk(): return lax.ppermute(value, 'blk', pairs)  36.3 us
    all_to_all x1, blocking collectives, per_device(): parts = lax.all_to_all(partial.astype(f16), 'rep', 0, 0).astype(f32)  19.3 us
    all_to_all x1, blocking collectives, per_device(): got = lax.all_to_all(sent, 'rep', 0, 0).astype(f32)  15.3 us
    unnamed x31, local copies, waits for them, and re-layouts  6.28 us
    all_to_all x1, starting transfers between devices, per_device(): lax.all_to_all(jnp.broadcast_to(grad[None], (8, 32, 256)), 'rep', 0, 0)  3.41 us
    pallas_call x1, Pallas kernels, per_device(): call(backward_kernel, (shape((16, TILE, OWN), f32), shape((16, TILE, OWN)...  3.04 us
  transfers between devices with their start and end apart: 36, of which 13 were waited for; matrix products, arithmetic and copies ran while one was open for 3% of the time, Pallas kernels for 0%

profile of v1, /device:TPU:32, one launch (start us, length us, event | category | flops | bytes accessed | tf_op | source)
XLA Modules:
  0.0 138.6 jit_solution(10257566323316340268)
XLA Ops:
  4.9 5.9 %collective-permute-start.8 = (bf16[2,272,128]{2,1,0:T(8,128)(2,1)S(1)}, bf16[2,272,128]{2,1,0:T(8,128)(2,1)S(1)}, u32[]{:S(2)}, u32[]{:S(2)}) collective-permute-start(bf16[2,272,128]{2,1,0:T(8,128)(2,1)S(1)} %pad_maximum_fusion.4.refs_0_), channel_id=1, source_target_pairs={{0,48},{8,88},{16,64},{24,104},{32,80},{40,120},{48,96},{56,8},{64... | collective-permute-start | bytes 417800 | tf_op jit(solution)/shard_map/ppermute | solution.py:33
  10.8 1.5 %collective-permute-start.5 = (bf16[2,272,128]{2,1,0:T(8,128)(2,1)S(1)}, bf16[2,272,128]{2,1,0:T(8,128)(2,1)S(1)}, u32[]{:S(2)}, u32[]{:S(2)}) collective-permute-start(bf16[2,272,128]{2,1,0:T(8,128)(2,1)S(1)} %pad_maximum_fusion.4.refs_0_), channel_id=1, source_target_pairs={{0,32},{8,104},{16,48},{24,120},{32,64},{40,8},{48,80},{56,24},{64... | collective-permute-start | bytes 417800 | tf_op jit(solution)/shard_map/ppermute | solution.py:33
  12.8 8.8 %collective-permute-done.11.refs_11_ = bf16[1,272,128]{2,1,0:T(8,128)(2,1)S(1)} collective-permute-done((bf16[1,272,128]{2,1,0:T(8,128)(2,1)S(1)}, bf16[1,272,128]{2,1,0:T(8,128)(2,1)S(1)}, u32[]{:S(2)}, u32[]{:S(2)}) %collective-permute-start.11) | collective-permute-done | bytes 69664 | tf_op jit(solution)/shard_map/ppermute | solution.py:33
  21.6 1.5 %collective-permute-start.12 = (bf16[1,272,128]{2,1,0:T(8,128)(2,1)S(1)}, bf16[1,272,128]{2,1,0:T(8,128)(2,1)S(1)}, u32[]{:S(2)}, u32[]{:S(2)}) collective-permute-start(bf16[1,272,128]{2,1,0:T(8,128)(2,1)S(1)} %collective-permute-done.11.refs_11_), channel_id=1, source_target_pairs={{0,128},{8,136},{16,144},{24,152},{32,160},{40,168},{48,176},{56,1... | collective-permute-start | bytes 208904 | tf_op jit(solution)/shard_map/ppermute | solution.py:33
  23.1 2.0 %collective-permute-start.2 = (bf16[2,272,128]{2,1,0:T(8,128)(2,1)S(1)}, bf16[2,272,128]{2,1,0:T(8,128)(2,1)S(1)}, u32[]{:S(2)}, u32[]{:S(2)}) collective-permute-start(bf16[2,272,128]{2,1,0:T(8,128)(2,1)S(1)} %pad_maximum_fusion.4.refs_0_), channel_id=1, source_target_pairs={{0,16},{8,120},{16,32},{24,8},{32,48},{40,24},{48,64},{56,40},{64,... | collective-permute-start | bytes 417800 | tf_op jit(solution)/shard_map/ppermute | solution.py:33
  25.6 1.5 %collective-permute-start.1 = (bf16[2,272,128]{2,1,0:T(8,128)(2,1)S(1)}, bf16[2,272,128]{2,1,0:T(8,128)(2,1)S(1)}, u32[]{:S(2)}, u32[]{:S(2)}) collective-permute-start(bf16[2,272,128]{2,1,0:T(8,128)(2,1)S(1)} %pad_maximum_fusion.4.refs_0_), channel_id=1, source_target_pairs={{0,128},{8,136},{16,144},{24,152},{32,160},{40,168},{48,176},{56,1... | collective-permute-start | bytes 417800 | tf_op jit(solution)/shard_map/ppermute | solution.py:33
  27.7 1.7 %collective-permute-done.2.refs_2_ = bf16[2,272,128]{2,1,0:T(8,128)(2,1)S(1)} collective-permute-done((bf16[2,272,128]{2,1,0:T(8,128)(2,1)S(1)}, bf16[2,272,128]{2,1,0:T(8,128)(2,1)S(1)}, u32[]{:S(2)}, u32[]{:S(2)}) %collective-permute-start.2) | collective-permute-done | bytes 139296 | tf_op jit(solution)/shard_map/ppermute | solution.py:33
  30.0 1.6 %collective-permute-done.9.refs_9_ = bf16[2,272,128]{2,1,0:T(8,128)(2,1)S(1)} collective-permute-done((bf16[2,272,128]{2,1,0:T(8,128)(2,1)S(1)}, bf16[2,272,128]{2,1,0:T(8,128)(2,1)S(1)}, u32[]{:S(2)}, u32[]{:S(2)}) %collective-permute-start.9) | collective-permute-done | bytes 139296 | tf_op jit(solution)/shard_map/ppermute | solution.py:33
  31.8 4.5 %collective-permute-done.6.refs_6_ = bf16[2,272,128]{2,1,0:T(8,128)(2,1)S(1)} collective-permute-done((bf16[2,272,128]{2,1,0:T(8,128)(2,1)S(1)}, bf16[2,272,128]{2,1,0:T(8,128)(2,1)S(1)}, u32[]{:S(2)}, u32[]{:S(2)}) %collective-permute-start.6) | collective-permute-done | bytes 139296 | tf_op jit(solution)/shard_map/ppermute | solution.py:33
  39.5 2.2 %copy-done = bf16[1,1,64,2,128,128]{5,4,3,2,1,0:T(8,128)(2,1)S(1)} copy-done((bf16[1,1,64,2,128,128]{5,4,3,2,1,0:T(8,128)(2,1)S(1)}, bf16[1,1,64,2,128,128]{5,4,3,2,1,0:T(8,128)(2,1)}, u32[]{:S(2)}) %copy-start) | copy-done | bytes 4194328
  41.7 2.0 %shard_map.122 = f32[8,272,128]{2,1,0:T(8,128)S(1)} custom-call(s32[11]{0:T(128)S(1)} %pad_add_fusion.place_ref, s32[128]{0:T(128)S(1)} %reshape.39.rows_ref, s32[64]{0:T(128)S(1)} %bitcast.101, bf16[64,256,128]{2,1,0:T(8,128)(2,1)S(1)} %bitcast.93, bf16[2,272,128]{2,1,0:T(8,128)(2,1)S(1)} %pad_maximum_fusion.4.refs_0_, ...), custom_call_target="tpu_custom_call" | custom-call | flops 536870912 | bytes 4194304 | tf_op jit(solution)/shard_map/pallas_call | solution.py:280
  43.9 19.3 %all_to_all.15 = f16[8,272,128]{2,1,0:T(8,128)(2,1)S(1)} all-to-all(f16[8,272,128]{2,1,0:T(8,128)(2,1)S(1)} %convert_element_type.123), channel_id=1, replica_groups=mesh['blk'=32,'rep'=8] {'rep'}, dimensions={0} | all-to-all | bytes 1114112 | tf_op jit(solution)/shard_map/all_to_all | solution.py:288
  63.3 1.4 %shard_map.123 = (bf16[256,512]{1,0:T(8,128)(2,1)}, f32[128,256]{1,0:T(8,128)S(1)}, f32[8,32,256]{2,1,0:T(8,128)S(1)}, f32[2,8,128]{2,1,0:T(8,128)S(1)}) custom-call(f32[8,272,128]{2,1,0:T(8,128)S(1)} %convert_element_type.124.parts_ref, bf16[128,512]{1,0:T(8,128)(2,1)S(1)} %copy-done.6, f32[1,512]{1,0:T(1,128)S(1)} %bitcast.100, s32[2,128]{1,0:T(2,128)S(1)} %bitcast.99, ...), custom_call_target="tpu_custom_call" | custom-call | flops 134217728 | bytes 4194304 | tf_op jit(solution)/shard_map/pallas_call | solution.py:289
  65.0 15.3 %all_to_all.16 = f16[8,160,256]{2,1,0:T(8,128)(2,1)S(1)} all-to-all(f16[8,160,256]{2,1,0:T(8,128)(2,1)S(1)} %pad_maximum_fusion), channel_id=1, replica_groups=mesh['blk'=32,'rep'=8] {'rep'}, dimensions={0} | all-to-all | bytes 1310720 | tf_op jit(solution)/shard_map/all_to_all | solution.py:303
  80.5 3.0 %shard_map.124 = (f32[16,128,256]{2,1,0:T(8,128)S(1)}, f32[16,128,256]{2,1,0:T(8,128)S(1)}) custom-call(s32[11]{0:T(128)S(1)} %pad_add_fusion.place_ref, s32[128]{0:T(128)S(1)} %reshape.39.rows_ref, s32[64]{0:T(128)S(1)} %bitcast.102, bf16[64,256,128]{2,1,0:T(8,128)(2,1)S(1)} %bitcast.94, f32[8,128,256]{2,1,0:T(8,128)S(1)} %slice.89.back_ref), custom_call_target="tpu_custom_call" | custom-call | flops 1073741824 | bytes 4194304 | tf_op jit(solution)/shard_map/pallas_call | solution.py:304
  84.5 2.1 %collective-permute-done.14 = f32[32,256]{1,0:T(8,128)S(1)} collective-permute-done((f32[32,256]{1,0:T(8,128)S(1)}, f32[32,256]{1,0:T(8,128)S(1)}, u32[]{:S(2)}, u32[]{:S(2)}) %collective-permute-start.14) | collective-permute-done | bytes 32800 | tf_op jit(solution)/shard_map/ppermute | solution.py:33
  87.2 3.4 %collective-permute-done.15 = f32[32,256]{1,0:T(8,128)S(1)} collective-permute-done((f32[32,256]{1,0:T(8,128)S(1)}, f32[32,256]{1,0:T(8,128)S(1)}, u32[]{:S(2)}, u32[]{:S(2)}) %collective-permute-start.15) | collective-permute-done | bytes 32800 | tf_op jit(solution)/shard_map/ppermute | solution.py:33
  91.4 3.1 %collective-permute-done.16 = f32[32,256]{1,0:T(8,128)S(1)} collective-permute-done((f32[32,256]{1,0:T(8,128)S(1)}, f32[32,256]{1,0:T(8,128)S(1)}, u32[]{:S(2)}, u32[]{:S(2)}) %collective-permute-start.16) | collective-permute-done | bytes 32800 | tf_op jit(solution)/shard_map/ppermute | solution.py:33
  94.5 2.5 %collective-permute-start.17 = (f32[32,256]{1,0:T(8,128)S(1)}, f32[32,256]{1,0:T(8,128)S(1)}, u32[]{:S(2)}, u32[]{:S(2)}) collective-permute-start(f32[32,256]{1,0:T(8,128)S(1)} %add.76), channel_id=1, source_target_pairs={{0,32},{8,40},{16,48},{24,56},{32,0},{40,8},{48,16},{56,24},{64,96... | collective-permute-start | bytes 98312 | tf_op jit(solution)/shard_map/ppermute | solution.py:33
  98.2 1.5 %collective-permute-start.32 = (f16[128,256]{1,0:T(8,128)(2,1)S(1)}, f16[128,256]{1,0:T(8,128)(2,1)S(1)}, u32[]{:S(2)}, u32[]{:S(2)}) collective-permute-start(f16[128,256]{1,0:T(8,128)(2,1)S(1)} %get-tuple-element.35), channel_id=1, source_target_pairs={{0,128},{8,136},{16,144},{24,152},{32,160},{40,168},{48,176},{56,1... | collective-permute-start | bytes 196616 | tf_op jit(solution)/shard_map/ppermute | solution.py:33
  99.7 3.8 %collective-permute-start.18 = (f32[32,256]{1,0:T(8,128)S(1)}, f32[32,256]{1,0:T(8,128)S(1)}, u32[]{:S(2)}, u32[]{:S(2)}) collective-permute-start(f32[32,256]{1,0:T(8,128)S(1)} %add.77), channel_id=1, source_target_pairs={{0,64},{8,72},{16,80},{24,88},{32,96},{40,104},{48,112},{56,120},{... | collective-permute-start | bytes 98312 | tf_op jit(solution)/shard_map/ppermute | solution.py:33
  103.8 1.7 %collective-permute-start.28 = (f16[128,256]{1,0:T(8,128)(2,1)S(1)}, f16[128,256]{1,0:T(8,128)(2,1)S(1)}, u32[]{:S(2)}, u32[]{:S(2)}) collective-permute-start(f16[128,256]{1,0:T(8,128)(2,1)S(1)} %get-tuple-element.37), channel_id=1, source_target_pairs={{0,128},{8,136},{16,144},{24,152},{32,160},{40,168},{48,176},{56,1... | collective-permute-start | bytes 196616 | tf_op jit(solution)/shard_map/ppermute | solution.py:33
  105.5 2.0 %collective-permute-done.18 = f32[32,256]{1,0:T(8,128)S(1)} collective-permute-done((f32[32,256]{1,0:T(8,128)S(1)}, f32[32,256]{1,0:T(8,128)S(1)}, u32[]{:S(2)}, u32[]{:S(2)}) %collective-permute-start.18) | collective-permute-done | bytes 32800 | tf_op jit(solution)/shard_map/ppermute | solution.py:33
  108.1 1.5 %collective-permute-start.24 = (f16[128,256]{1,0:T(8,128)(2,1)S(1)}, f16[128,256]{1,0:T(8,128)(2,1)S(1)}, u32[]{:S(2)}, u32[]{:S(2)}) collective-permute-start(f16[128,256]{1,0:T(8,128)(2,1)S(1)} %get-tuple-element.39), channel_id=1, source_target_pairs={{0,128},{8,136},{16,144},{24,152},{32,160},{40,168},{48,176},{56,1... | collective-permute-start | bytes 196616 | tf_op jit(solution)/shard_map/ppermute | solution.py:33
  110.9 3.4 %all-to-all-start.2 = ((f32[8,32,256]{2,1,0:T(8,128)}), f32[8,32,256]{2,1,0:T(8,128)S(1)}, u32[]{:S(2)}, u32[]{:S(2)}) async-start(f32[8,32,256]{2,1,0:T(8,128)} %broadcast_in_dim.8), calls=%async_computation.2 | async-start | bytes 524288 | tf_op jit(solution)/shard_map/all_to_all | solution.py:319
  114.3 1.6 %collective-permute-start.34 = (f16[128,256]{1,0:T(8,128)(2,1)S(1)}, f16[128,256]{1,0:T(8,128)(2,1)S(1)}, u32[]{:S(2)}, u32[]{:S(2)}) collective-permute-start(f16[128,256]{1,0:T(8,128)(2,1)S(1)} %get-tuple-element.34), channel_id=1, source_target_pairs={{0,128},{8,136},{16,144},{24,152},{32,160},{40,168},{48,176},{56,1... | collective-permute-start | bytes 196616 | tf_op jit(solution)/shard_map/ppermute | solution.py:33
  116.1 3.8 %collective-permute-start.21 = (f16[128,256]{1,0:T(8,128)(2,1)S(1)}, f16[128,256]{1,0:T(8,128)(2,1)S(1)}, u32[]{:S(2)}, u32[]{:S(2)}) collective-permute-start(f16[128,256]{1,0:T(8,128)(2,1)S(1)} %get-tuple-element.26), channel_id=1, source_target_pairs={{0,64},{8,72},{16,80},{24,88},{32,96},{40,104},{48,112},{56,120},{... | collective-permute-start | bytes 196616 | tf_op jit(solution)/shard_map/ppermute | solution.py:33
  119.9 2.1 %collective-permute-start.33 = (f16[128,256]{1,0:T(8,128)(2,1)S(1)}, f16[128,256]{1,0:T(8,128)(2,1)S(1)}, u32[]{:S(2)}, u32[]{:S(2)}) collective-permute-start(f16[128,256]{1,0:T(8,128)(2,1)S(1)} %get-tuple-element.27), channel_id=1, source_target_pairs={{0,112},{8,120},{16,0},{24,8},{32,16},{40,24},{48,32},{56,40},{64,... | collective-permute-start | bytes 196616 | tf_op jit(solution)/shard_map/ppermute | solution.py:33
  123.0 2.7 %collective-permute-start.29 = (f16[128,256]{1,0:T(8,128)(2,1)S(1)}, f16[128,256]{1,0:T(8,128)(2,1)S(1)}, u32[]{:S(2)}, u32[]{:S(2)}) collective-permute-start(f16[128,256]{1,0:T(8,128)(2,1)S(1)} %get-tuple-element.29), channel_id=1, source_target_pairs={{0,96},{8,104},{16,112},{24,120},{32,0},{40,8},{48,16},{56,24},{64... | collective-permute-start | bytes 196616 | tf_op jit(solution)/shard_map/ppermute | solution.py:33
  125.9 3.5 %collective-permute-start.25 = (f16[128,256]{1,0:T(8,128)(2,1)S(1)}, f16[128,256]{1,0:T(8,128)(2,1)S(1)}, u32[]{:S(2)}, u32[]{:S(2)}) collective-permute-start(f16[128,256]{1,0:T(8,128)(2,1)S(1)} %get-tuple-element.31), channel_id=1, source_target_pairs={{0,80},{8,88},{16,96},{24,104},{32,112},{40,120},{48,0},{56,8},{64... | collective-permute-start | bytes 196616 | tf_op jit(solution)/shard_map/ppermute | solution.py:33
  129.4 1.6 %collective-permute-start.23 = (f16[128,256]{1,0:T(8,128)(2,1)S(1)}, f16[128,256]{1,0:T(8,128)(2,1)S(1)}, u32[]{:S(2)}, u32[]{:S(2)}) collective-permute-start(f16[128,256]{1,0:T(8,128)(2,1)S(1)} %get-tuple-element.32), channel_id=1, source_target_pairs={{0,48},{8,56},{16,64},{24,72},{32,80},{40,88},{48,96},{56,104},{64... | collective-permute-start | bytes 196616 | tf_op jit(solution)/shard_map/ppermute | solution.py:33
  133.3 4.5 %collective-permute-done.23 = f16[128,256]{1,0:T(8,128)(2,1)S(1)} collective-permute-done((f16[128,256]{1,0:T(8,128)(2,1)S(1)}, f16[128,256]{1,0:T(8,128)(2,1)S(1)}, u32[]{:S(2)}, u32[]{:S(2)}) %collective-permute-start.23) | collective-permute-done | bytes 65568 | tf_op jit(solution)/shard_map/ppermute | solution.py:33
  (110 shorter events, 20.3 us)
Async XLA Ops:
  4.9 20.2 %collective-permute-start.8 = (bf16[2,272,128]{2,1,0:T(8,128)(2,1)S(1)}, bf16[2,272,128]{2,1,0:T(8,128)(2,1)S(1)}, u32[]{:S(2)}, u32[]{:S(2)}) collective-permute-start(bf16[2,272,128]{2,1,0:T(8,128)(2,1)S(1)} %pad_maximum_fusion.4.refs_0_), channel_id=1, source_target_pairs={{0,48},{8,88},{16,64},{24,104},{32,80},{40,120},{48,96},{56,8},{64... | collective-permute-start | bytes 417800 | tf_op jit(solution)/shard_map/ppermute | solution.py:33
  10.8 16.3 %collective-permute-start.5 = (bf16[2,272,128]{2,1,0:T(8,128)(2,1)S(1)}, bf16[2,272,128]{2,1,0:T(8,128)(2,1)S(1)}, u32[]{:S(2)}, u32[]{:S(2)}) collective-permute-start(bf16[2,272,128]{2,1,0:T(8,128)(2,1)S(1)} %pad_maximum_fusion.4.refs_0_), channel_id=1, source_target_pairs={{0,32},{8,104},{16,48},{24,120},{32,64},{40,8},{48,80},{56,24},{64... | collective-permute-start | bytes 417800 | tf_op jit(solution)/shard_map/ppermute | solution.py:33
  12.3 9.3 %collective-permute-start.11 = (bf16[1,272,128]{2,1,0:T(8,128)(2,1)S(1)}, bf16[1,272,128]{2,1,0:T(8,128)(2,1)S(1)}, u32[]{:S(2)}, u32[]{:S(2)}) collective-permute-start(bf16[1,272,128]{2,1,0:T(8,128)(2,1)S(1)} %bitcast.97), channel_id=1, source_target_pairs={{0,64},{8,72},{16,80},{24,88},{32,96},{40,104},{48,112},{56,120},{... | collective-permute-start | bytes 208904 | tf_op jit(solution)/shard_map/ppermute | solution.py:33
  21.6 6.0 %collective-permute-start.12 = (bf16[1,272,128]{2,1,0:T(8,128)(2,1)S(1)}, bf16[1,272,128]{2,1,0:T(8,128)(2,1)S(1)}, u32[]{:S(2)}, u32[]{:S(2)}) collective-permute-start(bf16[1,272,128]{2,1,0:T(8,128)(2,1)S(1)} %collective-permute-done.11.refs_11_), channel_id=1, source_target_pairs={{0,128},{8,136},{16,144},{24,152},{32,160},{40,168},{48,176},{56,1... | collective-permute-start | bytes 208904 | tf_op jit(solution)/shard_map/ppermute | solution.py:33
  23.1 6.4 %collective-permute-start.2 = (bf16[2,272,128]{2,1,0:T(8,128)(2,1)S(1)}, bf16[2,272,128]{2,1,0:T(8,128)(2,1)S(1)}, u32[]{:S(2)}, u32[]{:S(2)}) collective-permute-start(bf16[2,272,128]{2,1,0:T(8,128)(2,1)S(1)} %pad_maximum_fusion.4.refs_0_), channel_id=1, source_target_pairs={{0,16},{8,120},{16,32},{24,8},{32,48},{40,24},{48,64},{56,40},{64,... | collective-permute-start | bytes 417800 | tf_op jit(solution)/shard_map/ppermute | solution.py:33
  25.0 6.6 %collective-permute-start.9 = (bf16[2,272,128]{2,1,0:T(8,128)(2,1)S(1)}, bf16[2,272,128]{2,1,0:T(8,128)(2,1)S(1)}, u32[]{:S(2)}, u32[]{:S(2)}) collective-permute-start(bf16[2,272,128]{2,1,0:T(8,128)(2,1)S(1)} %collective-permute-done.8.refs_8_), channel_id=1, source_target_pairs={{0,128},{8,136},{16,144},{24,152},{32,160},{40,168},{48,176},{56,1... | collective-permute-start | bytes 417800 | tf_op jit(solution)/shard_map/ppermute | solution.py:33
  25.6 12.8 %collective-permute-start.1 = (bf16[2,272,128]{2,1,0:T(8,128)(2,1)S(1)}, bf16[2,272,128]{2,1,0:T(8,128)(2,1)S(1)}, u32[]{:S(2)}, u32[]{:S(2)}) collective-permute-start(bf16[2,272,128]{2,1,0:T(8,128)(2,1)S(1)} %pad_maximum_fusion.4.refs_0_), channel_id=1, source_target_pairs={{0,128},{8,136},{16,144},{24,152},{32,160},{40,168},{48,176},{56,1... | collective-permute-start | bytes 417800 | tf_op jit(solution)/shard_map/ppermute | solution.py:33
  27.1 9.3 %collective-permute-start.6 = (bf16[2,272,128]{2,1,0:T(8,128)(2,1)S(1)}, bf16[2,272,128]{2,1,0:T(8,128)(2,1)S(1)}, u32[]{:S(2)}, u32[]{:S(2)}) collective-permute-start(bf16[2,272,128]{2,1,0:T(8,128)(2,1)S(1)} %collective-permute-done.5.refs_5_), channel_id=1, source_target_pairs={{0,128},{8,136},{16,144},{24,152},{32,160},{40,168},{48,176},{56,1... | collective-permute-start | bytes 417800 | tf_op jit(solution)/shard_map/ppermute | solution.py:33
  27.6 10.7 %collective-permute-start.13 = (bf16[2,272,128]{2,1,0:T(8,128)(2,1)S(1)}, bf16[2,272,128]{2,1,0:T(8,128)(2,1)S(1)}, u32[]{:S(2)}, u32[]{:S(2)}) collective-permute-start(bf16[2,272,128]{2,1,0:T(8,128)(2,1)S(1)} %pad_maximum_fusion.5), channel_id=1, source_target_pairs={{0,8},{8,0},{16,24},{24,16},{32,40},{40,32},{48,56},{56,48},{64,72... | collective-permute-start | bytes 417800 | tf_op jit(solution)/shard_map/ppermute | solution.py:33
  29.5 8.3 %collective-permute-start.3 = (bf16[2,272,128]{2,1,0:T(8,128)(2,1)S(1)}, bf16[2,272,128]{2,1,0:T(8,128)(2,1)S(1)}, u32[]{:S(2)}, u32[]{:S(2)}) collective-permute-start(bf16[2,272,128]{2,1,0:T(8,128)(2,1)S(1)} %collective-permute-done.2.refs_2_), channel_id=1, source_target_pairs={{0,128},{8,136},{16,144},{24,152},{32,160},{40,168},{48,176},{56,1... | collective-permute-start | bytes 417800 | tf_op jit(solution)/shard_map/ppermute | solution.py:33
  31.7 6.7 %collective-permute-start.10 = (bf16[4,272,128]{2,1,0:T(8,128)(2,1)S(1)}, bf16[4,272,128]{2,1,0:T(8,128)(2,1)S(1)}, u32[]{:S(2)}, u32[]{:S(2)}) collective-permute-start(bf16[4,272,128]{2,1,0:T(8,128)(2,1)S(1)} %pad_maximum_fusion.3), channel_id=1, source_target_pairs={{0,8},{8,0},{16,24},{24,16},{32,40},{40,32},{48,56},{56,48},{64,72... | collective-permute-start | bytes 835592 | tf_op jit(solution)/shard_map/ppermute | solution.py:33
  83.8 13.2 %collective-permute-start.19 = (f16[16,128,256]{2,1,0:T(8,128)(2,1)S(1)}, f16[16,128,256]{2,1,0:T(8,128)(2,1)S(1)}, u32[]{:S(2)}, u32[]{:S(2)}) collective-permute-start(f16[16,128,256]{2,1,0:T(8,128)(2,1)S(1)} %convert_element_type.126), channel_id=1, source_target_pairs={{0,8},{8,0},{16,24},{24,16},{32,40},{40,32},{48,56},{56,48},{64,72... | collective-permute-start | bytes 3145736 | tf_op jit(solution)/shard_map/ppermute | solution.py:33
  86.6 3.9 %collective-permute-start.15 = (f32[32,256]{1,0:T(8,128)S(1)}, f32[32,256]{1,0:T(8,128)S(1)}, u32[]{:S(2)}, u32[]{:S(2)}) collective-permute-start(f32[32,256]{1,0:T(8,128)S(1)} %add.74), channel_id=1, source_target_pairs={{0,128},{8,136},{16,144},{24,152},{32,160},{40,168},{48,176},{56,1... | collective-permute-start | bytes 98312 | tf_op jit(solution)/shard_map/ppermute | solution.py:33
  90.5 3.9 %collective-permute-start.16 = (f32[32,256]{1,0:T(8,128)S(1)}, f32[32,256]{1,0:T(8,128)S(1)}, u32[]{:S(2)}, u32[]{:S(2)}) collective-permute-start(f32[32,256]{1,0:T(8,128)S(1)} %add.75), channel_id=1, source_target_pairs={{0,16},{8,24},{16,0},{24,8},{32,48},{40,56},{48,32},{56,40},{64,80... | collective-permute-start | bytes 98312 | tf_op jit(solution)/shard_map/ppermute | solution.py:33
  94.5 5.2 %collective-permute-start.17 = (f32[32,256]{1,0:T(8,128)S(1)}, f32[32,256]{1,0:T(8,128)S(1)}, u32[]{:S(2)}, u32[]{:S(2)}) collective-permute-start(f32[32,256]{1,0:T(8,128)S(1)} %add.76), channel_id=1, source_target_pairs={{0,32},{8,40},{16,48},{24,56},{32,0},{40,8},{48,16},{56,24},{64,96... | collective-permute-start | bytes 98312 | tf_op jit(solution)/shard_map/ppermute | solution.py:33
  97.5 10.6 %collective-permute-start.20 = (f16[128,256]{1,0:T(8,128)(2,1)S(1)}, f16[128,256]{1,0:T(8,128)(2,1)S(1)}, u32[]{:S(2)}, u32[]{:S(2)}) collective-permute-start(f16[128,256]{1,0:T(8,128)(2,1)S(1)} %get-tuple-element.33), channel_id=1, source_target_pairs={{0,128},{8,136},{16,144},{24,152},{32,160},{40,168},{48,176},{56,1... | collective-permute-start | bytes 196616 | tf_op jit(solution)/shard_map/ppermute | solution.py:33
  98.2 11.5 %collective-permute-start.32 = (f16[128,256]{1,0:T(8,128)(2,1)S(1)}, f16[128,256]{1,0:T(8,128)(2,1)S(1)}, u32[]{:S(2)}, u32[]{:S(2)}) collective-permute-start(f16[128,256]{1,0:T(8,128)(2,1)S(1)} %get-tuple-element.35), channel_id=1, source_target_pairs={{0,128},{8,136},{16,144},{24,152},{32,160},{40,168},{48,176},{56,1... | collective-permute-start | bytes 196616 | tf_op jit(solution)/shard_map/ppermute | solution.py:33
  99.7 7.9 %collective-permute-start.18 = (f32[32,256]{1,0:T(8,128)S(1)}, f32[32,256]{1,0:T(8,128)S(1)}, u32[]{:S(2)}, u32[]{:S(2)}) collective-permute-start(f32[32,256]{1,0:T(8,128)S(1)} %add.77), channel_id=1, source_target_pairs={{0,64},{8,72},{16,80},{24,88},{32,96},{40,104},{48,112},{56,120},{... | collective-permute-start | bytes 98312 | tf_op jit(solution)/shard_map/ppermute | solution.py:33
  103.5 10.8 %collective-permute-start.30 = (f16[128,256]{1,0:T(8,128)(2,1)S(1)}, f16[128,256]{1,0:T(8,128)(2,1)S(1)}, u32[]{:S(2)}, u32[]{:S(2)}) collective-permute-start(f16[128,256]{1,0:T(8,128)(2,1)S(1)} %get-tuple-element.36), channel_id=1, source_target_pairs={{0,128},{8,136},{16,144},{24,152},{32,160},{40,168},{48,176},{56,1... | collective-permute-start | bytes 196616 | tf_op jit(solution)/shard_map/ppermute | solution.py:33
  103.8 12.1 %collective-permute-start.28 = (f16[128,256]{1,0:T(8,128)(2,1)S(1)}, f16[128,256]{1,0:T(8,128)(2,1)S(1)}, u32[]{:S(2)}, u32[]{:S(2)}) collective-permute-start(f16[128,256]{1,0:T(8,128)(2,1)S(1)} %get-tuple-element.37), channel_id=1, source_target_pairs={{0,128},{8,136},{16,144},{24,152},{32,160},{40,168},{48,176},{56,1... | collective-permute-start | bytes 196616 | tf_op jit(solution)/shard_map/ppermute | solution.py:33
  107.6 8.3 %collective-permute-start.26 = (f16[128,256]{1,0:T(8,128)(2,1)S(1)}, f16[128,256]{1,0:T(8,128)(2,1)S(1)}, u32[]{:S(2)}, u32[]{:S(2)}) collective-permute-start(f16[128,256]{1,0:T(8,128)(2,1)S(1)} %get-tuple-element.38), channel_id=1, source_target_pairs={{0,128},{8,136},{16,144},{24,152},{32,160},{40,168},{48,176},{56,1... | collective-permute-start | bytes 196616 | tf_op jit(solution)/shard_map/ppermute | solution.py:33
  108.1 7.8 %collective-permute-start.24 = (f16[128,256]{1,0:T(8,128)(2,1)S(1)}, f16[128,256]{1,0:T(8,128)(2,1)S(1)}, u32[]{:S(2)}, u32[]{:S(2)}) collective-permute-start(f16[128,256]{1,0:T(8,128)(2,1)S(1)} %get-tuple-element.39), channel_id=1, source_target_pairs={{0,128},{8,136},{16,144},{24,152},{32,160},{40,168},{48,176},{56,1... | collective-permute-start | bytes 196616 | tf_op jit(solution)/shard_map/ppermute | solution.py:33
  109.6 6.3 %collective-permute-start.22 = (f16[128,256]{1,0:T(8,128)(2,1)S(1)}, f16[128,256]{1,0:T(8,128)(2,1)S(1)}, u32[]{:S(2)}, u32[]{:S(2)}) collective-permute-start(f16[128,256]{1,0:T(8,128)(2,1)S(1)} %get-tuple-element.40), channel_id=1, source_target_pairs={{0,128},{8,136},{16,144},{24,152},{32,160},{40,168},{48,176},{56,1... | collective-permute-start | bytes 196616 | tf_op jit(solution)/shard_map/ppermute | solution.py:33
  110.9 20.1 %all-to-all-start.2 = ((f32[8,32,256]{2,1,0:T(8,128)}), f32[8,32,256]{2,1,0:T(8,128)S(1)}, u32[]{:S(2)}, u32[]{:S(2)}) async-start(f32[8,32,256]{2,1,0:T(8,128)} %broadcast_in_dim.8), calls=%async_computation.2 | async-start | bytes 524288 | tf_op jit(solution)/shard_map/all_to_all | solution.py:319
  114.3 11.4 %collective-permute-start.34 = (f16[128,256]{1,0:T(8,128)(2,1)S(1)}, f16[128,256]{1,0:T(8,128)(2,1)S(1)}, u32[]{:S(2)}, u32[]{:S(2)}) collective-permute-start(f16[128,256]{1,0:T(8,128)(2,1)S(1)} %get-tuple-element.34), channel_id=1, source_target_pairs={{0,128},{8,136},{16,144},{24,152},{32,160},{40,168},{48,176},{56,1... | collective-permute-start | bytes 196616 | tf_op jit(solution)/shard_map/ppermute | solution.py:33
  116.1 9.9 %collective-permute-start.21 = (f16[128,256]{1,0:T(8,128)(2,1)S(1)}, f16[128,256]{1,0:T(8,128)(2,1)S(1)}, u32[]{:S(2)}, u32[]{:S(2)}) collective-permute-start(f16[128,256]{1,0:T(8,128)(2,1)S(1)} %get-tuple-element.26), channel_id=1, source_target_pairs={{0,64},{8,72},{16,80},{24,88},{32,96},{40,104},{48,112},{56,120},{... | collective-permute-start | bytes 196616 | tf_op jit(solution)/shard_map/ppermute | solution.py:33
  119.9 9.5 %collective-permute-start.33 = (f16[128,256]{1,0:T(8,128)(2,1)S(1)}, f16[128,256]{1,0:T(8,128)(2,1)S(1)}, u32[]{:S(2)}, u32[]{:S(2)}) collective-permute-start(f16[128,256]{1,0:T(8,128)(2,1)S(1)} %get-tuple-element.27), channel_id=1, source_target_pairs={{0,112},{8,120},{16,0},{24,8},{32,16},{40,24},{48,32},{56,40},{64,... | collective-permute-start | bytes 196616 | tf_op jit(solution)/shard_map/ppermute | solution.py:33
  122.5 10.1 %collective-permute-start.31 = (f16[128,256]{1,0:T(8,128)(2,1)S(1)}, f16[128,256]{1,0:T(8,128)(2,1)S(1)}, u32[]{:S(2)}, u32[]{:S(2)}) collective-permute-start(f16[128,256]{1,0:T(8,128)(2,1)S(1)} %get-tuple-element.28), channel_id=1, source_target_pairs={{0,16},{8,24},{16,32},{24,40},{32,48},{40,56},{48,64},{56,72},{64,... | collective-permute-start | bytes 196616 | tf_op jit(solution)/shard_map/ppermute | solution.py:33
  123.0 9.6 %collective-permute-start.29 = (f16[128,256]{1,0:T(8,128)(2,1)S(1)}, f16[128,256]{1,0:T(8,128)(2,1)S(1)}, u32[]{:S(2)}, u32[]{:S(2)}) collective-permute-start(f16[128,256]{1,0:T(8,128)(2,1)S(1)} %get-tuple-element.29), channel_id=1, source_target_pairs={{0,96},{8,104},{16,112},{24,120},{32,0},{40,8},{48,16},{56,24},{64... | collective-permute-start | bytes 196616 | tf_op jit(solution)/shard_map/ppermute | solution.py:33
  125.7 6.9 %collective-permute-start.27 = (f16[128,256]{1,0:T(8,128)(2,1)S(1)}, f16[128,256]{1,0:T(8,128)(2,1)S(1)}, u32[]{:S(2)}, u32[]{:S(2)}) collective-permute-start(f16[128,256]{1,0:T(8,128)(2,1)S(1)} %get-tuple-element.30), channel_id=1, source_target_pairs={{0,32},{8,40},{16,48},{24,56},{32,64},{40,72},{48,80},{56,88},{64,... | collective-permute-start | bytes 196616 | tf_op jit(solution)/shard_map/ppermute | solution.py:33
  125.9 7.3 %collective-permute-start.25 = (f16[128,256]{1,0:T(8,128)(2,1)S(1)}, f16[128,256]{1,0:T(8,128)(2,1)S(1)}, u32[]{:S(2)}, u32[]{:S(2)}) collective-permute-start(f16[128,256]{1,0:T(8,128)(2,1)S(1)} %get-tuple-element.31), channel_id=1, source_target_pairs={{0,80},{8,88},{16,96},{24,104},{32,112},{40,120},{48,0},{56,8},{64... | collective-permute-start | bytes 196616 | tf_op jit(solution)/shard_map/ppermute | solution.py:33
  129.4 8.4 %collective-permute-start.23 = (f16[128,256]{1,0:T(8,128)(2,1)S(1)}, f16[128,256]{1,0:T(8,128)(2,1)S(1)}, u32[]{:S(2)}, u32[]{:S(2)}) collective-permute-start(f16[128,256]{1,0:T(8,128)(2,1)S(1)} %get-tuple-element.32), channel_id=1, source_target_pairs={{0,48},{8,56},{16,64},{24,72},{32,80},{40,88},{48,96},{56,104},{64... | collective-permute-start | bytes 196616 | tf_op jit(solution)/shard_map/ppermute | solution.py:33
  (18 other events, 276.4 us)

commit v2 on v1

v2 whole, which is shorter than its diff:
```python
import functools

import jax
import jax.numpy as jnp
from jax import lax
from jax.experimental import pallas as pl
from jax.experimental.pallas import tpu as pltpu
from jax.sharding import PartitionSpec as P

f32, bf16, f16 = jnp.float32, jnp.bfloat16, jnp.float16

TILE = 128
OWN = 256
BLOCK = OWN + 16
N_X, N_Z, N_C = 2, 8, 2
N_Y = 4
SLOTS = 2
ROW_TILES = 16
VMEM_LIMIT = 16 * 1024 * 1024


def blk_index(x, z, c):
    return (x * N_Z + z) * N_C + c


def permute_blk(value, move):
    pairs = []
    for x in range(N_X):
        for z in range(N_Z):
            for c in range(N_C):
                pairs.append((blk_index(x, z, c), blk_index(*move(x, z, c))))
    return lax.ppermute(value, "blk", pairs)


def to_core(x, z, c):
    return x, z, 1 - c


def to_x(x, z, c):
    return 1 - x, z, c


def to_z_by_core(distance):
    return lambda x, z, c: (x, (z + (distance if c == 0 else -distance)) % N_Z, c)


def exponent_above(largest):
    return jnp.ceil(jnp.log2(jnp.maximum(largest, 1e-30))) + 1.0


def as_column(row):
    n = row.shape[1]
    diagonal = lax.broadcasted_iota(jnp.int32, (n, n), 0) == lax.broadcasted_iota(
        jnp.int32, (n, n), 1
    )
    return jnp.sum(jnp.where(diagonal, row, 0.0), axis=1, keepdims=True)


def scale_of(degree):
    scale = 1.0 / jnp.sqrt(degree.astype(f32))
    rows = [scale[i : i + 1, :] for i in range(scale.shape[0])]
    return jnp.concatenate(rows, 1), jnp.concatenate([as_column(r) for r in rows], 0)


def split(value):
    high = value.astype(bf16)
    return high, (value - high.astype(f32)).astype(bf16)


def scale_kernel(features_hbm, degree_hbm, cot_hbm, own_ref, features_ref, degree_ref, cot_ref, sems):
    copies = [
        pltpu.make_async_copy(src, dst, sems.at[i])
        for i, (src, dst) in enumerate(
            [(degree_hbm, degree_ref), (features_hbm, features_ref), (cot_hbm, cot_ref)]
        )
    ]
    for copy in copies:
        copy.start()
    copies[0].wait()
    _, column = scale_of(degree_ref[...])
    copies[1].wait()
    scaled = (features_ref[...].astype(f32) * column).astype(bf16)
    own_ref[0, :OWN, :] = scaled
    copies[2].wait()
    cot = jnp.max(jnp.abs(cot_ref[...].astype(f32)))
    feature = jnp.max(jnp.abs(scaled.astype(f32)))
    rows = lax.broadcasted_iota(jnp.int32, (BLOCK - OWN, TILE), 0)
    own_ref[0, OWN:, :] = jnp.where(rows < 8, cot, feature).astype(bf16)
    own_ref[1] = own_ref[0]


def column_block(at, dx, dz, dc):
    x, z, c = at // (N_Z * N_C), at // N_C % N_Z, at % N_C
    z = (z + N_Z + (1 - 2 * c) * dz) % N_Z
    return blk_index(x + dx - 2 * dx * x, z, c + dc - 2 * dc * c)


def add_products(order, place_ref, rows_ref, count_ref, tiles_ref, pieces, acc_ref):
    column_blocks = [
        column_block(place_ref[0], *block) for blocks in order for block in blocks
    ]
    refs = [(ref, at) for ref, blocks in zip(pieces, order, strict=True) for at in range(len(blocks))]
    largest = None
    for i, (ref, at) in enumerate(refs):
        marks = ref[at, OWN:, :].astype(f32)
        largest = marks if largest is None else jnp.maximum(largest, marks)
        for half in range(OWN // TILE):
            k = column_blocks[i] * (OWN // TILE) + half
            part = ref[at, half * TILE : (half + 1) * TILE, :]
            product = jnp.dot(tiles_ref[k], part, preferred_element_type=f32)
            for slot in range(SLOTS):
                row = rows_ref[k * SLOTS + slot]
                row = jnp.where(slot < count_ref[k], row, ROW_TILES)
                where = pl.ds(pl.multiple_of(row * TILE, TILE), TILE)
                acc_ref[where, :] += product[slot * TILE : (slot + 1) * TILE, :]
    return largest


def forward_kernel(order, place_ref, rows_ref, count_ref, tiles_ref, *refs):
    (acc_ref, marks_ref), refs = refs[-2:], refs[:-2]
    pieces = refs[-len(order) :]
    if len(refs) > len(order):
        acc_ref[...] = refs[0][...]
    else:
        acc_ref[...] = jnp.zeros_like(acc_ref)
    marks = add_products(order, place_ref, rows_ref, count_ref, tiles_ref, pieces, acc_ref)
    if len(refs) > len(order):
        marks = jnp.maximum(marks, refs[1][...])
    marks_ref[...] = marks


def forward_last_kernel(place_ref, rows_ref, count_ref, tiles_ref, begun_ref, begun_marks, *refs):
    pieces, (out_ref, acc_ref) = refs[:-2], refs[-2:]
    acc_ref[...] = begun_ref[...]
    largest = add_products(
        LAST_ORDER, place_ref, rows_ref, count_ref, tiles_ref, pieces, acc_ref
    )
    marks = exponent_above(jnp.maximum(largest, begun_marks[...]))
    shrink = 2.0 * jnp.exp2(-marks[8:9, :])
    for r in range(out_ref.shape[0]):
        out_ref[r, :OWN, :] = acc_ref[r * OWN : (r + 1) * OWN, :] * shrink
        out_ref[r, OWN:, :] = marks


FORWARD_ORDERS = [
    [[(0, 0, 0), (0, 0, 1)]],
    [[(1, 0, 0), (1, 0, 1)], [(0, -1, 0), (0, -1, 1), (0, -2, 0), (0, -2, 1)]],
    [[(1, -1, 0), (1, -1, 1), (1, -2, 0), (1, -2, 1)], [(0, -3, 0), (0, -3, 1), (0, 4, 0)]],
    [
        [(dx, i, dc) for dx in (0, 1) for i in (1, 2) for dc in (1, 0)],
        [(1, -3, 0), (1, -3, 1), (1, 4, 0)],
        [(0, 3, 1), (0, 3, 0), (0, 4, 1)],
    ],
]
LAST_ORDER = [[(1, 3, 1), (1, 3, 0), (1, 4, 1)]]


def middle_kernel(
    parts_ref,
    weight_ref,
    bias_ref,
    degree_ref,
    features_ref,
    cot_ref,
    hidden_ref,
    back_ref,
    grad_ref,
    factor_ref,
):
    row_scale, column_scale = scale_of(degree_ref[...])
    summed = jnp.zeros((OWN, TILE), f32)
    cot_mark = feature_mark = None
    for r in range(parts_ref.shape[0]):
        cot_r, feature_r = parts_ref[r, OWN : OWN + 1, :], parts_ref[r, OWN + 8 : OWN + 9, :]
        summed += parts_ref[r, :OWN, :] * (0.5 * jnp.exp2(feature_r))
        cot_mark = cot_r if cot_mark is None else jnp.maximum(cot_mark, cot_r)
        feature_mark = feature_r if feature_mark is None else jnp.maximum(feature_mark, feature_r)
    weight = weight_ref[...]
    high, low = split(summed)
    mixed = jnp.dot(high, weight, preferred_element_type=f32)
    mixed += jnp.dot(low, weight, preferred_element_type=f32)
    pre = column_scale * mixed + bias_ref[...]
    root = 0.7978845608028654
    square = pre * pre
    bent = jnp.tanh(root * pre * (1.0 + 0.044715 * square))
    half_up = 0.5 * (1.0 + bent)
    hidden_ref[...] = (pre * half_up).astype(bf16)
    slope = half_up + 0.5 * pre * (1.0 - bent * bent) * (root * (1.0 + 0.134145 * square))
    shrink = jnp.exp2(-cot_mark[:, :1])
    grad = cot_ref[...].astype(f32) * shrink * slope
    high, low = split(grad)
    across = (((1,), (1,)), ((), ()))
    back = lax.dot_general(weight, high, across, preferred_element_type=f32)
    back += lax.dot_general(weight, low, across, preferred_element_type=f32)
    weight_mark = exponent_above(jnp.max(jnp.abs(weight.astype(f32)), axis=(0, 1), keepdims=True))
    back_ref[...] = back * row_scale * (64.0 * jnp.exp2(-weight_mark))
    down = (((0,), (0,)), ((), ()))
    features = features_ref[...]
    local = lax.dot_general(features, high, down, preferred_element_type=f32)
    local += lax.dot_general(features, low, down, preferred_element_type=f32)
    local = local * (0.25 * jnp.exp2(-feature_mark[:, :1]))
    for r in range(grad_ref.shape[0]):
        i, j = r // 2, r % 2
        grad_ref[r] = local[i * 32 : (i + 1) * 32, j * 256 : (j + 1) * 256]
    one = jnp.ones((8, TILE), f32)
    factor_ref[0] = one * (16.0 * jnp.exp2(cot_mark + weight_mark))
    factor_ref[1] = one * (jnp.exp2(cot_mark + feature_mark) / 64.0)


def backward_kernel(orders, place_ref, rows_ref, count_ref, tiles_ref, back_ref, *refs):
    outs, group_ref = refs[:-1], refs[-1]
    for r in range(ROW_TILES):
        value = back_ref[r // 2, :, (r % 2) * TILE : (r % 2 + 1) * TILE] * (1.0 / 1024.0)
        high, low = split(value)
        group_ref[r, :TILE, :] = high
        group_ref[r, TILE:, :] = low
    group_ref[ROW_TILES] = jnp.zeros(group_ref.shape[1:], bf16)
    for ref, order in zip(outs, orders, strict=True):
        for at, block in enumerate(order):
            block = column_block(place_ref[0], *block)
            for half in range(OWN // TILE):
                k = block * (OWN // TILE) + half
                picked = []
                for slot in range(SLOTS):
                    row = rows_ref[k * SLOTS + slot]
                    picked.append(group_ref[jnp.where(slot < count_ref[k], row, ROW_TILES)])
                both = jnp.dot(
                    jnp.concatenate(picked, 1), tiles_ref[k], preferred_element_type=f32
                )
                ref[at, :, half * TILE : (half + 1) * TILE] = both[:TILE] + both[TILE:]


def sum_kernel(place_ref, own_ref, mine_ref, theirs_ref, out_ref):
    z, c = place_ref[0] // N_C % N_Z, place_ref[0] % N_C
    total = None
    for at in range(N_Z):
        below = (z - at + N_Z) % N_Z
        index = jnp.where(below <= 4, below, N_Z - below)
        side = jnp.where(below <= 4, c, 1 - c)
        index = jnp.maximum(index, 1) - 1
        value = jnp.where(side == 0, mine_ref[index], theirs_ref[index])
        value = jnp.where(below == 0, own_ref[...], value)
        total = value if total is None else total + value
    out_ref[...] = total


def assemble_kernel(slices_ref, factor_ref, out_ref):
    factor = jnp.concatenate([factor_ref[1, :1, :]] * 2, 1)
    for r in range(slices_ref.shape[0]):
        i, j = r // 2, r % 2
        out_ref[i * 32 : (i + 1) * 32, j * 256 : (j + 1) * 256] = slices_ref[r] * factor


GIVE_FAR = [(dx, *rest) for dx in (1, 0) for rest in ((4, 1), (-3, 1), (-3, 0))]
GIVE_NEAR = [(dx, *rest) for dx in (1, 0) for rest in ((-2, 1), (-2, 0), (-1, 1), (-1, 0), (0, 1))]
KEEP_FAR = [(dx, *rest) for dx in (1, 0) for rest in ((4, 0), (3, 0), (3, 1))]
KEEP_NEAR = [(dx, *rest) for dx in (1, 0) for rest in ((2, 0), (2, 1), (1, 0), (1, 1), (0, 0))]


SMEM = pl.BlockSpec(memory_space=pltpu.SMEM)
VMEM = pl.BlockSpec(memory_space=pltpu.VMEM)
HBM = pl.BlockSpec(memory_space=pltpu.HBM)


def shape(dims, dtype):
    return jax.ShapeDtypeStruct(dims, dtype)


def call(kernel, outs, ins, scratch=(), cost=0):
    return pl.pallas_call(
        kernel,
        out_shape=outs,
        in_specs=ins,
        out_specs=jax.tree.map(lambda _: VMEM, outs),
        scratch_shapes=list(scratch),
        compiler_params=pltpu.CompilerParams(vmem_limit_bytes=VMEM_LIMIT),
        cost_estimate=pl.CostEstimate(flops=cost, bytes_accessed=1 << 20, transcendentals=0),
    )


def after(value, *others):
    return lax.optimization_barrier((value, *others))[0]


def together(*values):
    return lax.optimization_barrier(values)


def gather_blocks(own, forward):
    pair = lax.dynamic_update_slice(own, permute_blk(own[:1], to_core), (1, 0, 0))
    *begun, pair_x, near_1, near_2 = together(
        *forward(0, pair),
        permute_blk(pair, to_x),
        permute_blk(pair, to_z_by_core(1)),
        permute_blk(pair, to_z_by_core(2)),
    )
    near = jnp.concatenate([near_1, near_2])
    *begun, far, near_x = together(
        *forward(1, *begun, pair_x, near),
        permute_blk(near[:3], to_z_by_core(2)),
        permute_blk(near, to_x),
    )
    *begun, far_core, near_core, far_x = together(
        *forward(2, *begun, near_x, far),
        permute_blk(far, to_core),
        permute_blk(jnp.concatenate([near, near_x]), to_core),
        permute_blk(far, to_x),
    )
    return together(
        *forward(3, *begun, near_core, far_x, far_core), permute_blk(far_x, to_core)
    )


def scatter_terms(give_far, give_near, keep_far, keep_near, grad):
    def send(move, *values):
        sizes = [value.size // OWN for value in values]
        message = [value.astype(f16).reshape(-1, OWN) for value in values]
        got = permute_blk(jnp.concatenate(message) if len(message) > 1 else message[0], move)
        got = got.astype(f32)
        starts = [sum(sizes[:i]) for i in range(len(sizes))]
        return [
            got[at : at + size].reshape(value.shape)
            for at, size, value in zip(starts, sizes, values)
        ]

    def rounded(value):
        return value.astype(f16).astype(f32)

    far, more = send(to_core, give_far, grad)
    far, grad = keep_far + far, rounded(rounded(grad) + more)
    far_x, more = send(to_x, far[:3], grad)
    far, grad = far[3:] + far_x, rounded(grad + more)
    (near,) = send(to_core, give_near)
    near = keep_near + near
    (near_x,) = send(to_x, near[:5])
    passed, grad_2 = send(to_z_by_core(2), far, grad)
    near = near[5:] + near_x
    two = jnp.concatenate([near[:1] + passed[:1], near[1:2]])
    got_2, grad_4 = send(to_z_by_core(2), two, grad_2)
    got_1, grad_1, grad_3 = send(to_z_by_core(1), near[2:4] + passed[1:], grad, grad_2)
    got = got_2 + got_1
    mine = jnp.stack([grad_1, grad_2, grad_3, grad_4])
    other, theirs = send(to_core, got[1], mine)
    return near[4] + got[0] + other, grad, mine, theirs


def per_device(
    node_features,
    weight_matrix,
    bias_vector,
    node_degree,
    tile_values,
    tile_row,
    tile_count,
    cotangent,
):
    n_out = weight_matrix.shape[1]
    tiles = tile_values.reshape(-1, SLOTS * TILE, TILE)
    rows = tile_row.reshape(-1)
    count = tile_count.reshape(-1)
    degree = node_degree.reshape(OWN // TILE, TILE)
    place = lax.axis_index("blk").astype(jnp.int32).reshape(1)

    own = call(
        scale_kernel,
        shape((2, BLOCK, TILE), bf16),
        [HBM] * 3,
        [
            pltpu.VMEM((OWN, TILE), bf16),
            pltpu.VMEM((OWN // TILE, TILE), jnp.int32),
            pltpu.VMEM((OWN, n_out), bf16),
            pltpu.SemaphoreType.DMA((3,)),
        ],
    )(node_features, degree, cotangent)
    acc = shape(((ROW_TILES + 1) * TILE, TILE), f32)
    marks = shape((BLOCK - OWN, TILE), f32)

    smem = (after(rows, own), after(count, own))

    def products(kernel, outs, scratch, *pieces):
        ins = [SMEM] * 3 + [VMEM] * (1 + len(pieces))
        return call(kernel, outs, ins, scratch, 1 << 29)(place, *smem, tiles, *pieces)

    def forward(step, *pieces):
        kernel = functools.partial(forward_kernel, FORWARD_ORDERS[step])
        return products(kernel, (acc, marks), [], *pieces)

    partial = products(
        forward_last_kernel,
        shape((8, BLOCK, TILE), f32),
        [pltpu.VMEM(acc.shape, f32)],
        *gather_blocks(own, forward),
    )
    parts = lax.all_to_all(partial.astype(f16), "rep", 0, 0).astype(f32)
    hidden, back, grad, factor = call(
        middle_kernel,
        (
            shape((OWN, n_out), bf16),
            shape((TILE, OWN), f32),
            shape((8, 32, 256), f32),
            shape((2, 8, TILE), f32),
        ),
        [VMEM] * 6,
        cost=1 << 27,
    )(parts, weight_matrix, bias_vector.reshape(1, -1), degree, node_features, cotangent)

    sent = jnp.concatenate([jnp.broadcast_to(back[None], (8, TILE, OWN)), grad], 1).astype(f16)
    got = lax.all_to_all(sent, "rep", 0, 0).astype(f32)
    got_back = got[:, :TILE]

    orders = (GIVE_FAR, GIVE_NEAR, KEEP_FAR, KEEP_NEAR)
    terms = products(
        functools.partial(backward_kernel, orders),
        tuple(shape((len(order), TILE, OWN), f32) for order in orders),
        [pltpu.VMEM((ROW_TILES + 1, 2 * TILE, TILE), bf16)],
        got_back,
    )
    total, *grads = scatter_terms(*terms, jnp.sum(got[:, TILE:], 0))
    row_scale = 1.0 / jnp.sqrt(node_degree.astype(f32))
    input_grad = ((total * row_scale[None, :]).T * factor[0, :1, :]).astype(bf16)

    grad = call(sum_kernel, shape((32, 256), f32), [SMEM] + [VMEM] * 3)(place, *grads)
    grad = jnp.broadcast_to(grad.astype(f16)[None], (8, 32, 256))
    slices = lax.all_to_all(grad, "rep", 0, 0).astype(f32)
    weight_grad = call(assemble_kernel, shape((TILE, n_out), f32), [VMEM] * 2)(slices, factor)
    return hidden, weight_grad, input_grad


def solution(mesh):
    in_specs = (
        P(("blk", "rep"), None),
        P(),
        P(),
        P(("blk", "rep")),
        P("blk", "rep", None, None, None, None),
        P("blk", "rep", None, None),
        P("blk", "rep", None),
        P(("blk", "rep"), None),
    )
    out_specs = (P(("blk", "rep"), None), P(), P(("blk", "rep"), None))
    return jax.shard_map(
        per_device, mesh=mesh, in_specs=in_specs, out_specs=out_specs, check_vma=False
    )
```

time: 140 us -> 126 us (0.900)
  starting transfers between devices: 49.4 us -> 23.3 us
  waiting for transfers between devices: 36.3 us -> 43.3 us
  Pallas kernels: 6.82 us -> 10.6 us
    ppermute x35 -> x18, starting transfers between devices: 46 us -> 19.9 us  [permute_blk(): return lax.ppermute(value, 'blk', pairs)]
    all_to_all x1, waiting for transfers between devices: 0.01 us -> 7.29 us  [per_device(): slices = lax.all_to_all(grad, 'rep', 0, 0).astype(f32)]
    pallas_call x3 -> x9, Pallas kernels: 5.4 us -> 9.14 us  [the longest x6 7.84 us: products(): call(kernel, outs, ins, scratch, 1 << 29)(place, *smem, tiles, *pieces)]
    unnamed x31 -> x27, local copies, waits for them, and re-layouts: 6.28 us -> 6.86 us
    ppermute x35 -> x18, waiting for transfers between devices: 36.3 us -> 36.1 us  [permute_blk(): return lax.ppermute(value, 'blk', pairs)]
  transfers between devices with their start and end apart: 36 -> 19, of which waited for: 13 -> 11; matrix products, arithmetic and copies ran while one was open for 3% -> 2% of each run, Pallas kernels for 0% -> 3%
where the time goes in v2:
time: 126 us; the launch traced here: 123 us
  waiting for transfers between devices  43.3 us (34%)
  blocking collectives  34.8 us (28%)
  starting transfers between devices  23.3 us (18%)
  Pallas kernels  10.6 us (8%)
  local copies, waits for them, and re-layouts  7.94 us (6%)
  other arithmetic  2.12 us (2%)
    ppermute x18, waiting for transfers between devices, permute_blk(): return lax.ppermute(value, 'blk', pairs)  36.1 us
    ppermute x18, starting transfers between devices, permute_blk(): return lax.ppermute(value, 'blk', pairs)  19.9 us
    all_to_all x1, blocking collectives, per_device(): parts = lax.all_to_all(partial.astype(f16), 'rep', 0, 0).astype(f32)  19.5 us
    all_to_all x1, blocking collectives, per_device(): got = lax.all_to_all(sent, 'rep', 0, 0).astype(f32)  15.3 us
    pallas_call x6, Pallas kernels, products(): call(kernel, outs, ins, scratch, 1 << 29)(place, *smem, tiles, *pieces)  7.84 us
    all_to_all x1, waiting for transfers between devices, per_device(): slices = lax.all_to_all(grad, 'rep', 0, 0).astype(f32)  7.29 us
    unnamed x27, local copies, waits for them, and re-layouts  6.86 us
    all_to_all x1, starting transfers between devices, per_device(): slices = lax.all_to_all(grad, 'rep', 0, 0).astype(f32)  3.37 us
  transfers between devices with their start and end apart: 19, of which 11 were waited for; matrix products, arithmetic and copies ran while one was open for 2% of the time, Pallas kernels for 3%

profile of v2, /device:TPU:32, one launch (start us, length us, event | category | flops | bytes accessed | tf_op | source)
XLA Modules:
  0.0 123.2 jit_solution(3447706580478938406)
XLA Ops:
  0.6 0.9 copy-done.2
  1.6 0.8 copy-done.4
  3.7 0.8 copy.13
  5.0 1.6 %collective-permute-start.1 = (bf16[2,272,128]{2,1,0:T(8,128)(2,1)S(1)}, bf16[2,272,128]{2,1,0:T(8,128)(2,1)S(1)}, u32[]{:S(2)}, u32[]{:S(2)}) collective-permute-start(bf16[2,272,128]{2,1,0:T(8,128)(2,1)S(1)} %constant_dynamic-update-slice_fusion.2.refs_0_), channel_id=1, source_target_pairs={{0,128},{8,136},{16,144},{24,152},{32,160},{40,168},{48,176},{56,1... | collective-permute-start | bytes 417800 | tf_op jit(solution)/shard_map/ppermute | solution.py:32
  6.6 1.9 %collective-permute-start.2 = (bf16[2,272,128]{2,1,0:T(8,128)(2,1)S(1)}, bf16[2,272,128]{2,1,0:T(8,128)(2,1)S(1)}, u32[]{:S(2)}, u32[]{:S(2)}) collective-permute-start(bf16[2,272,128]{2,1,0:T(8,128)(2,1)S(1)} %constant_dynamic-update-slice_fusion.2.refs_0_), channel_id=1, source_target_pairs={{0,16},{8,120},{16,32},{24,8},{32,48},{40,24},{48,64},{56,40},{64,... | collective-permute-start | bytes 417800 | tf_op jit(solution)/shard_map/ppermute | solution.py:32
  8.5 4.5 %collective-permute-start.3 = (bf16[2,272,128]{2,1,0:T(8,128)(2,1)S(1)}, bf16[2,272,128]{2,1,0:T(8,128)(2,1)S(1)}, u32[]{:S(2)}, u32[]{:S(2)}) collective-permute-start(bf16[2,272,128]{2,1,0:T(8,128)(2,1)S(1)} %constant_dynamic-update-slice_fusion.2.refs_0_), channel_id=1, source_target_pairs={{0,32},{8,104},{16,48},{24,120},{32,64},{40,8},{48,80},{56,24},{64... | collective-permute-start | bytes 417800 | tf_op jit(solution)/shard_map/ppermute | solution.py:32
  13.0 2.2 %copy-done = bf16[1,1,64,2,128,128]{5,4,3,2,1,0:T(8,128)(2,1)S(1)} copy-done((bf16[1,1,64,2,128,128]{5,4,3,2,1,0:T(8,128)(2,1)S(1)}, bf16[1,1,64,2,128,128]{5,4,3,2,1,0:T(8,128)(2,1)}, u32[]{:S(2)}) %copy-start) | copy-done | bytes 4194328
  15.8 0.8 shard_map.104
  17.3 2.5 %collective-permute-start.4 = (bf16[3,272,128]{2,1,0:T(8,128)(2,1)S(1)}, bf16[3,272,128]{2,1,0:T(8,128)(2,1)S(1)}, u32[]{:S(2)}, u32[]{:S(2)}) collective-permute-start(bf16[3,272,128]{2,1,0:T(8,128)(2,1)S(1)} %slice.137), channel_id=1, source_target_pairs={{0,32},{8,104},{16,48},{24,120},{32,64},{40,8},{48,80},{56,24},{64... | collective-permute-start | bytes 626696 | tf_op jit(solution)/shard_map/ppermute | solution.py:32
  19.8 0.9 shard_map.105
  20.7 6.8 %collective-permute-done.4.refs_3_ = bf16[3,272,128]{2,1,0:T(8,128)(2,1)S(1)} collective-permute-done((bf16[3,272,128]{2,1,0:T(8,128)(2,1)S(1)}, bf16[3,272,128]{2,1,0:T(8,128)(2,1)S(1)}, u32[]{:S(2)}, u32[]{:S(2)}) %collective-permute-start.4) | collective-permute-done | bytes 208928 | tf_op jit(solution)/shard_map/ppermute | solution.py:32
  28.2 1.5 %collective-permute-start.8 = (bf16[3,272,128]{2,1,0:T(8,128)(2,1)S(1)}, bf16[3,272,128]{2,1,0:T(8,128)(2,1)S(1)}, u32[]{:S(2)}, u32[]{:S(2)}) collective-permute-start(bf16[3,272,128]{2,1,0:T(8,128)(2,1)S(1)} %collective-permute-done.4.refs_3_), channel_id=1, source_target_pairs={{0,128},{8,136},{16,144},{24,152},{32,160},{40,168},{48,176},{56,1... | collective-permute-start | bytes 626696 | tf_op jit(solution)/shard_map/ppermute | solution.py:32
  29.7 1.0 shard_map.106
  30.7 4.7 %collective-permute-done.8.refs_3_ = bf16[3,272,128]{2,1,0:T(8,128)(2,1)S(1)} collective-permute-done((bf16[3,272,128]{2,1,0:T(8,128)(2,1)S(1)}, bf16[3,272,128]{2,1,0:T(8,128)(2,1)S(1)}, u32[]{:S(2)}, u32[]{:S(2)}) %collective-permute-start.8) | collective-permute-done | bytes 208928 | tf_op jit(solution)/shard_map/ppermute | solution.py:32
  35.4 1.2 %shard_map.107 = (f32[2176,128]{1,0:T(8,128)S(1)}, f32[16,128]{1,0:T(8,128)S(1)}) custom-call(s32[1]{0:T(128)} %bitcast.place_ref, s32[128]{0:T(128)S(1)} %reshape.86.rows_ref, s32[64]{0:T(128)S(1)} %bitcast.67, bf16[64,256,128]{2,1,0:T(8,128)(2,1)S(1)} %bitcast.60, f32[2176,128]{1,0:T(8,128)S(1)} %get-tuple-element.55.refs_0_, ...), custom_call_target="tpu_custom_call" | custom-call | flops 536870912 | bytes 1048576 | tf_op jit(solution)/shard_map/pallas_call | solution.py:382
  36.8 0.9 shard_map.108
  37.9 19.5 %all_to_all.15 = f16[8,272,128]{2,1,0:T(8,128)(2,1)S(1)} all-to-all(f16[8,272,128]{2,1,0:T(8,128)(2,1)S(1)} %convert_element_type.100), channel_id=1, replica_groups=mesh['blk'=32,'rep'=8] {'rep'}, dimensions={0} | all-to-all | bytes 1114112 | tf_op jit(solution)/shard_map/all_to_all | solution.py:394
  57.5 1.4 %shard_map.109 = (bf16[256,512]{1,0:T(8,128)(2,1)}, f32[128,256]{1,0:T(8,128)S(1)}, f32[8,32,256]{2,1,0:T(8,128)S(1)}, f32[2,8,128]{2,1,0:T(8,128)S(1)}) custom-call(f32[8,272,128]{2,1,0:T(8,128)S(1)} %convert_element_type.101.parts_ref, bf16[128,512]{1,0:T(8,128)(2,1)S(1)} %copy-done.6, f32[1,512]{1,0:T(1,128)S(1)} %bitcast.72, s32[2,128]{1,0:T(2,128)S(1)} %bitcast.71, ...), custom_call_target="tpu_custom_call" | custom-call | flops 134217728 | bytes 1048576 | tf_op jit(solution)/shard_map/pallas_call | solution.py:395
  59.2 15.3 %all_to_all.16 = f16[8,160,256]{2,1,0:T(8,128)(2,1)S(1)} all-to-all(f16[8,160,256]{2,1,0:T(8,128)(2,1)S(1)} %pad_maximum_fusion), channel_id=1, replica_groups=mesh['blk'=32,'rep'=8] {'rep'}, dimensions={0} | all-to-all | bytes 1310720 | tf_op jit(solution)/shard_map/all_to_all | solution.py:408
  74.7 3.0 %shard_map.110 = (f32[6,128,256]{2,1,0:T(8,128)S(1)}, f32[10,128,256]{2,1,0:T(8,128)S(1)}, f32[6,128,256]{2,1,0:T(8,128)S(1)}, f32[10,128,256]{2,1,0:T(8,128)S(1)}) custom-call(s32[1]{0:T(128)} %bitcast.place_ref, s32[128]{0:T(128)S(1)} %reshape.86.rows_ref, s32[64]{0:T(128)S(1)} %bitcast.69, bf16[64,256,128]{2,1,0:T(8,128)(2,1)S(1)} %bitcast.62, ...), custom_call_target="tpu_custom_call" | custom-call | flops 536870912 | bytes 1048576 | tf_op jit(solution)/shard_map/pallas_call | solution.py:382
  78.0 1.7 %collective-permute-done.10 = f16[800,256]{1,0:T(8,128)(2,1)S(1)} collective-permute-done((f16[800,256]{1,0:T(8,128)(2,1)S(1)}, f16[800,256]{1,0:T(8,128)(2,1)S(1)}, u32[]{:S(2)}, u32[]{:S(2)}) %collective-permute-start.10) | collective-permute-done | bytes 409632 | tf_op jit(solution)/shard_map/ppermute | solution.py:32
  81.0 6.4 %collective-permute-done.11 = f16[416,256]{1,0:T(8,128)(2,1)S(1)} collective-permute-done((f16[416,256]{1,0:T(8,128)(2,1)S(1)}, f16[416,256]{1,0:T(8,128)(2,1)S(1)}, u32[]{:S(2)}, u32[]{:S(2)}) %collective-permute-start.11) | collective-permute-done | bytes 213024 | tf_op jit(solution)/shard_map/ppermute | solution.py:32
  87.7 1.3 %collective-permute-start.14 = (f16[416,256]{1,0:T(8,128)(2,1)S(1)}, f16[416,256]{1,0:T(8,128)(2,1)S(1)}, u32[]{:S(2)}, u32[]{:S(2)}) collective-permute-start(f16[416,256]{1,0:T(8,128)(2,1)S(1)} %pad_maximum_fusion.4), channel_id=1, source_target_pairs={{0,32},{8,104},{16,48},{24,120},{32,64},{40,8},{48,80},{56,24},{64... | collective-permute-start | bytes 638984 | tf_op jit(solution)/shard_map/ppermute | solution.py:32
  90.0 7.7 %collective-permute-done.14 = f16[416,256]{1,0:T(8,128)(2,1)S(1)} collective-permute-done((f16[416,256]{1,0:T(8,128)(2,1)S(1)}, f16[416,256]{1,0:T(8,128)(2,1)S(1)}, u32[]{:S(2)}, u32[]{:S(2)}) %collective-permute-start.14) | collective-permute-done | bytes 213024 | tf_op jit(solution)/shard_map/ppermute | solution.py:32
  97.7 1.6 %collective-permute-done.13 = f16[640,256]{1,0:T(8,128)(2,1)S(1)} collective-permute-done((f16[640,256]{1,0:T(8,128)(2,1)S(1)}, f16[640,256]{1,0:T(8,128)(2,1)S(1)}, u32[]{:S(2)}, u32[]{:S(2)}) %collective-permute-start.13) | collective-permute-done | bytes 327712 | tf_op jit(solution)/shard_map/ppermute | solution.py:32
  100.1 3.3 %collective-permute-start.15 = (f16[320,256]{1,0:T(8,128)(2,1)S(1)}, f16[320,256]{1,0:T(8,128)(2,1)S(1)}, u32[]{:S(2)}, u32[]{:S(2)}) collective-permute-start(f16[320,256]{1,0:T(8,128)(2,1)S(1)} %pad_maximum_fusion.5), channel_id=1, source_target_pairs={{0,16},{8,120},{16,32},{24,8},{32,48},{40,24},{48,64},{56,40},{64,... | collective-permute-start | bytes 491528 | tf_op jit(solution)/shard_map/ppermute | solution.py:32
  103.4 5.2 %collective-permute-done.16 = f16[288,256]{1,0:T(8,128)(2,1)S(1)} collective-permute-done((f16[288,256]{1,0:T(8,128)(2,1)S(1)}, f16[288,256]{1,0:T(8,128)(2,1)S(1)}, u32[]{:S(2)}, u32[]{:S(2)}) %collective-permute-start.16) | collective-permute-done | bytes 147488 | tf_op jit(solution)/shard_map/ppermute | solution.py:32
  108.9 1.3 %collective-permute-done.17 = f16[256,256]{1,0:T(8,128)(2,1)S(1)} collective-permute-done((f16[256,256]{1,0:T(8,128)(2,1)S(1)}, f16[256,256]{1,0:T(8,128)(2,1)S(1)}, u32[]{:S(2)}, u32[]{:S(2)}) %collective-permute-start.17) | collective-permute-done | bytes 131104 | tf_op jit(solution)/shard_map/ppermute | solution.py:32
  111.1 3.4 %all-to-all-start.2 = ((f16[8,32,256]{2,1,0:T(8,128)(2,1)}), f16[8,32,256]{2,1,0:T(8,128)(2,1)S(1)}, u32[]{:S(2)}, u32[]{:S(2)}) async-start(f16[8,32,256]{2,1,0:T(8,128)(2,1)} %broadcast_in_dim.5), calls=%async_computation.2 | async-start | bytes 262144 | tf_op jit(solution)/shard_map/all_to_all | solution.py:424
  114.5 0.7 copy.14
  115.2 7.3 %all-to-all-done.2 = f16[8,32,256]{2,1,0:T(8,128)(2,1)S(1)} async-done(((f16[8,32,256]{2,1,0:T(8,128)(2,1)}), f16[8,32,256]{2,1,0:T(8,128)(2,1)S(1)}, u32[]{:S(2)}, u32[]{:S(2)}) %all-to-all-start.2) | async-done | bytes 131104 | tf_op jit(solution)/shard_map/all_to_all | solution.py:424
  122.5 0.7 shard_map.112
  (101 shorter events, 9.1 us)
Async XLA Ops:
  0.6 1.0 copy-start.2
  1.6 0.8 copy-start.4
  2.4 0.7 copy-start.9
  3.6 1.3 %collective-permute-start = (bf16[1,272,128]{2,1,0:T(8,128)(2,1)S(1)}, bf16[1,272,128]{2,1,0:T(8,128)(2,1)S(1)}, u32[]{:S(2)}, u32[]{:S(2)}) collective-permute-start(bf16[1,272,128]{2,1,0:T(8,128)(2,1)S(1)} %slice.136), channel_id=1, source_target_pairs={{0,8},{8,0},{16,24},{24,16},{32,40},{40,32},{48,56},{56,48},{64,72... | collective-permute-start | bytes 208904 | tf_op jit(solution)/shard_map/ppermute | solution.py:32
  5.0 11.6 %collective-permute-start.1 = (bf16[2,272,128]{2,1,0:T(8,128)(2,1)S(1)}, bf16[2,272,128]{2,1,0:T(8,128)(2,1)S(1)}, u32[]{:S(2)}, u32[]{:S(2)}) collective-permute-start(bf16[2,272,128]{2,1,0:T(8,128)(2,1)S(1)} %constant_dynamic-update-slice_fusion.2.refs_0_), channel_id=1, source_target_pairs={{0,128},{8,136},{16,144},{24,152},{32,160},{40,168},{48,176},{56,1... | collective-permute-start | bytes 417800 | tf_op jit(solution)/shard_map/ppermute | solution.py:32
  6.6 10.0 %collective-permute-start.2 = (bf16[2,272,128]{2,1,0:T(8,128)(2,1)S(1)}, bf16[2,272,128]{2,1,0:T(8,128)(2,1)S(1)}, u32[]{:S(2)}, u32[]{:S(2)}) collective-permute-start(bf16[2,272,128]{2,1,0:T(8,128)(2,1)S(1)} %constant_dynamic-update-slice_fusion.2.refs_0_), channel_id=1, source_target_pairs={{0,16},{8,120},{16,32},{24,8},{32,48},{40,24},{48,64},{56,40},{64,... | collective-permute-start | bytes 417800 | tf_op jit(solution)/shard_map/ppermute | solution.py:32
  8.5 8.1 %collective-permute-start.3 = (bf16[2,272,128]{2,1,0:T(8,128)(2,1)S(1)}, bf16[2,272,128]{2,1,0:T(8,128)(2,1)S(1)}, u32[]{:S(2)}, u32[]{:S(2)}) collective-permute-start(bf16[2,272,128]{2,1,0:T(8,128)(2,1)S(1)} %constant_dynamic-update-slice_fusion.2.refs_0_), channel_id=1, source_target_pairs={{0,32},{8,104},{16,48},{24,120},{32,64},{40,8},{48,80},{56,24},{64... | collective-permute-start | bytes 417800 | tf_op jit(solution)/shard_map/ppermute | solution.py:32
  13.0 2.2 %copy-start = (bf16[1,1,64,2,128,128]{5,4,3,2,1,0:T(8,128)(2,1)S(1)}, bf16[1,1,64,2,128,128]{5,4,3,2,1,0:T(8,128)(2,1)}, u32[]{:S(2)}) copy-start(bf16[1,1,64,2,128,128]{5,4,3,2,1,0:T(8,128)(2,1)} %param.12) | copy-start | bytes 12582916
  15.2 0.7 copy-start.7
  15.8 4.0 %copy-start.1 = (bf16[1,1,64,2,128,128]{5,4,3,2,1,0:T(8,128)(2,1)S(1)}, bf16[1,1,64,2,128,128]{5,4,3,2,1,0:T(8,128)(2,1)}, u32[]{:S(2)}) copy-start(bf16[1,1,64,2,128,128]{5,4,3,2,1,0:T(8,128)(2,1)} %param.12) | copy-start | bytes 12582916
  15.8 4.0 %copy-start.8 = (s32[1,1,64]{2,1,0:T(1,128)S(1)}, s32[1,1,64]{2,1,0:T(1,128)}, u32[]{:S(2)}) copy-start(s32[1,1,64]{2,1,0:T(1,128)} %param.14) | copy-start | bytes 772
  16.7 10.9 %collective-permute-start.5 = (bf16[4,272,128]{2,1,0:T(8,128)(2,1)S(1)}, bf16[4,272,128]{2,1,0:T(8,128)(2,1)S(1)}, u32[]{:S(2)}, u32[]{:S(2)}) collective-permute-start(bf16[4,272,128]{2,1,0:T(8,128)(2,1)S(1)} %constant_dynamic-update-slice_fusion.refs_3_), channel_id=1, source_target_pairs={{0,128},{8,136},{16,144},{24,152},{32,160},{40,168},{48,176},{56,1... | collective-permute-start | bytes 835592 | tf_op jit(solution)/shard_map/ppermute | solution.py:32
  17.3 10.2 %collective-permute-start.4 = (bf16[3,272,128]{2,1,0:T(8,128)(2,1)S(1)}, bf16[3,272,128]{2,1,0:T(8,128)(2,1)S(1)}, u32[]{:S(2)}, u32[]{:S(2)}) collective-permute-start(bf16[3,272,128]{2,1,0:T(8,128)(2,1)S(1)} %slice.137), channel_id=1, source_target_pairs={{0,32},{8,104},{16,48},{24,120},{32,64},{40,8},{48,80},{56,24},{64... | collective-permute-start | bytes 626696 | tf_op jit(solution)/shard_map/ppermute | solution.py:32
  27.6 7.8 %collective-permute-start.7 = (bf16[8,272,128]{2,1,0:T(8,128)(2,1)S(1)}, bf16[8,272,128]{2,1,0:T(8,128)(2,1)S(1)}, u32[]{:S(2)}, u32[]{:S(2)}) collective-permute-start(bf16[8,272,128]{2,1,0:T(8,128)(2,1)S(1)} %pad_maximum_fusion.1), channel_id=1, source_target_pairs={{0,8},{8,0},{16,24},{24,16},{32,40},{40,32},{48,56},{56,48},{64,72... | collective-permute-start | bytes 1671176 | tf_op jit(solution)/shard_map/ppermute | solution.py:32
  27.7 3.0 %collective-permute-start.6 = (bf16[3,272,128]{2,1,0:T(8,128)(2,1)S(1)}, bf16[3,272,128]{2,1,0:T(8,128)(2,1)S(1)}, u32[]{:S(2)}, u32[]{:S(2)}) collective-permute-start(bf16[3,272,128]{2,1,0:T(8,128)(2,1)S(1)} %collective-permute-done.4.refs_3_), channel_id=1, source_target_pairs={{0,8},{8,0},{16,24},{24,16},{32,40},{40,32},{48,56},{56,48},{64,72... | collective-permute-start | bytes 626696 | tf_op jit(solution)/shard_map/ppermute | solution.py:32
  28.2 7.2 %collective-permute-start.8 = (bf16[3,272,128]{2,1,0:T(8,128)(2,1)S(1)}, bf16[3,272,128]{2,1,0:T(8,128)(2,1)S(1)}, u32[]{:S(2)}, u32[]{:S(2)}) collective-permute-start(bf16[3,272,128]{2,1,0:T(8,128)(2,1)S(1)} %collective-permute-done.4.refs_3_), channel_id=1, source_target_pairs={{0,128},{8,136},{16,144},{24,152},{32,160},{40,168},{48,176},{56,1... | collective-permute-start | bytes 626696 | tf_op jit(solution)/shard_map/ppermute | solution.py:32
  35.4 1.5 %collective-permute-start.9 = (bf16[3,272,128]{2,1,0:T(8,128)(2,1)S(1)}, bf16[3,272,128]{2,1,0:T(8,128)(2,1)S(1)}, u32[]{:S(2)}, u32[]{:S(2)}) collective-permute-start(bf16[3,272,128]{2,1,0:T(8,128)(2,1)S(1)} %collective-permute-done.8.refs_3_), channel_id=1, source_target_pairs={{0,8},{8,0},{16,24},{24,16},{32,40},{40,32},{48,56},{56,48},{64,72... | collective-permute-start | bytes 626696 | tf_op jit(solution)/shard_map/ppermute | solution.py:32
  37.8 19.6 %copy-start.3 = (bf16[256,512]{1,0:T(8,128)(2,1)S(1)}, bf16[256,512]{1,0:T(8,128)(2,1)}, u32[]{:S(2)}) copy-start(bf16[256,512]{1,0:T(8,128)(2,1)} %cot_ref.1) | copy-start | bytes 786436
  37.8 19.6 %copy-start.5 = (bf16[256,128]{1,0:T(8,128)(2,1)S(1)}, bf16[256,128]{1,0:T(8,128)(2,1)}, u32[]{:S(2)}) copy-start(bf16[256,128]{1,0:T(8,128)(2,1)} %features_ref.1) | copy-start | bytes 196612
  37.8 19.6 %copy-start.6 = (bf16[128,512]{1,0:T(8,128)(2,1)S(1)}, bf16[128,512]{1,0:T(8,128)(2,1)}, u32[]{:S(2)}) copy-start(bf16[128,512]{1,0:T(8,128)(2,1)} %weight_ref.1) | copy-start | bytes 393220
  37.9 19.6 %copy-start.10 = (s32[256]{0:T(256)S(1)}, s32[256]{0:T(256)}, u32[]{:S(2)}) copy-start(s32[256]{0:T(256)} %param.11) | copy-start | bytes 3076
  37.9 19.6 %copy-start.11 = (f32[512]{0:T(512)S(1)}, f32[512]{0:T(512)}, u32[]{:S(2)}) copy-start(f32[512]{0:T(512)} %param.10) | copy-start | bytes 6148
  77.9 1.8 %collective-permute-start.10 = (f16[800,256]{1,0:T(8,128)(2,1)S(1)}, f16[800,256]{1,0:T(8,128)(2,1)S(1)}, u32[]{:S(2)}, u32[]{:S(2)}) collective-permute-start(f16[800,256]{1,0:T(8,128)(2,1)S(1)} %pad_maximum_fusion.2), channel_id=1, source_target_pairs={{0,8},{8,0},{16,24},{24,16},{32,40},{40,32},{48,56},{56,48},{64,72... | collective-permute-start | bytes 1228808 | tf_op jit(solution)/shard_map/ppermute | solution.py:32
  80.1 7.4 %collective-permute-start.11 = (f16[416,256]{1,0:T(8,128)(2,1)S(1)}, f16[416,256]{1,0:T(8,128)(2,1)S(1)}, u32[]{:S(2)}, u32[]{:S(2)}) collective-permute-start(f16[416,256]{1,0:T(8,128)(2,1)S(1)} %pad_maximum_fusion.3), channel_id=1, source_target_pairs={{0,128},{8,136},{16,144},{24,152},{32,160},{40,168},{48,176},{56,1... | collective-permute-start | bytes 638984 | tf_op jit(solution)/shard_map/ppermute | solution.py:32
  80.9 8.0 %collective-permute-start.12 = (f16[1280,256]{1,0:T(8,128)(2,1)S(1)}, f16[1280,256]{1,0:T(8,128)(2,1)S(1)}, u32[]{:S(2)}, u32[]{:S(2)}) collective-permute-start(f16[1280,256]{1,0:T(8,128)(2,1)S(1)} %bitcast.80), channel_id=1, source_target_pairs={{0,8},{8,0},{16,24},{24,16},{32,40},{40,32},{48,56},{56,48},{64,72... | collective-permute-start | bytes 1966088 | tf_op jit(solution)/shard_map/ppermute | solution.py:32
  87.7 10.0 %collective-permute-start.14 = (f16[416,256]{1,0:T(8,128)(2,1)S(1)}, f16[416,256]{1,0:T(8,128)(2,1)S(1)}, u32[]{:S(2)}, u32[]{:S(2)}) collective-permute-start(f16[416,256]{1,0:T(8,128)(2,1)S(1)} %pad_maximum_fusion.4), channel_id=1, source_target_pairs={{0,32},{8,104},{16,48},{24,120},{32,64},{40,8},{48,80},{56,24},{64... | collective-permute-start | bytes 638984 | tf_op jit(solution)/shard_map/ppermute | solution.py:32
  89.2 10.1 %collective-permute-start.13 = (f16[640,256]{1,0:T(8,128)(2,1)S(1)}, f16[640,256]{1,0:T(8,128)(2,1)S(1)}, u32[]{:S(2)}, u32[]{:S(2)}) collective-permute-start(f16[640,256]{1,0:T(8,128)(2,1)S(1)} %bitcast.84), channel_id=1, source_target_pairs={{0,128},{8,136},{16,144},{24,152},{32,160},{40,168},{48,176},{56,1... | collective-permute-start | bytes 983048 | tf_op jit(solution)/shard_map/ppermute | solution.py:32
  99.6 8.9 %collective-permute-start.16 = (f16[288,256]{1,0:T(8,128)(2,1)S(1)}, f16[288,256]{1,0:T(8,128)(2,1)S(1)}, u32[]{:S(2)}, u32[]{:S(2)}) collective-permute-start(f16[288,256]{1,0:T(8,128)(2,1)S(1)} %pad_maximum_fusion.6), channel_id=1, source_target_pairs={{0,32},{8,104},{16,48},{24,120},{32,64},{40,8},{48,80},{56,24},{64... | collective-permute-start | bytes 442376 | tf_op jit(solution)/shard_map/ppermute | solution.py:32
  100.1 8.5 %collective-permute-start.15 = (f16[320,256]{1,0:T(8,128)(2,1)S(1)}, f16[320,256]{1,0:T(8,128)(2,1)S(1)}, u32[]{:S(2)}, u32[]{:S(2)}) collective-permute-start(f16[320,256]{1,0:T(8,128)(2,1)S(1)} %pad_maximum_fusion.5), channel_id=1, source_target_pairs={{0,16},{8,120},{16,32},{24,8},{32,48},{40,24},{48,64},{56,40},{64,... | collective-permute-start | bytes 491528 | tf_op jit(solution)/shard_map/ppermute | solution.py:32
  108.8 1.4 %collective-permute-start.17 = (f16[256,256]{1,0:T(8,128)(2,1)S(1)}, f16[256,256]{1,0:T(8,128)(2,1)S(1)}, u32[]{:S(2)}, u32[]{:S(2)}) collective-permute-start(f16[256,256]{1,0:T(8,128)(2,1)S(1)} %pad_maximum_fusion.9), channel_id=1, source_target_pairs={{0,8},{8,0},{16,24},{24,16},{32,40},{40,32},{48,56},{56,48},{64,72... | collective-permute-start | bytes 393224 | tf_op jit(solution)/shard_map/ppermute | solution.py:32
  111.1 11.4 %all-to-all-start.2 = ((f16[8,32,256]{2,1,0:T(8,128)(2,1)}), f16[8,32,256]{2,1,0:T(8,128)(2,1)S(1)}, u32[]{:S(2)}, u32[]{:S(2)}) async-start(f16[8,32,256]{2,1,0:T(8,128)(2,1)} %broadcast_in_dim.5), calls=%async_computation.2 | async-start | bytes 262144 | tf_op jit(solution)/shard_map/all_to_all | solution.py:424

commit v3 on v2

--- a/solution.py
+++ b/solution.py
@@ -38,6 +38,10 @@
 
 def to_x(x, z, c):
     return 1 - x, z, c
+
+
+def to_z_xor(bits, other_x=0):
+    return lambda x, z, c: (x ^ other_x, z ^ bits, c)
 
 
 def to_z_by_core(distance):
@@ -148,9 +152,9 @@
     [[(1, -1, 0), (1, -1, 1), (1, -2, 0), (1, -2, 1)], [(0, -3, 0), (0, -3, 1), (0, 4, 0)]],
     [
         [(dx, i, dc) for dx in (0, 1) for i in (1, 2) for dc in (1, 0)],
-        [(1, -3, 0), (1, -3, 1), (1, 4, 0)],
         [(0, 3, 1), (0, 3, 0), (0, 4, 1)],
     ],
+    [[(1, -3, 0), (1, -3, 1), (1, 4, 0)]],
 ]
 LAST_ORDER = [[(1, 3, 1), (1, 3, 0), (1, 4, 1)]]
 
@@ -230,25 +234,24 @@
                 ref[at, :, half * TILE : (half + 1) * TILE] = both[:TILE] + both[TILE:]
 
 
-def sum_kernel(place_ref, own_ref, mine_ref, theirs_ref, out_ref):
-    z, c = place_ref[0] // N_C % N_Z, place_ref[0] % N_C
-    total = None
-    for at in range(N_Z):
-        below = (z - at + N_Z) % N_Z
-        index = jnp.where(below <= 4, below, N_Z - below)
-        side = jnp.where(below <= 4, c, 1 - c)
-        index = jnp.maximum(index, 1) - 1
-        value = jnp.where(side == 0, mine_ref[index], theirs_ref[index])
-        value = jnp.where(below == 0, own_ref[...], value)
-        total = value if total is None else total + value
-    out_ref[...] = total
-
-
-def assemble_kernel(slices_ref, factor_ref, out_ref):
+def join_kernel(first_ref, second_ref, _, out_ref):
+    n = first_ref.shape[0]
+    out_ref[:n] = first_ref[...]
+    out_ref[n:] = second_ref[...]
+
+
+def copy_kernel(value_ref, *refs):
+    refs[-1][...] = value_ref[...]
+
+
+def finish_kernel(mine_ref, theirs_ref, degree_ref, factor_ref, slices_ref, input_ref, weight_ref):
     factor = jnp.concatenate([factor_ref[1, :1, :]] * 2, 1)
     for r in range(slices_ref.shape[0]):
         i, j = r // 2, r % 2
-        out_ref[i * 32 : (i + 1) * 32, j * 256 : (j + 1) * 256] = slices_ref[r] * factor
+        weight_ref[i * 32 : (i + 1) * 32, j * 256 : (j + 1) * 256] = slices_ref[r] * factor
+    _, column_scale = scale_of(degree_ref[...])
+    total = (mine_ref[...] + theirs_ref[...]).T
+    input_ref[...] = (column_scale * total * factor_ref[0, :1, :]).astype(bf16)
 
 
 GIVE_FAR = [(dx, *rest) for dx in (1, 0) for rest in ((4, 1), (-3, 1), (-3, 0))]
@@ -300,48 +303,62 @@
         permute_blk(near[:3], to_z_by_core(2)),
         permute_blk(near, to_x),
     )
-    *begun, far_core, near_core, far_x = together(
+    far_x = permute_blk(far, to_x)
+    all_near = call(join_kernel, shape((8, BLOCK, TILE), bf16), [VMEM] * 3, cost=1 << 31)(
+        near, near_x, far
+    )
+    *begun, far_core, near_core = together(
         *forward(2, *begun, near_x, far),
         permute_blk(far, to_core),
-        permute_blk(jnp.concatenate([near, near_x]), to_core),
-        permute_blk(far, to_x),
-    )
-    return together(
-        *forward(3, *begun, near_core, far_x, far_core), permute_blk(far_x, to_core)
-    )
-
-
-def scatter_terms(give_far, give_near, keep_far, keep_near, grad):
-    def send(move, *values):
-        sizes = [value.size // OWN for value in values]
-        message = [value.astype(f16).reshape(-1, OWN) for value in values]
-        got = permute_blk(jnp.concatenate(message) if len(message) > 1 else message[0], move)
-        got = got.astype(f32)
-        starts = [sum(sizes[:i]) for i in range(len(sizes))]
-        return [
-            got[at : at + size].reshape(value.shape)
-            for at, size, value in zip(starts, sizes, values)
-        ]
-
+        permute_blk(all_near, to_core),
+    )
+    *begun, far_x = together(*forward(3, *begun, near_core, far_core), far_x)
+    return together(*forward(4, *begun, far_x), permute_blk(far_x, to_core))
+
+
+def behind(value, *others):
+    corners = [other.reshape(-1, OWN)[:16, :TILE].astype(f32) for other in others]
+    ins = [VMEM] * (1 + len(others))
+    return call(copy_kernel, shape(value.shape, value.dtype), ins, cost=1 << 31)(value, *corners)
+
+
+def scatter_terms(backward, grad):
     def rounded(value):
         return value.astype(f16).astype(f32)
 
-    far, more = send(to_core, give_far, grad)
+    def with_grad(terms, grad):
+        return jnp.concatenate([terms.reshape(-1, OWN), grad]).astype(f16)
+
+    def parted(got, terms):
+        n = terms.shape[0] * TILE
+        got = got.astype(f32)
+        return got[:n].reshape(terms.shape), got[n:]
+
+    give_far, keep_far = backward(GIVE_FAR, KEEP_FAR)
+    far, more = parted(permute_blk(with_grad(give_far, grad), to_core), give_far)
+    give_near, keep_near = backward(GIVE_NEAR, KEEP_NEAR)
     far, grad = keep_far + far, rounded(rounded(grad) + more)
-    far_x, more = send(to_x, far[:3], grad)
-    far, grad = far[3:] + far_x, rounded(grad + more)
-    (near,) = send(to_core, give_near)
-    near = keep_near + near
-    (near_x,) = send(to_x, near[:5])
-    passed, grad_2 = send(to_z_by_core(2), far, grad)
+    out = after(with_grad(far[:3], grad))
+    mine = behind(grad, out).astype(f16)
+    fan = [permute_blk(mine, to_z_xor(1, other_x)).astype(f32) for other_x in (0, 1)]
+    far_x, more = parted(permute_blk(out, to_x), far[:3])
+    near = keep_near + permute_blk(give_near.astype(f16), to_core).astype(f32)
+    far = far[3:] + far_x
+    grad = rounded((grad + more) + (fan[0] + fan[1]))
+    out = after(with_grad(far, grad))
+    near_out = after(near[:5].astype(f16))
+    mine = behind(grad, out, near_out).astype(f16)
+    grad = grad + permute_blk(mine, to_z_xor(4)).astype(f32)
+    near_x = permute_blk(near_out, to_x).astype(f32)
+    out = permute_blk(out, to_z_by_core(2))
+    passed, more = parted(out, far)
+    grad = grad + (more + permute_blk(out[-32:], to_core).astype(f32))
     near = near[5:] + near_x
-    two = jnp.concatenate([near[:1] + passed[:1], near[1:2]])
-    got_2, grad_4 = send(to_z_by_core(2), two, grad_2)
-    got_1, grad_1, grad_3 = send(to_z_by_core(1), near[2:4] + passed[1:], grad, grad_2)
-    got = got_2 + got_1
-    mine = jnp.stack([grad_1, grad_2, grad_3, grad_4])
-    other, theirs = send(to_core, got[1], mine)
-    return near[4] + got[0] + other, grad, mine, theirs
+    two = jnp.concatenate([near[:1] + passed[:1], near[1:2]]).astype(f16)
+    two, one = together(two, (near[2:4] + passed[1:]).astype(f16))
+    grad = after(jnp.broadcast_to(grad.astype(f16)[None], (8, 32, 256)), two, one)
+    got = permute_blk(two, to_z_by_core(2)).astype(f32) + permute_blk(one, to_z_by_core(1)).astype(f32)
+    return near[4] + got[0], permute_blk(got[1].astype(f16), to_core).astype(f32), grad
 
 
 def per_device(
@@ -408,21 +425,19 @@
     got = lax.all_to_all(sent, "rep", 0, 0).astype(f32)
     got_back = got[:, :TILE]
 
-    orders = (GIVE_FAR, GIVE_NEAR, KEEP_FAR, KEEP_NEAR)
-    terms = products(
-        functools.partial(backward_kernel, orders),
-        tuple(shape((len(order), TILE, OWN), f32) for order in orders),
-        [pltpu.VMEM((ROW_TILES + 1, 2 * TILE, TILE), bf16)],
-        got_back,
-    )
-    total, *grads = scatter_terms(*terms, jnp.sum(got[:, TILE:], 0))
-    row_scale = 1.0 / jnp.sqrt(node_degree.astype(f32))
-    input_grad = ((total * row_scale[None, :]).T * factor[0, :1, :]).astype(bf16)
-
-    grad = call(sum_kernel, shape((32, 256), f32), [SMEM] + [VMEM] * 3)(place, *grads)
-    grad = jnp.broadcast_to(grad.astype(f16)[None], (8, 32, 256))
+    def backward(*orders):
+        return products(
+            functools.partial(backward_kernel, orders),
+            tuple(shape((len(order), TILE, OWN), f32) for order in orders),
+            [pltpu.VMEM((ROW_TILES + 1, 2 * TILE, TILE), bf16)],
+            got_back,
+        )
+
+    *halves, grad = scatter_terms(backward, jnp.sum(got[:, TILE:], 0))
     slices = lax.all_to_all(grad, "rep", 0, 0).astype(f32)
-    weight_grad = call(assemble_kernel, shape((TILE, n_out), f32), [VMEM] * 2)(slices, factor)
+    input_grad, weight_grad = call(
+        finish_kernel, (shape((OWN, TILE), bf16), shape((TILE, n_out), f32)), [VMEM] * 5
+    )(*halves, degree, factor, slices)
     return hidden, weight_grad, input_grad
 
 

time: 126 us -> 116 us (0.921); the launches traced: 123 us -> 116 us
  waiting for transfers between devices: 43.3 us -> 30.4 us
  starting transfers between devices: 23.3 us -> 28.6 us
  Pallas kernels: 10.6 us -> 12.3 us
    ppermute x18 -> x22, waiting for transfers between devices: 36.1 us -> 22.6 us  [permute_blk(): return lax.ppermute(value, 'blk', pairs)]
    ppermute x18 -> x22, starting transfers between devices: 19.9 us -> 25.2 us  [permute_blk(): return lax.ppermute(value, 'blk', pairs)]
    pallas_call x6 -> x8, Pallas kernels: 7.84 us -> 9.37 us  [products(): call(kernel, outs, ins, scratch, 1 << 29)(place, *smem, tiles, *pieces)]
    unnamed x27 -> x26, local copies, waits for them, and re-layouts: 6.86 us -> 6.12 us
  transfers between devices with their start and end apart: 19 -> 23, of which waited for: 11 -> 10; matrix products, arithmetic and copies ran while one was open for 2% -> 2% of each run, Pallas kernels for 3% -> 6%
where the time goes in v3:
time: 116 us
  blocking collectives  34.1 us (29%)
  waiting for transfers between devices  30.4 us (26%)
  starting transfers between devices  28.6 us (25%)
  Pallas kernels  12.3 us (11%)
  local copies, waits for them, and re-layouts  7.2 us (6%)
  other arithmetic  1.82 us (2%)
  between operations  1.2 us (1%)
    ppermute x22, starting transfers between devices, permute_blk(): return lax.ppermute(value, 'blk', pairs)  25.2 us
    ppermute x22, waiting for transfers between devices, permute_blk(): return lax.ppermute(value, 'blk', pairs)  22.6 us
    all_to_all x1, blocking collectives, per_device(): parts = lax.all_to_all(partial.astype(f16), 'rep', 0, 0).astype(f32)  19 us
    all_to_all x1, blocking collectives, per_device(): got = lax.all_to_all(sent, 'rep', 0, 0).astype(f32)  15.1 us
    pallas_call x8, Pallas kernels, products(): call(kernel, outs, ins, scratch, 1 << 29)(place, *smem, tiles, *pieces)  9.37 us
    all_to_all x1, waiting for transfers between devices, per_device(): slices = lax.all_to_all(grad, 'rep', 0, 0).astype(f32)  7.83 us
    unnamed x26, local copies, waits for them, and re-layouts  6.12 us
    all_to_all x1, starting transfers between devices, per_device(): slices = lax.all_to_all(grad, 'rep', 0, 0).astype(f32)  3.37 us
  transfers between devices with their start and end apart: 23, of which 10 were waited for; matrix products, arithmetic and copies ran while one was open for 2% of the time, Pallas kernels for 6%

profile of v3, /device:TPU:32, one launch (start us, length us, event | category | flops | bytes accessed | tf_op | source)
XLA Modules:
  0.0 115.6 jit_solution(10740708037540466859)
XLA Ops:
  0.6 0.9 copy-done.2
  1.6 0.8 copy-done.4
  5.0 3.3 %collective-permute-start.3 = (bf16[2,272,128]{2,1,0:T(8,128)(2,1)S(1)}, bf16[2,272,128]{2,1,0:T(8,128)(2,1)S(1)}, u32[]{:S(2)}, u32[]{:S(2)}) collective-permute-start(bf16[2,272,128]{2,1,0:T(8,128)(2,1)S(1)} %constant_dynamic-update-slice_fusion.2.refs_0_), channel_id=1, source_target_pairs={{0,32},{8,104},{16,48},{24,120},{32,64},{40,8},{48,80},{56,24},{64... | collective-permute-start | bytes 417800 | tf_op jit(solution)/shard_map/ppermute | solution.py:32
  8.3 3.1 %collective-permute-start.2 = (bf16[2,272,128]{2,1,0:T(8,128)(2,1)S(1)}, bf16[2,272,128]{2,1,0:T(8,128)(2,1)S(1)}, u32[]{:S(2)}, u32[]{:S(2)}) collective-permute-start(bf16[2,272,128]{2,1,0:T(8,128)(2,1)S(1)} %constant_dynamic-update-slice_fusion.2.refs_0_), channel_id=1, source_target_pairs={{0,16},{8,120},{16,32},{24,8},{32,48},{40,24},{48,64},{56,40},{64,... | collective-permute-start | bytes 417800 | tf_op jit(solution)/shard_map/ppermute | solution.py:32
  11.5 1.5 %collective-permute-start.1 = (bf16[2,272,128]{2,1,0:T(8,128)(2,1)S(1)}, bf16[2,272,128]{2,1,0:T(8,128)(2,1)S(1)}, u32[]{:S(2)}, u32[]{:S(2)}) collective-permute-start(bf16[2,272,128]{2,1,0:T(8,128)(2,1)S(1)} %constant_dynamic-update-slice_fusion.2.refs_0_), channel_id=1, source_target_pairs={{0,128},{8,136},{16,144},{24,152},{32,160},{40,168},{48,176},{56,1... | collective-permute-start | bytes 417800 | tf_op jit(solution)/shard_map/ppermute | solution.py:32
  13.0 2.2 %copy-done = bf16[1,1,64,2,128,128]{5,4,3,2,1,0:T(8,128)(2,1)S(1)} copy-done((bf16[1,1,64,2,128,128]{5,4,3,2,1,0:T(8,128)(2,1)S(1)}, bf16[1,1,64,2,128,128]{5,4,3,2,1,0:T(8,128)(2,1)}, u32[]{:S(2)}) %copy-start) | copy-done | bytes 4194328
  15.8 0.8 shard_map.104
  16.7 1.6 %collective-permute-start.5 = (bf16[4,272,128]{2,1,0:T(8,128)(2,1)S(1)}, bf16[4,272,128]{2,1,0:T(8,128)(2,1)S(1)}, u32[]{:S(2)}, u32[]{:S(2)}) collective-permute-start(bf16[4,272,128]{2,1,0:T(8,128)(2,1)S(1)} %constant_dynamic-update-slice_fusion.refs_3_.first_ref), channel_id=1, source_target_pairs={{0,128},{8,136},{16,144},{24,152},{32,160},{40,168},{48,176},{56,1... | collective-permute-start | bytes 835592 | tf_op jit(solution)/shard_map/ppermute | solution.py:32
  18.3 1.8 %collective-permute-start.4 = (bf16[3,272,128]{2,1,0:T(8,128)(2,1)S(1)}, bf16[3,272,128]{2,1,0:T(8,128)(2,1)S(1)}, u32[]{:S(2)}, u32[]{:S(2)}) collective-permute-start(bf16[3,272,128]{2,1,0:T(8,128)(2,1)S(1)} %slice.116), channel_id=1, source_target_pairs={{0,32},{8,104},{16,48},{24,120},{32,64},{40,8},{48,80},{56,24},{64... | collective-permute-start | bytes 626696 | tf_op jit(solution)/shard_map/ppermute | solution.py:32
  20.1 0.9 shard_map.105
  21.0 7.5 %collective-permute-done.4.refs_3_._ = bf16[3,272,128]{2,1,0:T(8,128)(2,1)S(1)} collective-permute-done((bf16[3,272,128]{2,1,0:T(8,128)(2,1)S(1)}, bf16[3,272,128]{2,1,0:T(8,128)(2,1)S(1)}, u32[]{:S(2)}, u32[]{:S(2)}) %collective-permute-start.4) | collective-permute-done | bytes 208928 | tf_op jit(solution)/shard_map/ppermute | solution.py:32
  29.7 1.0 shard_map.106
  30.9 1.1 shard_map.108
  32.0 4.3 %collective-permute-done.8.refs_2_ = bf16[3,272,128]{2,1,0:T(8,128)(2,1)S(1)} collective-permute-done((bf16[3,272,128]{2,1,0:T(8,128)(2,1)S(1)}, bf16[3,272,128]{2,1,0:T(8,128)(2,1)S(1)}, u32[]{:S(2)}, u32[]{:S(2)}) %collective-permute-start.8) | collective-permute-done | bytes 208928 | tf_op jit(solution)/shard_map/ppermute | solution.py:32
  36.3 0.8 shard_map.109
  37.8 0.9 shard_map.110
  38.8 19.0 %all_to_all.15 = f16[8,272,128]{2,1,0:T(8,128)(2,1)S(1)} all-to-all(f16[8,272,128]{2,1,0:T(8,128)(2,1)S(1)} %convert_element_type.98), channel_id=1, replica_groups=mesh['blk'=32,'rep'=8] {'rep'}, dimensions={0} | all-to-all | bytes 1114112 | tf_op jit(solution)/shard_map/all_to_all | solution.py:411
  58.0 1.4 %shard_map.111 = (bf16[256,512]{1,0:T(8,128)(2,1)}, f32[128,256]{1,0:T(8,128)S(1)}, f32[8,32,256]{2,1,0:T(8,128)S(1)}, f32[2,8,128]{2,1,0:T(8,128)S(1)}) custom-call(f32[8,272,128]{2,1,0:T(8,128)S(1)} %convert_element_type.99.parts_ref, bf16[128,512]{1,0:T(8,128)(2,1)S(1)} %copy-done.6, f32[1,512]{1,0:T(1,128)S(1)} %bitcast.43, s32[2,128]{1,0:T(2,128)S(1)} %bitcast.41, ...), custom_call_target="tpu_custom_call" | custom-call | flops 134217728 | bytes 1048576 | tf_op jit(solution)/shard_map/pallas_call | solution.py:412
  59.6 15.1 %all_to_all.16 = f16[8,160,256]{2,1,0:T(8,128)(2,1)S(1)} all-to-all(f16[8,160,256]{2,1,0:T(8,128)(2,1)S(1)} %pad_maximum_fusion), channel_id=1, replica_groups=mesh['blk'=32,'rep'=8] {'rep'}, dimensions={0} | all-to-all | bytes 1310720 | tf_op jit(solution)/shard_map/all_to_all | solution.py:425
  75.0 1.7 %shard_map.113 = (f32[6,128,256]{2,1,0:T(8,128)S(1)}, f32[6,128,256]{2,1,0:T(8,128)S(1)}) custom-call(s32[1]{0:T(128)} %bitcast.place_ref, s32[128]{0:T(128)S(1)} %reshape.53.rows_ref, s32[64]{0:T(128)S(1)} %bitcast.38, bf16[64,256,128]{2,1,0:T(8,128)(2,1)S(1)} %bitcast.30, f32[8,128,256]{2,1,0:T(8,128)S(1)} %slice.117.back_ref), custom_call_target="tpu_custom_call" | custom-call | flops 536870912 | bytes 1048576 | tf_op jit(solution)/shard_map/pallas_call | solution.py:399
  77.1 1.7 %collective-permute-done.12 = f16[800,256]{1,0:T(8,128)(2,1)S(1)} collective-permute-done((f16[800,256]{1,0:T(8,128)(2,1)S(1)}, f16[800,256]{1,0:T(8,128)(2,1)S(1)}, u32[]{:S(2)}, u32[]{:S(2)}) %collective-permute-start.12) | collective-permute-done | bytes 409632 | tf_op jit(solution)/shard_map/ppermute | solution.py:32
  79.6 1.4 %collective-permute-start.15 = (f16[32,256]{1,0:T(8,128)(2,1)S(1)}, f16[32,256]{1,0:T(8,128)(2,1)S(1)}, u32[]{:S(2)}, u32[]{:S(2)}) collective-permute-start(f16[32,256]{1,0:T(8,128)(2,1)S(1)} %convert_element_type.110), channel_id=1, source_target_pairs={{0,144},{8,152},{16,128},{24,136},{32,176},{40,184},{48,160},{56,1... | collective-permute-start | bytes 49160 | tf_op jit(solution)/shard_map/ppermute | solution.py:32
  81.0 1.9 %collective-permute-start.14 = (f16[32,256]{1,0:T(8,128)(2,1)S(1)}, f16[32,256]{1,0:T(8,128)(2,1)S(1)}, u32[]{:S(2)}, u32[]{:S(2)}) collective-permute-start(f16[32,256]{1,0:T(8,128)(2,1)S(1)} %convert_element_type.110), channel_id=1, source_target_pairs={{0,16},{8,24},{16,0},{24,8},{32,48},{40,56},{48,32},{56,40},{64,80... | collective-permute-start | bytes 49160 | tf_op jit(solution)/shard_map/ppermute | solution.py:32
  82.9 2.2 %shard_map.112 = (f32[10,128,256]{2,1,0:T(8,128)S(1)}, f32[10,128,256]{2,1,0:T(8,128)S(1)}) custom-call(s32[1]{0:T(128)} %bitcast.place_ref, s32[128]{0:T(128)S(1)} %reshape.53.rows_ref, s32[64]{0:T(128)S(1)} %bitcast.39, bf16[64,256,128]{2,1,0:T(8,128)(2,1)S(1)} %bitcast.31, f32[8,128,256]{2,1,0:T(8,128)S(1)} %slice.117.back_ref), custom_call_target="tpu_custom_call" | custom-call | flops 536870912 | bytes 1048576 | tf_op jit(solution)/shard_map/pallas_call | solution.py:399
  85.3 1.6 %collective-permute-done.13 = f16[416,256]{1,0:T(8,128)(2,1)S(1)} collective-permute-done((f16[416,256]{1,0:T(8,128)(2,1)S(1)}, f16[416,256]{1,0:T(8,128)(2,1)S(1)}, u32[]{:S(2)}, u32[]{:S(2)}) %collective-permute-start.13) | collective-permute-done | bytes 213024 | tf_op jit(solution)/shard_map/ppermute | solution.py:32
  88.6 3.0 %collective-permute-start.20 = (f16[32,256]{1,0:T(8,128)(2,1)S(1)}, f16[32,256]{1,0:T(8,128)(2,1)S(1)}, u32[]{:S(2)}, u32[]{:S(2)}) collective-permute-start(f16[32,256]{1,0:T(8,128)(2,1)S(1)} %convert_element_type.123), channel_id=1, source_target_pairs={{0,64},{8,72},{16,80},{24,88},{32,96},{40,104},{48,112},{56,120},{... | collective-permute-start | bytes 49160 | tf_op jit(solution)/shard_map/ppermute | solution.py:32
  91.6 6.2 %collective-permute-done.16 = f16[416,256]{1,0:T(8,128)(2,1)S(1)} collective-permute-done((f16[416,256]{1,0:T(8,128)(2,1)S(1)}, f16[416,256]{1,0:T(8,128)(2,1)S(1)}, u32[]{:S(2)}, u32[]{:S(2)}) %collective-permute-start.16) | collective-permute-done | bytes 213024 | tf_op jit(solution)/shard_map/ppermute | solution.py:32
  98.1 1.4 %collective-permute-start.17 = (f16[2,128,256]{2,1,0:T(8,128)(2,1)S(1)}, f16[2,128,256]{2,1,0:T(8,128)(2,1)S(1)}, u32[]{:S(2)}, u32[]{:S(2)}) collective-permute-start(f16[2,128,256]{2,1,0:T(8,128)(2,1)S(1)} %pad_maximum_fusion.4), channel_id=1, source_target_pairs={{0,32},{8,104},{16,48},{24,120},{32,64},{40,8},{48,80},{56,24},{64... | collective-permute-start | bytes 393224 | tf_op jit(solution)/shard_map/ppermute | solution.py:32
  99.5 3.0 %collective-permute-start.18 = (f16[2,128,256]{2,1,0:T(8,128)(2,1)S(1)}, f16[2,128,256]{2,1,0:T(8,128)(2,1)S(1)}, u32[]{:S(2)}, u32[]{:S(2)}) collective-permute-start(f16[2,128,256]{2,1,0:T(8,128)(2,1)S(1)} %fusion.1), channel_id=1, source_target_pairs={{0,16},{8,120},{16,32},{24,8},{32,48},{40,24},{48,64},{56,40},{64,... | collective-permute-start | bytes 393224 | tf_op jit(solution)/shard_map/ppermute | solution.py:32
  103.2 3.4 %all-to-all-start.2 = ((f16[8,32,256]{2,1,0:T(8,128)(2,1)}), f16[8,32,256]{2,1,0:T(8,128)(2,1)S(1)}, u32[]{:S(2)}, u32[]{:S(2)}) async-start(f16[8,32,256]{2,1,0:T(8,128)(2,1)} %broadcast_in_dim.5), calls=%async_computation.2 | async-start | bytes 262144 | tf_op jit(solution)/shard_map/all_to_all | solution.py:437
  106.8 7.8 %all-to-all-done.2 = f16[8,32,256]{2,1,0:T(8,128)(2,1)S(1)} async-done(((f16[8,32,256]{2,1,0:T(8,128)(2,1)}), f16[8,32,256]{2,1,0:T(8,128)(2,1)S(1)}, u32[]{:S(2)}, u32[]{:S(2)}) %all-to-all-start.2) | async-done | bytes 131104 | tf_op jit(solution)/shard_map/all_to_all | solution.py:437
  114.7 0.9 shard_map.116
  (105 shorter events, 10.0 us)
Async XLA Ops:
  0.6 1.0 copy-start.2
  3.6 1.3 %collective-permute-start = (bf16[1,272,128]{2,1,0:T(8,128)(2,1)S(1)}, bf16[1,272,128]{2,1,0:T(8,128)(2,1)S(1)}, u32[]{:S(2)}, u32[]{:S(2)}) collective-permute-start(bf16[1,272,128]{2,1,0:T(8,128)(2,1)S(1)} %slice.115), channel_id=1, source_target_pairs={{0,8},{8,0},{16,24},{24,16},{32,40},{40,32},{48,56},{56,48},{64,72... | collective-permute-start | bytes 208904 | tf_op jit(solution)/shard_map/ppermute | solution.py:32
  5.0 11.6 %collective-permute-start.3 = (bf16[2,272,128]{2,1,0:T(8,128)(2,1)S(1)}, bf16[2,272,128]{2,1,0:T(8,128)(2,1)S(1)}, u32[]{:S(2)}, u32[]{:S(2)}) collective-permute-start(bf16[2,272,128]{2,1,0:T(8,128)(2,1)S(1)} %constant_dynamic-update-slice_fusion.2.refs_0_), channel_id=1, source_target_pairs={{0,32},{8,104},{16,48},{24,120},{32,64},{40,8},{48,80},{56,24},{64... | collective-permute-start | bytes 417800 | tf_op jit(solution)/shard_map/ppermute | solution.py:32
  8.3 8.3 %collective-permute-start.2 = (bf16[2,272,128]{2,1,0:T(8,128)(2,1)S(1)}, bf16[2,272,128]{2,1,0:T(8,128)(2,1)S(1)}, u32[]{:S(2)}, u32[]{:S(2)}) collective-permute-start(bf16[2,272,128]{2,1,0:T(8,128)(2,1)S(1)} %constant_dynamic-update-slice_fusion.2.refs_0_), channel_id=1, source_target_pairs={{0,16},{8,120},{16,32},{24,8},{32,48},{40,24},{48,64},{56,40},{64,... | collective-permute-start | bytes 417800 | tf_op jit(solution)/shard_map/ppermute | solution.py:32
  11.5 5.2 %collective-permute-start.1 = (bf16[2,272,128]{2,1,0:T(8,128)(2,1)S(1)}, bf16[2,272,128]{2,1,0:T(8,128)(2,1)S(1)}, u32[]{:S(2)}, u32[]{:S(2)}) collective-permute-start(bf16[2,272,128]{2,1,0:T(8,128)(2,1)S(1)} %constant_dynamic-update-slice_fusion.2.refs_0_), channel_id=1, source_target_pairs={{0,128},{8,136},{16,144},{24,152},{32,160},{40,168},{48,176},{56,1... | collective-permute-start | bytes 417800 | tf_op jit(solution)/shard_map/ppermute | solution.py:32
  13.0 2.2 %copy-start = (bf16[1,1,64,2,128,128]{5,4,3,2,1,0:T(8,128)(2,1)S(1)}, bf16[1,1,64,2,128,128]{5,4,3,2,1,0:T(8,128)(2,1)}, u32[]{:S(2)}) copy-start(bf16[1,1,64,2,128,128]{5,4,3,2,1,0:T(8,128)(2,1)} %param.12) | copy-start | bytes 12582916
  15.8 4.3 %copy-start.1 = (bf16[1,1,64,2,128,128]{5,4,3,2,1,0:T(8,128)(2,1)S(1)}, bf16[1,1,64,2,128,128]{5,4,3,2,1,0:T(8,128)(2,1)}, u32[]{:S(2)}) copy-start(bf16[1,1,64,2,128,128]{5,4,3,2,1,0:T(8,128)(2,1)} %param.12) | copy-start | bytes 12582916
  16.7 11.8 %collective-permute-start.5 = (bf16[4,272,128]{2,1,0:T(8,128)(2,1)S(1)}, bf16[4,272,128]{2,1,0:T(8,128)(2,1)S(1)}, u32[]{:S(2)}, u32[]{:S(2)}) collective-permute-start(bf16[4,272,128]{2,1,0:T(8,128)(2,1)S(1)} %constant_dynamic-update-slice_fusion.refs_3_.first_ref), channel_id=1, source_target_pairs={{0,128},{8,136},{16,144},{24,152},{32,160},{40,168},{48,176},{56,1... | collective-permute-start | bytes 835592 | tf_op jit(solution)/shard_map/ppermute | solution.py:32
  18.3 10.2 %collective-permute-start.4 = (bf16[3,272,128]{2,1,0:T(8,128)(2,1)S(1)}, bf16[3,272,128]{2,1,0:T(8,128)(2,1)S(1)}, u32[]{:S(2)}, u32[]{:S(2)}) collective-permute-start(bf16[3,272,128]{2,1,0:T(8,128)(2,1)S(1)} %slice.116), channel_id=1, source_target_pairs={{0,32},{8,104},{16,48},{24,120},{32,64},{40,8},{48,80},{56,24},{64... | collective-permute-start | bytes 626696 | tf_op jit(solution)/shard_map/ppermute | solution.py:32
  28.5 1.2 %copy-start.8 = (s32[1,1,64]{2,1,0:T(1,128)S(1)}, s32[1,1,64]{2,1,0:T(1,128)}, u32[]{:S(2)}) copy-start(s32[1,1,64]{2,1,0:T(1,128)} %param.14) | copy-start | bytes 772
  28.6 2.3 %collective-permute-start.7 = (bf16[8,272,128]{2,1,0:T(8,128)(2,1)S(1)}, bf16[8,272,128]{2,1,0:T(8,128)(2,1)S(1)}, u32[]{:S(2)}, u32[]{:S(2)}) collective-permute-start(bf16[8,272,128]{2,1,0:T(8,128)(2,1)S(1)} %shard_map.107), channel_id=1, source_target_pairs={{0,8},{8,0},{16,24},{24,16},{32,40},{40,32},{48,56},{56,48},{64,72... | collective-permute-start | bytes 1671176 | tf_op jit(solution)/shard_map/ppermute | solution.py:32
  28.7 2.2 %collective-permute-start.6 = (bf16[3,272,128]{2,1,0:T(8,128)(2,1)S(1)}, bf16[3,272,128]{2,1,0:T(8,128)(2,1)S(1)}, u32[]{:S(2)}, u32[]{:S(2)}) collective-permute-start(bf16[3,272,128]{2,1,0:T(8,128)(2,1)S(1)} %collective-permute-done.4.refs_3_._), channel_id=1, source_target_pairs={{0,8},{8,0},{16,24},{24,16},{32,40},{40,32},{48,56},{56,48},{64,72... | collective-permute-start | bytes 626696 | tf_op jit(solution)/shard_map/ppermute | solution.py:32
  29.2 7.2 %collective-permute-start.8 = (bf16[3,272,128]{2,1,0:T(8,128)(2,1)S(1)}, bf16[3,272,128]{2,1,0:T(8,128)(2,1)S(1)}, u32[]{:S(2)}, u32[]{:S(2)}) collective-permute-start(bf16[3,272,128]{2,1,0:T(8,128)(2,1)S(1)} %collective-permute-done.4.refs_3_._), channel_id=1, source_target_pairs={{0,128},{8,136},{16,144},{24,152},{32,160},{40,168},{48,176},{56,1... | collective-permute-start | bytes 626696 | tf_op jit(solution)/shard_map/ppermute | solution.py:32
  36.3 1.5 %collective-permute-start.9 = (bf16[3,272,128]{2,1,0:T(8,128)(2,1)S(1)}, bf16[3,272,128]{2,1,0:T(8,128)(2,1)S(1)}, u32[]{:S(2)}, u32[]{:S(2)}) collective-permute-start(bf16[3,272,128]{2,1,0:T(8,128)(2,1)S(1)} %collective-permute-done.8.refs_2_), channel_id=1, source_target_pairs={{0,8},{8,0},{16,24},{24,16},{32,40},{40,32},{48,56},{56,48},{64,72... | collective-permute-start | bytes 626696 | tf_op jit(solution)/shard_map/ppermute | solution.py:32
  38.8 19.1 %copy-start.3 = (bf16[256,512]{1,0:T(8,128)(2,1)S(1)}, bf16[256,512]{1,0:T(8,128)(2,1)}, u32[]{:S(2)}) copy-start(bf16[256,512]{1,0:T(8,128)(2,1)} %cot_ref.1) | copy-start | bytes 786436
  38.8 19.1 %copy-start.5 = (bf16[256,128]{1,0:T(8,128)(2,1)S(1)}, bf16[256,128]{1,0:T(8,128)(2,1)}, u32[]{:S(2)}) copy-start(bf16[256,128]{1,0:T(8,128)(2,1)} %features_ref.1) | copy-start | bytes 196612
  38.8 19.1 %copy-start.6 = (bf16[128,512]{1,0:T(8,128)(2,1)S(1)}, bf16[128,512]{1,0:T(8,128)(2,1)}, u32[]{:S(2)}) copy-start(bf16[128,512]{1,0:T(8,128)(2,1)} %weight_ref.1) | copy-start | bytes 393220
  38.8 19.1 %copy-start.10 = (s32[256]{0:T(256)S(1)}, s32[256]{0:T(256)}, u32[]{:S(2)}) copy-start(s32[256]{0:T(256)} %param.11) | copy-start | bytes 3076
  38.8 19.1 %copy-start.11 = (f32[512]{0:T(512)S(1)}, f32[512]{0:T(512)}, u32[]{:S(2)}) copy-start(f32[512]{0:T(512)} %param.10) | copy-start | bytes 6148
  76.8 2.0 %collective-permute-start.12 = (f16[800,256]{1,0:T(8,128)(2,1)S(1)}, f16[800,256]{1,0:T(8,128)(2,1)S(1)}, u32[]{:S(2)}, u32[]{:S(2)}) collective-permute-start(f16[800,256]{1,0:T(8,128)(2,1)S(1)} %pad_maximum_fusion.1), channel_id=1, source_target_pairs={{0,8},{8,0},{16,24},{24,16},{32,40},{40,32},{48,56},{56,48},{64,72... | collective-permute-start | bytes 1228808 | tf_op jit(solution)/shard_map/ppermute | solution.py:32
  79.2 7.7 %collective-permute-start.13 = (f16[416,256]{1,0:T(8,128)(2,1)S(1)}, f16[416,256]{1,0:T(8,128)(2,1)S(1)}, u32[]{:S(2)}, u32[]{:S(2)}) collective-permute-start(f16[416,256]{1,0:T(8,128)(2,1)S(1)} %pad_maximum_fusion.2), channel_id=1, source_target_pairs={{0,128},{8,136},{16,144},{24,152},{32,160},{40,168},{48,176},{56,1... | collective-permute-start | bytes 638984 | tf_op jit(solution)/shard_map/ppermute | solution.py:32
  79.6 7.4 %collective-permute-start.15 = (f16[32,256]{1,0:T(8,128)(2,1)S(1)}, f16[32,256]{1,0:T(8,128)(2,1)S(1)}, u32[]{:S(2)}, u32[]{:S(2)}) collective-permute-start(f16[32,256]{1,0:T(8,128)(2,1)S(1)} %convert_element_type.110), channel_id=1, source_target_pairs={{0,144},{8,152},{16,128},{24,136},{32,176},{40,184},{48,160},{56,1... | collective-permute-start | bytes 49160 | tf_op jit(solution)/shard_map/ppermute | solution.py:32
  81.0 6.0 %collective-permute-start.14 = (f16[32,256]{1,0:T(8,128)(2,1)S(1)}, f16[32,256]{1,0:T(8,128)(2,1)S(1)}, u32[]{:S(2)}, u32[]{:S(2)}) collective-permute-start(f16[32,256]{1,0:T(8,128)(2,1)S(1)} %convert_element_type.110), channel_id=1, source_target_pairs={{0,16},{8,24},{16,0},{24,8},{32,48},{40,56},{48,32},{56,40},{64,80... | collective-permute-start | bytes 49160 | tf_op jit(solution)/shard_map/ppermute | solution.py:32
  85.2 2.7 %collective-permute-start.10 = (f16[10,128,256]{2,1,0:T(8,128)(2,1)S(1)}, f16[10,128,256]{2,1,0:T(8,128)(2,1)S(1)}, u32[]{:S(2)}, u32[]{:S(2)}) collective-permute-start(f16[10,128,256]{2,1,0:T(8,128)(2,1)S(1)} %convert_element_type.101), channel_id=1, source_target_pairs={{0,8},{8,0},{16,24},{24,16},{32,40},{40,32},{48,56},{56,48},{64,72... | collective-permute-start | bytes 1966088 | tf_op jit(solution)/shard_map/ppermute | solution.py:32
  87.2 10.6 %collective-permute-start.16 = (f16[416,256]{1,0:T(8,128)(2,1)S(1)}, f16[416,256]{1,0:T(8,128)(2,1)S(1)}, u32[]{:S(2)}, u32[]{:S(2)}) collective-permute-start(f16[416,256]{1,0:T(8,128)(2,1)S(1)} %pad_maximum_fusion.3), channel_id=1, source_target_pairs={{0,32},{8,104},{16,48},{24,120},{32,64},{40,8},{48,80},{56,24},{64... | collective-permute-start | bytes 638984 | tf_op jit(solution)/shard_map/ppermute | solution.py:32
  88.2 9.7 %collective-permute-start.11 = (f16[5,128,256]{2,1,0:T(8,128)(2,1)S(1)}, f16[5,128,256]{2,1,0:T(8,128)(2,1)S(1)}, u32[]{:S(2)}, u32[]{:S(2)}) collective-permute-start(f16[5,128,256]{2,1,0:T(8,128)(2,1)S(1)} %slice_convert_fusion), channel_id=1, source_target_pairs={{0,128},{8,136},{16,144},{24,152},{32,160},{40,168},{48,176},{56,1... | collective-permute-start | bytes 983048 | tf_op jit(solution)/shard_map/ppermute | solution.py:32
  88.6 13.9 %collective-permute-start.20 = (f16[32,256]{1,0:T(8,128)(2,1)S(1)}, f16[32,256]{1,0:T(8,128)(2,1)S(1)}, u32[]{:S(2)}, u32[]{:S(2)}) collective-permute-start(f16[32,256]{1,0:T(8,128)(2,1)S(1)} %convert_element_type.123), channel_id=1, source_target_pairs={{0,64},{8,72},{16,80},{24,88},{32,96},{40,104},{48,112},{56,120},{... | collective-permute-start | bytes 49160 | tf_op jit(solution)/shard_map/ppermute | solution.py:32
  97.8 4.7 %collective-permute-start.21 = (f16[32,256]{1,0:T(8,128)(2,1)S(1)}, f16[32,256]{1,0:T(8,128)(2,1)S(1)}, u32[]{:S(2)}, u32[]{:S(2)}) collective-permute-start(f16[32,256]{1,0:T(8,128)(2,1)S(1)} %slice.139), channel_id=1, source_target_pairs={{0,8},{8,0},{16,24},{24,16},{32,40},{40,32},{48,56},{56,48},{64,72... | collective-permute-start | bytes 49160 | tf_op jit(solution)/shard_map/ppermute | solution.py:32
  98.1 8.5 %collective-permute-start.17 = (f16[2,128,256]{2,1,0:T(8,128)(2,1)S(1)}, f16[2,128,256]{2,1,0:T(8,128)(2,1)S(1)}, u32[]{:S(2)}, u32[]{:S(2)}) collective-permute-start(f16[2,128,256]{2,1,0:T(8,128)(2,1)S(1)} %pad_maximum_fusion.4), channel_id=1, source_target_pairs={{0,32},{8,104},{16,48},{24,120},{32,64},{40,8},{48,80},{56,24},{64... | collective-permute-start | bytes 393224 | tf_op jit(solution)/shard_map/ppermute | solution.py:32
  99.5 7.1 %collective-permute-start.18 = (f16[2,128,256]{2,1,0:T(8,128)(2,1)S(1)}, f16[2,128,256]{2,1,0:T(8,128)(2,1)S(1)}, u32[]{:S(2)}, u32[]{:S(2)}) collective-permute-start(f16[2,128,256]{2,1,0:T(8,128)(2,1)S(1)} %fusion.1), channel_id=1, source_target_pairs={{0,16},{8,120},{16,32},{24,8},{32,48},{40,24},{48,64},{56,40},{64,... | collective-permute-start | bytes 393224 | tf_op jit(solution)/shard_map/ppermute | solution.py:32
  103.2 11.4 %all-to-all-start.2 = ((f16[8,32,256]{2,1,0:T(8,128)(2,1)}), f16[8,32,256]{2,1,0:T(8,128)(2,1)S(1)}, u32[]{:S(2)}, u32[]{:S(2)}) async-start(f16[8,32,256]{2,1,0:T(8,128)(2,1)} %broadcast_in_dim.5), calls=%async_computation.2 | async-start | bytes 262144 | tf_op jit(solution)/shard_map/all_to_all | solution.py:437
  106.7 8.0 %collective-permute-start.19 = (f16[128,256]{1,0:T(8,128)(2,1)S(1)}, f16[128,256]{1,0:T(8,128)(2,1)S(1)}, u32[]{:S(2)}, u32[]{:S(2)}) collective-permute-start(f16[128,256]{1,0:T(8,128)(2,1)S(1)} %get-tuple-element.97), channel_id=1, source_target_pairs={{0,8},{8,0},{16,24},{24,16},{32,40},{40,32},{48,56},{56,48},{64,72... | collective-permute-start | bytes 196616 | tf_op jit(solution)/shard_map/ppermute | solution.py:32
  (3 other events, 2.2 us)

commit v4 on v3

--- a/solution.py
+++ b/solution.py
@@ -71,7 +71,9 @@
     return high, (value - high.astype(f32)).astype(bf16)
 
 
-def scale_kernel(features_hbm, degree_hbm, cot_hbm, own_ref, features_ref, degree_ref, cot_ref, sems):
+def scale_kernel(
+    features_hbm, degree_hbm, cot_hbm, own_ref, pair_ref, features_ref, degree_ref, cot_ref, sems
+):
     copies = [
         pltpu.make_async_copy(src, dst, sems.at[i])
         for i, (src, dst) in enumerate(
@@ -90,7 +92,8 @@
     feature = jnp.max(jnp.abs(scaled.astype(f32)))
     rows = lax.broadcasted_iota(jnp.int32, (BLOCK - OWN, TILE), 0)
     own_ref[0, OWN:, :] = jnp.where(rows < 8, cot, feature).astype(bf16)
-    own_ref[1] = own_ref[0]
+    pair_ref[0] = own_ref[0]
+    pair_ref[1] = own_ref[0]
 
 
 def column_block(at, dx, dz, dc):
@@ -269,14 +272,14 @@
     return jax.ShapeDtypeStruct(dims, dtype)
 
 
-def call(kernel, outs, ins, scratch=(), cost=0):
+def call(kernel, outs, ins, scratch=(), cost=0, limit=VMEM_LIMIT):
     return pl.pallas_call(
         kernel,
         out_shape=outs,
         in_specs=ins,
         out_specs=jax.tree.map(lambda _: VMEM, outs),
         scratch_shapes=list(scratch),
-        compiler_params=pltpu.CompilerParams(vmem_limit_bytes=VMEM_LIMIT),
+        compiler_params=pltpu.CompilerParams(vmem_limit_bytes=limit),
         cost_estimate=pl.CostEstimate(flops=cost, bytes_accessed=1 << 20, transcendentals=0),
     )
 
@@ -289,13 +292,13 @@
     return lax.optimization_barrier(values)
 
 
-def gather_blocks(own, forward):
-    pair = lax.dynamic_update_slice(own, permute_blk(own[:1], to_core), (1, 0, 0))
-    *begun, pair_x, near_1, near_2 = together(
+def gather_blocks(own, pair, forward):
+    pair = lax.dynamic_update_slice(pair, permute_blk(own, to_core), (1, 0, 0))
+    *begun, near_2, near_1, pair_x = together(
         *forward(0, pair),
+        permute_blk(pair, to_z_by_core(2)),
+        permute_blk(pair, to_z_by_core(1)),
         permute_blk(pair, to_x),
-        permute_blk(pair, to_z_by_core(1)),
-        permute_blk(pair, to_z_by_core(2)),
     )
     near = jnp.concatenate([near_1, near_2])
     *begun, far, near_x = together(
@@ -334,7 +337,8 @@
         got = got.astype(f32)
         return got[:n].reshape(terms.shape), got[n:]
 
-    give_far, keep_far = backward(GIVE_FAR, KEEP_FAR)
+    (give_far,) = backward(GIVE_FAR)
+    (keep_far,) = backward(KEEP_FAR)
     far, more = parted(permute_blk(with_grad(give_far, grad), to_core), give_far)
     give_near, keep_near = backward(GIVE_NEAR, KEEP_NEAR)
     far, grad = keep_far + far, rounded(rounded(grad) + more)
@@ -352,10 +356,11 @@
     near_x = permute_blk(near_out, to_x).astype(f32)
     out = permute_blk(out, to_z_by_core(2))
     passed, more = parted(out, far)
-    grad = grad + (more + permute_blk(out[-32:], to_core).astype(f32))
     near = near[5:] + near_x
     two = jnp.concatenate([near[:1] + passed[:1], near[1:2]]).astype(f16)
     two, one = together(two, (near[2:4] + passed[1:]).astype(f16))
+    mine = behind(more, two, one).astype(f16)
+    grad = grad + (more + permute_blk(mine, to_core).astype(f32))
     grad = after(jnp.broadcast_to(grad.astype(f16)[None], (8, 32, 256)), two, one)
     got = permute_blk(two, to_z_by_core(2)).astype(f32) + permute_blk(one, to_z_by_core(1)).astype(f32)
     return near[4] + got[0], permute_blk(got[1].astype(f16), to_core).astype(f32), grad
@@ -378,9 +383,9 @@
     degree = node_degree.reshape(OWN // TILE, TILE)
     place = lax.axis_index("blk").astype(jnp.int32).reshape(1)
 
-    own = call(
+    own, pair = call(
         scale_kernel,
-        shape((2, BLOCK, TILE), bf16),
+        (shape((1, BLOCK, TILE), bf16), shape((2, BLOCK, TILE), bf16)),
         [HBM] * 3,
         [
             pltpu.VMEM((OWN, TILE), bf16),
@@ -388,6 +393,7 @@
             pltpu.VMEM((OWN, n_out), bf16),
             pltpu.SemaphoreType.DMA((3,)),
         ],
+        limit=None,
     )(node_features, degree, cotangent)
     acc = shape(((ROW_TILES + 1) * TILE, TILE), f32)
     marks = shape((BLOCK - OWN, TILE), f32)
@@ -406,7 +412,7 @@
         forward_last_kernel,
         shape((8, BLOCK, TILE), f32),
         [pltpu.VMEM(acc.shape, f32)],
-        *gather_blocks(own, forward),
+        *gather_blocks(own, pair, forward),
     )
     parts = lax.all_to_all(partial.astype(f16), "rep", 0, 0).astype(f32)
     hidden, back, grad, factor = call(

time: 116 us -> 115 us (level)
  starting transfers between devices: 28.6 us -> 26.1 us
  Pallas kernels: 12.3 us -> 14.4 us
    ppermute x22, starting transfers between devices: 25.2 us -> 22.7 us  [permute_blk(): return lax.ppermute(value, 'blk', pairs)]
    unnamed x26 -> x22, local copies, waits for them, and re-layouts: 6.12 us -> 4.56 us
    pallas_call x1, Pallas kernels: 0.5 us -> 1.87 us  [per_device(): call(scale_kernel, (shape((1, BLOCK, TILE), bf16), shape((2, BLOCK, TILE)...]
    pallas_call x8 -> x9, Pallas kernels: 9.37 us -> 10.2 us  [products(): call(kernel, outs, ins, scratch, 1 << 29)(place, *smem, tiles, *pieces)]
  transfers between devices with their start and end apart: 23 -> 23, of which waited for: 10 -> 8; matrix products, arithmetic and copies ran while one was open for 2% -> 2% of each run, Pallas kernels for 6% -> 7%
where the time goes in v4:
time: 115 us
  blocking collectives  34.4 us (30%)
  waiting for transfers between devices  30.8 us (27%)
  starting transfers between devices  26.1 us (23%)
  Pallas kernels  14.4 us (13%)
  local copies, waits for them, and re-layouts  6.26 us (5%)
  other arithmetic  1.73 us (2%)
  between operations  1.29 us (1%)
    ppermute x22, waiting for transfers between devices, permute_blk(): return lax.ppermute(value, 'blk', pairs)  22.9 us
    ppermute x22, starting transfers between devices, permute_blk(): return lax.ppermute(value, 'blk', pairs)  22.7 us
    all_to_all x1, blocking collectives, per_device(): parts = lax.all_to_all(partial.astype(f16), 'rep', 0, 0).astype(f32)  19.3 us
    all_to_all x1, blocking collectives, per_device(): got = lax.all_to_all(sent, 'rep', 0, 0).astype(f32)  15.1 us
    pallas_call x9, Pallas kernels, products(): call(kernel, outs, ins, scratch, 1 << 29)(place, *smem, tiles, *pieces)  10.2 us
    all_to_all x1, waiting for transfers between devices, per_device(): slices = lax.all_to_all(grad, 'rep', 0, 0).astype(f32)  7.83 us
    unnamed x22, local copies, waits for them, and re-layouts  4.56 us
    all_to_all x1, starting transfers between devices, per_device(): slices = lax.all_to_all(grad, 'rep', 0, 0).astype(f32)  3.37 us
  transfers between devices with their start and end apart: 23, of which 8 were waited for; matrix products, arithmetic and copies ran while one was open for 2% of the time, Pallas kernels for 7%

profile of v4, /device:TPU:32, one launch (start us, length us, event | category | flops | bytes accessed | tf_op | source)
XLA Modules:
  0.0 114.9 jit_solution(18439471335873768175)
XLA Ops:
  0.6 1.9 %shard_map.103 = (bf16[1,272,128]{2,1,0:T(8,128)(2,1)}, bf16[2,272,128]{2,1,0:T(8,128)(2,1)}) custom-call(bf16[256,128]{1,0:T(8,128)(2,1)} %features_ref.1, s32[2,128]{1,0:T(2,128)} %bitcast.44, bf16[256,512]{1,0:T(8,128)(2,1)} %cot_ref.1), custom_call_target="tpu_custom_call" | custom-call | bytes 1048576 | tf_op jit(solution)/shard_map/pallas_call | solution.py:386
  2.6 1.5 %collective-permute-done = bf16[1,272,128]{2,1,0:T(8,128)(2,1)S(1)} collective-permute-done((bf16[1,272,128]{2,1,0:T(8,128)(2,1)}, bf16[1,272,128]{2,1,0:T(8,128)(2,1)S(1)}, u32[]{:S(2)}, u32[]{:S(2)}) %collective-permute-start) | collective-permute-done | bytes 69664 | tf_op jit(solution)/shard_map/ppermute | solution.py:32
  4.7 3.3 %collective-permute-start.1 = (bf16[2,272,128]{2,1,0:T(8,128)(2,1)}, bf16[2,272,128]{2,1,0:T(8,128)(2,1)S(1)}, u32[]{:S(2)}, u32[]{:S(2)}) collective-permute-start(bf16[2,272,128]{2,1,0:T(8,128)(2,1)} %constant_dynamic-update-slice_fusion.2.refs_0_), channel_id=1, source_target_pairs={{0,32},{8,104},{16,48},{24,120},{32,64},{40,8},{48,80},{56,24},{64... | collective-permute-start | bytes 417800 | tf_op jit(solution)/shard_map/ppermute | solution.py:32
  8.0 3.1 %collective-permute-start.2 = (bf16[2,272,128]{2,1,0:T(8,128)(2,1)}, bf16[2,272,128]{2,1,0:T(8,128)(2,1)S(1)}, u32[]{:S(2)}, u32[]{:S(2)}) collective-permute-start(bf16[2,272,128]{2,1,0:T(8,128)(2,1)} %constant_dynamic-update-slice_fusion.2.refs_0_), channel_id=1, source_target_pairs={{0,16},{8,120},{16,32},{24,8},{32,48},{40,24},{48,64},{56,40},{64,... | collective-permute-start | bytes 417800 | tf_op jit(solution)/shard_map/ppermute | solution.py:32
  11.1 1.5 %collective-permute-start.3 = (bf16[2,272,128]{2,1,0:T(8,128)(2,1)}, bf16[2,272,128]{2,1,0:T(8,128)(2,1)S(1)}, u32[]{:S(2)}, u32[]{:S(2)}) collective-permute-start(bf16[2,272,128]{2,1,0:T(8,128)(2,1)} %constant_dynamic-update-slice_fusion.2.refs_0_), channel_id=1, source_target_pairs={{0,128},{8,136},{16,144},{24,152},{32,160},{40,168},{48,176},{56,1... | collective-permute-start | bytes 417800 | tf_op jit(solution)/shard_map/ppermute | solution.py:32
  13.5 2.2 %copy-done = bf16[1,1,64,2,128,128]{5,4,3,2,1,0:T(8,128)(2,1)S(1)} copy-done((bf16[1,1,64,2,128,128]{5,4,3,2,1,0:T(8,128)(2,1)S(1)}, bf16[1,1,64,2,128,128]{5,4,3,2,1,0:T(8,128)(2,1)}, u32[]{:S(2)}) %copy-start) | copy-done | bytes 4194328
  15.7 0.9 copy-done.4
  17.3 0.8 shard_map.104
  18.8 1.6 %collective-permute-start.4 = (bf16[3,272,128]{2,1,0:T(8,128)(2,1)S(1)}, bf16[3,272,128]{2,1,0:T(8,128)(2,1)S(1)}, u32[]{:S(2)}, u32[]{:S(2)}) collective-permute-start(bf16[3,272,128]{2,1,0:T(8,128)(2,1)S(1)} %slice.115), channel_id=1, source_target_pairs={{0,32},{8,104},{16,48},{24,120},{32,64},{40,8},{48,80},{56,24},{64... | collective-permute-start | bytes 626696 | tf_op jit(solution)/shard_map/ppermute | solution.py:32
  20.3 0.9 shard_map.105
  21.3 7.7 %collective-permute-done.4.refs_3_._ = bf16[3,272,128]{2,1,0:T(8,128)(2,1)S(1)} collective-permute-done((bf16[3,272,128]{2,1,0:T(8,128)(2,1)S(1)}, bf16[3,272,128]{2,1,0:T(8,128)(2,1)S(1)}, u32[]{:S(2)}, u32[]{:S(2)}) %collective-permute-start.4) | collective-permute-done | bytes 208928 | tf_op jit(solution)/shard_map/ppermute | solution.py:32
  29.6 1.1 collective-permute-start.8
  30.6 1.0 shard_map.106
  31.6 1.1 %shard_map.108 = (f32[2176,128]{1,0:T(8,128)S(1)}, f32[16,128]{1,0:T(8,128)S(1)}) custom-call(s32[1]{0:T(128)} %bitcast.place_ref, s32[128]{0:T(128)S(1)} %reshape.59.rows_ref, s32[64]{0:T(128)S(1)} %bitcast.38, bf16[64,256,128]{2,1,0:T(8,128)(2,1)S(1)} %bitcast.29, f32[2176,128]{1,0:T(8,128)S(1)} %get-tuple-element.66.refs_0_, ...), custom_call_target="tpu_custom_call" | custom-call | flops 536870912 | bytes 1048576 | tf_op jit(solution)/shard_map/pallas_call | solution.py:405
  32.8 3.9 %collective-permute-done.8.refs_2_ = bf16[3,272,128]{2,1,0:T(8,128)(2,1)S(1)} collective-permute-done((bf16[3,272,128]{2,1,0:T(8,128)(2,1)S(1)}, bf16[3,272,128]{2,1,0:T(8,128)(2,1)S(1)}, u32[]{:S(2)}, u32[]{:S(2)}) %collective-permute-start.8) | collective-permute-done | bytes 208928 | tf_op jit(solution)/shard_map/ppermute | solution.py:32
  36.7 0.8 shard_map.109
  38.2 0.9 shard_map.110
  39.2 19.3 %all_to_all.15 = f16[8,272,128]{2,1,0:T(8,128)(2,1)S(1)} all-to-all(f16[8,272,128]{2,1,0:T(8,128)(2,1)S(1)} %convert_element_type.107), channel_id=1, replica_groups=mesh['blk'=32,'rep'=8] {'rep'}, dimensions={0} | all-to-all | bytes 1114112 | tf_op jit(solution)/shard_map/all_to_all | solution.py:417
  58.6 1.4 %shard_map.111 = (bf16[256,512]{1,0:T(8,128)(2,1)}, f32[128,256]{1,0:T(8,128)S(1)}, f32[8,32,256]{2,1,0:T(8,128)S(1)}, f32[2,8,128]{2,1,0:T(8,128)S(1)}) custom-call(f32[8,272,128]{2,1,0:T(8,128)S(1)} %convert_element_type.108.parts_ref, bf16[128,512]{1,0:T(8,128)(2,1)S(1)} %copy-done.5, f32[1,512]{1,0:T(1,128)S(1)} %bitcast.47, s32[2,128]{1,0:T(2,128)S(1)} %bitcast.45, ...), custom_call_target="tpu_custom_call" | custom-call | flops 134217728 | bytes 1048576 | tf_op jit(solution)/shard_map/pallas_call | solution.py:418
  60.3 15.1 %all_to_all.16 = f16[8,160,256]{2,1,0:T(8,128)(2,1)S(1)} all-to-all(f16[8,160,256]{2,1,0:T(8,128)(2,1)S(1)} %pad_maximum_fusion), channel_id=1, replica_groups=mesh['blk'=32,'rep'=8] {'rep'}, dimensions={0} | all-to-all | bytes 1310720 | tf_op jit(solution)/shard_map/all_to_all | solution.py:431
  75.6 1.2 %shard_map.114 = f32[6,128,256]{2,1,0:T(8,128)S(1)} custom-call(s32[1]{0:T(128)} %bitcast.place_ref, s32[128]{0:T(128)S(1)} %reshape.59.rows_ref, s32[64]{0:T(128)S(1)} %bitcast.41, bf16[64,256,128]{2,1,0:T(8,128)(2,1)S(1)} %bitcast.32, f32[8,128,256]{2,1,0:T(8,128)S(1)} %slice.116.back_ref), custom_call_target="tpu_custom_call" | custom-call | flops 536870912 | bytes 1048576 | tf_op jit(solution)/shard_map/pallas_call | solution.py:405
  77.3 1.2 %shard_map.113 = f32[6,128,256]{2,1,0:T(8,128)S(1)} custom-call(s32[1]{0:T(128)} %bitcast.place_ref, s32[128]{0:T(128)S(1)} %reshape.59.rows_ref, s32[64]{0:T(128)S(1)} %bitcast.42, bf16[64,256,128]{2,1,0:T(8,128)(2,1)S(1)} %bitcast.33, f32[8,128,256]{2,1,0:T(8,128)S(1)} %slice.116.back_ref), custom_call_target="tpu_custom_call" | custom-call | flops 536870912 | bytes 1048576 | tf_op jit(solution)/shard_map/pallas_call | solution.py:405
  80.3 2.7 %collective-permute-start.14 = (f16[32,256]{1,0:T(8,128)(2,1)S(1)}, f16[32,256]{1,0:T(8,128)(2,1)S(1)}, u32[]{:S(2)}, u32[]{:S(2)}) collective-permute-start(f16[32,256]{1,0:T(8,128)(2,1)S(1)} %convert_element_type.119), channel_id=1, source_target_pairs={{0,16},{8,24},{16,0},{24,8},{32,48},{40,56},{48,32},{56,40},{64,80... | collective-permute-start | bytes 49160 | tf_op jit(solution)/shard_map/ppermute | solution.py:32
  83.1 2.2 %shard_map.112 = (f32[10,128,256]{2,1,0:T(8,128)S(1)}, f32[10,128,256]{2,1,0:T(8,128)S(1)}) custom-call(s32[1]{0:T(128)} %bitcast.place_ref, s32[128]{0:T(128)S(1)} %reshape.59.rows_ref, s32[64]{0:T(128)S(1)} %bitcast.43, bf16[64,256,128]{2,1,0:T(8,128)(2,1)S(1)} %bitcast.34, f32[8,128,256]{2,1,0:T(8,128)S(1)} %slice.116.back_ref), custom_call_target="tpu_custom_call" | custom-call | flops 536870912 | bytes 1048576 | tf_op jit(solution)/shard_map/pallas_call | solution.py:405
  85.5 1.6 %collective-permute-done.13 = f16[416,256]{1,0:T(8,128)(2,1)S(1)} collective-permute-done((f16[416,256]{1,0:T(8,128)(2,1)S(1)}, f16[416,256]{1,0:T(8,128)(2,1)S(1)}, u32[]{:S(2)}, u32[]{:S(2)}) %collective-permute-start.13) | collective-permute-done | bytes 213024 | tf_op jit(solution)/shard_map/ppermute | solution.py:32
  88.1 0.8 collective-permute-start.11
  88.8 2.0 %collective-permute-start.20 = (f16[32,256]{1,0:T(8,128)(2,1)S(1)}, f16[32,256]{1,0:T(8,128)(2,1)S(1)}, u32[]{:S(2)}, u32[]{:S(2)}) collective-permute-start(f16[32,256]{1,0:T(8,128)(2,1)S(1)} %convert_element_type.132), channel_id=1, source_target_pairs={{0,64},{8,72},{16,80},{24,88},{32,96},{40,104},{48,112},{56,120},{... | collective-permute-start | bytes 49160 | tf_op jit(solution)/shard_map/ppermute | solution.py:32
  90.8 7.1 %collective-permute-done.16 = f16[416,256]{1,0:T(8,128)(2,1)S(1)} collective-permute-done((f16[416,256]{1,0:T(8,128)(2,1)S(1)}, f16[416,256]{1,0:T(8,128)(2,1)S(1)}, u32[]{:S(2)}, u32[]{:S(2)}) %collective-permute-start.16) | collective-permute-done | bytes 213024 | tf_op jit(solution)/shard_map/ppermute | solution.py:32
  98.5 3.3 %collective-permute-start.17 = (f16[2,128,256]{2,1,0:T(8,128)(2,1)S(1)}, f16[2,128,256]{2,1,0:T(8,128)(2,1)S(1)}, u32[]{:S(2)}, u32[]{:S(2)}) collective-permute-start(f16[2,128,256]{2,1,0:T(8,128)(2,1)S(1)} %pad_maximum_fusion.4), channel_id=1, source_target_pairs={{0,32},{8,104},{16,48},{24,120},{32,64},{40,8},{48,80},{56,24},{64... | collective-permute-start | bytes 393224 | tf_op jit(solution)/shard_map/ppermute | solution.py:32
  102.5 3.4 %all-to-all-start.2 = ((f16[8,32,256]{2,1,0:T(8,128)(2,1)}), f16[8,32,256]{2,1,0:T(8,128)(2,1)S(1)}, u32[]{:S(2)}, u32[]{:S(2)}) async-start(f16[8,32,256]{2,1,0:T(8,128)(2,1)} %broadcast_in_dim.5), calls=%async_computation.2 | async-start | bytes 262144 | tf_op jit(solution)/shard_map/all_to_all | solution.py:443
  106.1 7.8 %all-to-all-done.2 = f16[8,32,256]{2,1,0:T(8,128)(2,1)S(1)} async-done(((f16[8,32,256]{2,1,0:T(8,128)(2,1)}), f16[8,32,256]{2,1,0:T(8,128)(2,1)S(1)}, u32[]{:S(2)}, u32[]{:S(2)}) %all-to-all-start.2) | async-done | bytes 131104 | tf_op jit(solution)/shard_map/all_to_all | solution.py:443
  114.0 0.9 shard_map.118
  (105 shorter events, 9.5 us)
Async XLA Ops:
  2.5 1.6 %collective-permute-start = (bf16[1,272,128]{2,1,0:T(8,128)(2,1)}, bf16[1,272,128]{2,1,0:T(8,128)(2,1)S(1)}, u32[]{:S(2)}, u32[]{:S(2)}) collective-permute-start(bf16[1,272,128]{2,1,0:T(8,128)(2,1)} %get-tuple-element.47), channel_id=1, source_target_pairs={{0,8},{8,0},{16,24},{24,16},{32,40},{40,32},{48,56},{56,48},{64,72... | collective-permute-start | bytes 208904 | tf_op jit(solution)/shard_map/ppermute | solution.py:32
  4.7 13.3 %collective-permute-start.1 = (bf16[2,272,128]{2,1,0:T(8,128)(2,1)}, bf16[2,272,128]{2,1,0:T(8,128)(2,1)S(1)}, u32[]{:S(2)}, u32[]{:S(2)}) collective-permute-start(bf16[2,272,128]{2,1,0:T(8,128)(2,1)} %constant_dynamic-update-slice_fusion.2.refs_0_), channel_id=1, source_target_pairs={{0,32},{8,104},{16,48},{24,120},{32,64},{40,8},{48,80},{56,24},{64... | collective-permute-start | bytes 417800 | tf_op jit(solution)/shard_map/ppermute | solution.py:32
  8.0 10.1 %collective-permute-start.2 = (bf16[2,272,128]{2,1,0:T(8,128)(2,1)}, bf16[2,272,128]{2,1,0:T(8,128)(2,1)S(1)}, u32[]{:S(2)}, u32[]{:S(2)}) collective-permute-start(bf16[2,272,128]{2,1,0:T(8,128)(2,1)} %constant_dynamic-update-slice_fusion.2.refs_0_), channel_id=1, source_target_pairs={{0,16},{8,120},{16,32},{24,8},{32,48},{40,24},{48,64},{56,40},{64,... | collective-permute-start | bytes 417800 | tf_op jit(solution)/shard_map/ppermute | solution.py:32
  11.1 7.0 %collective-permute-start.3 = (bf16[2,272,128]{2,1,0:T(8,128)(2,1)}, bf16[2,272,128]{2,1,0:T(8,128)(2,1)S(1)}, u32[]{:S(2)}, u32[]{:S(2)}) collective-permute-start(bf16[2,272,128]{2,1,0:T(8,128)(2,1)} %constant_dynamic-update-slice_fusion.2.refs_0_), channel_id=1, source_target_pairs={{0,128},{8,136},{16,144},{24,152},{32,160},{40,168},{48,176},{56,1... | collective-permute-start | bytes 417800 | tf_op jit(solution)/shard_map/ppermute | solution.py:32
  13.5 2.2 %copy-start = (bf16[1,1,64,2,128,128]{5,4,3,2,1,0:T(8,128)(2,1)S(1)}, bf16[1,1,64,2,128,128]{5,4,3,2,1,0:T(8,128)(2,1)}, u32[]{:S(2)}) copy-start(bf16[1,1,64,2,128,128]{5,4,3,2,1,0:T(8,128)(2,1)} %param.12) | copy-start | bytes 12582916
  15.7 0.9 copy-start.4
  17.3 3.1 %copy-start.1 = (bf16[1,1,64,2,128,128]{5,4,3,2,1,0:T(8,128)(2,1)S(1)}, bf16[1,1,64,2,128,128]{5,4,3,2,1,0:T(8,128)(2,1)}, u32[]{:S(2)}) copy-start(bf16[1,1,64,2,128,128]{5,4,3,2,1,0:T(8,128)(2,1)} %param.12) | copy-start | bytes 12582916
  17.3 3.1 %copy-start.7 = (s32[1,1,64]{2,1,0:T(1,128)S(1)}, s32[1,1,64]{2,1,0:T(1,128)}, u32[]{:S(2)}) copy-start(s32[1,1,64]{2,1,0:T(1,128)} %param.14) | copy-start | bytes 772
  18.1 10.8 %collective-permute-start.5 = (bf16[4,272,128]{2,1,0:T(8,128)(2,1)S(1)}, bf16[4,272,128]{2,1,0:T(8,128)(2,1)S(1)}, u32[]{:S(2)}, u32[]{:S(2)}) collective-permute-start(bf16[4,272,128]{2,1,0:T(8,128)(2,1)S(1)} %constant_dynamic-update-slice_fusion.refs_3_.first_ref), channel_id=1, source_target_pairs={{0,128},{8,136},{16,144},{24,152},{32,160},{40,168},{48,176},{56,1... | collective-permute-start | bytes 835592 | tf_op jit(solution)/shard_map/ppermute | solution.py:32
  18.8 10.2 %collective-permute-start.4 = (bf16[3,272,128]{2,1,0:T(8,128)(2,1)S(1)}, bf16[3,272,128]{2,1,0:T(8,128)(2,1)S(1)}, u32[]{:S(2)}, u32[]{:S(2)}) collective-permute-start(bf16[3,272,128]{2,1,0:T(8,128)(2,1)S(1)} %slice.115), channel_id=1, source_target_pairs={{0,32},{8,104},{16,48},{24,120},{32,64},{40,8},{48,80},{56,24},{64... | collective-permute-start | bytes 626696 | tf_op jit(solution)/shard_map/ppermute | solution.py:32
  29.0 2.7 %collective-permute-start.7 = (bf16[8,272,128]{2,1,0:T(8,128)(2,1)S(1)}, bf16[8,272,128]{2,1,0:T(8,128)(2,1)S(1)}, u32[]{:S(2)}, u32[]{:S(2)}) collective-permute-start(bf16[8,272,128]{2,1,0:T(8,128)(2,1)S(1)} %shard_map.107), channel_id=1, source_target_pairs={{0,8},{8,0},{16,24},{24,16},{32,40},{40,32},{48,56},{56,48},{64,72... | collective-permute-start | bytes 1671176 | tf_op jit(solution)/shard_map/ppermute | solution.py:32
  29.1 2.6 %collective-permute-start.6 = (bf16[3,272,128]{2,1,0:T(8,128)(2,1)S(1)}, bf16[3,272,128]{2,1,0:T(8,128)(2,1)S(1)}, u32[]{:S(2)}, u32[]{:S(2)}) collective-permute-start(bf16[3,272,128]{2,1,0:T(8,128)(2,1)S(1)} %collective-permute-done.4.refs_3_._), channel_id=1, source_target_pairs={{0,8},{8,0},{16,24},{24,16},{32,40},{40,32},{48,56},{56,48},{64,72... | collective-permute-start | bytes 626696 | tf_op jit(solution)/shard_map/ppermute | solution.py:32
  29.6 7.2 %collective-permute-start.8 = (bf16[3,272,128]{2,1,0:T(8,128)(2,1)S(1)}, bf16[3,272,128]{2,1,0:T(8,128)(2,1)S(1)}, u32[]{:S(2)}, u32[]{:S(2)}) collective-permute-start(bf16[3,272,128]{2,1,0:T(8,128)(2,1)S(1)} %collective-permute-done.4.refs_3_._), channel_id=1, source_target_pairs={{0,128},{8,136},{16,144},{24,152},{32,160},{40,168},{48,176},{56,1... | collective-permute-start | bytes 626696 | tf_op jit(solution)/shard_map/ppermute | solution.py:32
  36.7 1.5 %collective-permute-start.9 = (bf16[3,272,128]{2,1,0:T(8,128)(2,1)S(1)}, bf16[3,272,128]{2,1,0:T(8,128)(2,1)S(1)}, u32[]{:S(2)}, u32[]{:S(2)}) collective-permute-start(bf16[3,272,128]{2,1,0:T(8,128)(2,1)S(1)} %collective-permute-done.8.refs_2_), channel_id=1, source_target_pairs={{0,8},{8,0},{16,24},{24,16},{32,40},{40,32},{48,56},{56,48},{64,72... | collective-permute-start | bytes 626696 | tf_op jit(solution)/shard_map/ppermute | solution.py:32
  39.2 19.4 %copy-start.2 = (bf16[256,512]{1,0:T(8,128)(2,1)S(1)}, bf16[256,512]{1,0:T(8,128)(2,1)}, u32[]{:S(2)}) copy-start(bf16[256,512]{1,0:T(8,128)(2,1)} %cot_ref.1) | copy-start | bytes 786436
  39.2 19.4 %copy-start.3 = (bf16[256,128]{1,0:T(8,128)(2,1)S(1)}, bf16[256,128]{1,0:T(8,128)(2,1)}, u32[]{:S(2)}) copy-start(bf16[256,128]{1,0:T(8,128)(2,1)} %features_ref.1) | copy-start | bytes 196612
  39.2 19.4 %copy-start.5 = (bf16[128,512]{1,0:T(8,128)(2,1)S(1)}, bf16[128,512]{1,0:T(8,128)(2,1)}, u32[]{:S(2)}) copy-start(bf16[128,512]{1,0:T(8,128)(2,1)} %weight_ref.1) | copy-start | bytes 393220
  39.2 19.4 %copy-start.8 = (s32[256]{0:T(256)S(1)}, s32[256]{0:T(256)}, u32[]{:S(2)}) copy-start(s32[256]{0:T(256)} %param.11) | copy-start | bytes 3076
  39.2 19.4 %copy-start.9 = (f32[512]{0:T(512)S(1)}, f32[512]{0:T(512)}, u32[]{:S(2)}) copy-start(f32[512]{0:T(512)} %param.10) | copy-start | bytes 6148
  77.0 2.0 %collective-permute-start.12 = (f16[800,256]{1,0:T(8,128)(2,1)S(1)}, f16[800,256]{1,0:T(8,128)(2,1)S(1)}, u32[]{:S(2)}, u32[]{:S(2)}) collective-permute-start(f16[800,256]{1,0:T(8,128)(2,1)S(1)} %pad_maximum_fusion.1), channel_id=1, source_target_pairs={{0,8},{8,0},{16,24},{24,16},{32,40},{40,32},{48,56},{56,48},{64,72... | collective-permute-start | bytes 1228808 | tf_op jit(solution)/shard_map/ppermute | solution.py:32
  79.4 7.7 %collective-permute-start.13 = (f16[416,256]{1,0:T(8,128)(2,1)S(1)}, f16[416,256]{1,0:T(8,128)(2,1)S(1)}, u32[]{:S(2)}, u32[]{:S(2)}) collective-permute-start(f16[416,256]{1,0:T(8,128)(2,1)S(1)} %pad_maximum_fusion.2), channel_id=1, source_target_pairs={{0,128},{8,136},{16,144},{24,152},{32,160},{40,168},{48,176},{56,1... | collective-permute-start | bytes 638984 | tf_op jit(solution)/shard_map/ppermute | solution.py:32
  80.0 7.1 %collective-permute-start.15 = (f16[32,256]{1,0:T(8,128)(2,1)S(1)}, f16[32,256]{1,0:T(8,128)(2,1)S(1)}, u32[]{:S(2)}, u32[]{:S(2)}) collective-permute-start(f16[32,256]{1,0:T(8,128)(2,1)S(1)} %convert_element_type.119), channel_id=1, source_target_pairs={{0,144},{8,152},{16,128},{24,136},{32,176},{40,184},{48,160},{56,1... | collective-permute-start | bytes 49160 | tf_op jit(solution)/shard_map/ppermute | solution.py:32
  80.3 6.8 %collective-permute-start.14 = (f16[32,256]{1,0:T(8,128)(2,1)S(1)}, f16[32,256]{1,0:T(8,128)(2,1)S(1)}, u32[]{:S(2)}, u32[]{:S(2)}) collective-permute-start(f16[32,256]{1,0:T(8,128)(2,1)S(1)} %convert_element_type.119), channel_id=1, source_target_pairs={{0,16},{8,24},{16,0},{24,8},{32,48},{40,56},{48,32},{56,40},{64,80... | collective-permute-start | bytes 49160 | tf_op jit(solution)/shard_map/ppermute | solution.py:32
  85.4 2.4 %collective-permute-start.10 = (f16[10,128,256]{2,1,0:T(8,128)(2,1)S(1)}, f16[10,128,256]{2,1,0:T(8,128)(2,1)S(1)}, u32[]{:S(2)}, u32[]{:S(2)}) collective-permute-start(f16[10,128,256]{2,1,0:T(8,128)(2,1)S(1)} %convert_element_type.110), channel_id=1, source_target_pairs={{0,8},{8,0},{16,24},{24,16},{32,40},{40,32},{48,56},{56,48},{64,72... | collective-permute-start | bytes 1966088 | tf_op jit(solution)/shard_map/ppermute | solution.py:32
  87.4 10.5 %collective-permute-start.16 = (f16[416,256]{1,0:T(8,128)(2,1)S(1)}, f16[416,256]{1,0:T(8,128)(2,1)S(1)}, u32[]{:S(2)}, u32[]{:S(2)}) collective-permute-start(f16[416,256]{1,0:T(8,128)(2,1)S(1)} %pad_maximum_fusion.3), channel_id=1, source_target_pairs={{0,32},{8,104},{16,48},{24,120},{32,64},{40,8},{48,80},{56,24},{64... | collective-permute-start | bytes 638984 | tf_op jit(solution)/shard_map/ppermute | solution.py:32
  88.1 9.9 %collective-permute-start.11 = (f16[5,128,256]{2,1,0:T(8,128)(2,1)S(1)}, f16[5,128,256]{2,1,0:T(8,128)(2,1)S(1)}, u32[]{:S(2)}, u32[]{:S(2)}) collective-permute-start(f16[5,128,256]{2,1,0:T(8,128)(2,1)S(1)} %slice_convert_fusion), channel_id=1, source_target_pairs={{0,128},{8,136},{16,144},{24,152},{32,160},{40,168},{48,176},{56,1... | collective-permute-start | bytes 983048 | tf_op jit(solution)/shard_map/ppermute | solution.py:32
  88.8 13.0 %collective-permute-start.20 = (f16[32,256]{1,0:T(8,128)(2,1)S(1)}, f16[32,256]{1,0:T(8,128)(2,1)S(1)}, u32[]{:S(2)}, u32[]{:S(2)}) collective-permute-start(f16[32,256]{1,0:T(8,128)(2,1)S(1)} %convert_element_type.132), channel_id=1, source_target_pairs={{0,64},{8,72},{16,80},{24,88},{32,96},{40,104},{48,112},{56,120},{... | collective-permute-start | bytes 49160 | tf_op jit(solution)/shard_map/ppermute | solution.py:32
  98.3 3.6 %collective-permute-start.21 = (f16[32,256]{1,0:T(8,128)(2,1)S(1)}, f16[32,256]{1,0:T(8,128)(2,1)S(1)}, u32[]{:S(2)}, u32[]{:S(2)}) collective-permute-start(f16[32,256]{1,0:T(8,128)(2,1)S(1)} %convert_element_type.136), channel_id=1, source_target_pairs={{0,8},{8,0},{16,24},{24,16},{32,40},{40,32},{48,56},{56,48},{64,72... | collective-permute-start | bytes 49160 | tf_op jit(solution)/shard_map/ppermute | solution.py:32
  98.4 7.6 %collective-permute-start.18 = (f16[2,128,256]{2,1,0:T(8,128)(2,1)S(1)}, f16[2,128,256]{2,1,0:T(8,128)(2,1)S(1)}, u32[]{:S(2)}, u32[]{:S(2)}) collective-permute-start(f16[2,128,256]{2,1,0:T(8,128)(2,1)S(1)} %fusion.1), channel_id=1, source_target_pairs={{0,16},{8,120},{16,32},{24,8},{32,48},{40,24},{48,64},{56,40},{64,... | collective-permute-start | bytes 393224 | tf_op jit(solution)/shard_map/ppermute | solution.py:32
  98.5 7.4 %collective-permute-start.17 = (f16[2,128,256]{2,1,0:T(8,128)(2,1)S(1)}, f16[2,128,256]{2,1,0:T(8,128)(2,1)S(1)}, u32[]{:S(2)}, u32[]{:S(2)}) collective-permute-start(f16[2,128,256]{2,1,0:T(8,128)(2,1)S(1)} %pad_maximum_fusion.4), channel_id=1, source_target_pairs={{0,32},{8,104},{16,48},{24,120},{32,64},{40,8},{48,80},{56,24},{64... | collective-permute-start | bytes 393224 | tf_op jit(solution)/shard_map/ppermute | solution.py:32
  102.5 11.4 %all-to-all-start.2 = ((f16[8,32,256]{2,1,0:T(8,128)(2,1)}), f16[8,32,256]{2,1,0:T(8,128)(2,1)S(1)}, u32[]{:S(2)}, u32[]{:S(2)}) async-start(f16[8,32,256]{2,1,0:T(8,128)(2,1)} %broadcast_in_dim.5), calls=%async_computation.2 | async-start | bytes 262144 | tf_op jit(solution)/shard_map/all_to_all | solution.py:443
  106.0 8.0 %collective-permute-start.19 = (f16[128,256]{1,0:T(8,128)(2,1)S(1)}, f16[128,256]{1,0:T(8,128)(2,1)S(1)}, u32[]{:S(2)}, u32[]{:S(2)}) collective-permute-start(f16[128,256]{1,0:T(8,128)(2,1)S(1)} %get-tuple-element.97), channel_id=1, source_target_pairs={{0,8},{8,0},{16,24},{24,16},{32,40},{40,32},{48,56},{56,48},{64,72... | collective-permute-start | bytes 196616 | tf_op jit(solution)/shard_map/ppermute | solution.py:32
  (1 other events, 0.7 us)

commit v5 on v4

--- a/solution.py
+++ b/solution.py
@@ -206,9 +206,10 @@
     local = lax.dot_general(features, high, down, preferred_element_type=f32)
     local += lax.dot_general(features, low, down, preferred_element_type=f32)
     local = local * (0.25 * jnp.exp2(-feature_mark[:, :1]))
-    for r in range(grad_ref.shape[0]):
-        i, j = r // 2, r % 2
-        grad_ref[r] = local[i * 32 : (i + 1) * 32, j * 256 : (j + 1) * 256]
+    for i in range(N_Y):
+        for j in range(2):
+            part = local[i * 32 : (i + 1) * 32, j * 256 : (j + 1) * 256]
+            grad_ref[i, j * 32 : (j + 1) * 32, :] = part
     one = jnp.ones((8, TILE), f32)
     factor_ref[0] = one * (16.0 * jnp.exp2(cot_mark + weight_mark))
     factor_ref[1] = one * (jnp.exp2(cot_mark + feature_mark) / 64.0)
@@ -249,9 +250,10 @@
 
 def finish_kernel(mine_ref, theirs_ref, degree_ref, factor_ref, slices_ref, input_ref, weight_ref):
     factor = jnp.concatenate([factor_ref[1, :1, :]] * 2, 1)
-    for r in range(slices_ref.shape[0]):
-        i, j = r // 2, r % 2
-        weight_ref[i * 32 : (i + 1) * 32, j * 256 : (j + 1) * 256] = slices_ref[r] * factor
+    for i in range(N_Y):
+        for j in range(2):
+            part = slices_ref[i, j * 32 : (j + 1) * 32, :] * factor
+            weight_ref[i * 32 : (i + 1) * 32, j * 256 : (j + 1) * 256] = part
     _, column_scale = scale_of(degree_ref[...])
     total = (mine_ref[...] + theirs_ref[...]).T
     input_ref[...] = (column_scale * total * factor_ref[0, :1, :]).astype(bf16)
@@ -361,7 +363,7 @@
     two, one = together(two, (near[2:4] + passed[1:]).astype(f16))
     mine = behind(more, two, one).astype(f16)
     grad = grad + (more + permute_blk(mine, to_core).astype(f32))
-    grad = after(jnp.broadcast_to(grad.astype(f16)[None], (8, 32, 256)), two, one)
+    grad = after(jnp.broadcast_to(grad.astype(f16)[None], (N_Y, 64, 256)), two, one)
     got = permute_blk(two, to_z_by_core(2)).astype(f32) + permute_blk(one, to_z_by_core(1)).astype(f32)
     return near[4] + got[0], permute_blk(got[1].astype(f16), to_core).astype(f32), grad
 
@@ -420,14 +422,14 @@
         (
             shape((OWN, n_out), bf16),
             shape((TILE, OWN), f32),
-            shape((8, 32, 256), f32),
+            shape((N_Y, 64, 256), f32),
             shape((2, 8, TILE), f32),
         ),
         [VMEM] * 6,
         cost=1 << 27,
     )(parts, weight_matrix, bias_vector.reshape(1, -1), degree, node_features, cotangent)
 
-    sent = jnp.concatenate([jnp.broadcast_to(back[None], (8, TILE, OWN)), grad], 1).astype(f16)
+    sent = jnp.concatenate([jnp.broadcast_to(back[None], (8, TILE, OWN)), jnp.concatenate([grad, grad])], 1).astype(f16)
     got = lax.all_to_all(sent, "rep", 0, 0).astype(f32)
     got_back = got[:, :TILE]
 
@@ -440,7 +442,8 @@
         )
 
     *halves, grad = scatter_terms(backward, jnp.sum(got[:, TILE:], 0))
-    slices = lax.all_to_all(grad, "rep", 0, 0).astype(f32)
+    along_y = [list(range(N_Y)), list(range(N_Y, 2 * N_Y))]
+    slices = lax.all_to_all(grad, "rep", 0, 0, axis_index_groups=along_y).astype(f32)
     input_grad, weight_grad = call(
         finish_kernel, (shape((OWN, TILE), bf16), shape((TILE, n_out), f32)), [VMEM] * 5
     )(*halves, degree, factor, slices)

time: 115 us -> 116 us (level)
  blocking collectives: 34.4 us -> 35.7 us
    all_to_all x1, waiting for transfers between devices: 7.83 us -> 5.75 us  [per_device(): lax.all_to_all(grad, 'rep', 0, 0, axis_index_groups=along_y).astype(f32)]
    ppermute x22, waiting for transfers between devices: 22.9 us -> 24.9 us  [permute_blk(): return lax.ppermute(value, 'blk', pairs)]
    all_to_all x1, blocking collectives: 15.1 us -> 16.4 us  [per_device(): got = lax.all_to_all(sent, 'rep', 0, 0).astype(f32)]
where the time goes in v5:
time: 116 us
  blocking collectives  35.7 us (31%)
  waiting for transfers between devices  30.6 us (26%)
  starting transfers between devices  25.7 us (22%)
  Pallas kernels  14.4 us (12%)
  local copies, waits for them, and re-layouts  6.26 us (5%)
  other arithmetic  1.86 us (2%)
  between operations  1.29 us (1%)
    ppermute x22, waiting for transfers between devices, permute_blk(): return lax.ppermute(value, 'blk', pairs)  24.9 us
    ppermute x22, starting transfers between devices, permute_blk(): return lax.ppermute(value, 'blk', pairs)  22.4 us
    all_to_all x1, blocking collectives, per_device(): parts = lax.all_to_all(partial.astype(f16), 'rep', 0, 0).astype(f32)  19.3 us
    all_to_all x1, blocking collectives, per_device(): got = lax.all_to_all(sent, 'rep', 0, 0).astype(f32)  16.4 us
    pallas_call x9, Pallas kernels, products(): call(kernel, outs, ins, scratch, 1 << 29)(place, *smem, tiles, *pieces)  10.2 us
    all_to_all x1, waiting for transfers between devices, per_device(): lax.all_to_all(grad, 'rep', 0, 0, axis_index_groups=along_y).astype(f32)  5.75 us
    unnamed x22, local copies, waits for them, and re-layouts  4.56 us
    all_to_all x1, starting transfers between devices, per_device(): lax.all_to_all(grad, 'rep', 0, 0, axis_index_groups=along_y).astype(f32)  3.33 us
  transfers between devices with their start and end apart: 23, of which 8 were waited for; matrix products, arithmetic and copies ran while one was open for 2% of the time, Pallas kernels for 7%

profile of v5, /device:TPU:32, one launch (start us, length us, event | category | flops | bytes accessed | tf_op | source)
XLA Modules:
  0.0 115.9 jit_solution(13207858569050021180)
XLA Ops:
  0.6 1.9 %shard_map.103 = (bf16[1,272,128]{2,1,0:T(8,128)(2,1)}, bf16[2,272,128]{2,1,0:T(8,128)(2,1)}) custom-call(bf16[256,128]{1,0:T(8,128)(2,1)} %features_ref.1, s32[2,128]{1,0:T(2,128)} %bitcast.44, bf16[256,512]{1,0:T(8,128)(2,1)} %cot_ref.1), custom_call_target="tpu_custom_call" | custom-call | bytes 1048576 | tf_op jit(solution)/shard_map/pallas_call | solution.py:388
  2.6 1.5 %collective-permute-done = bf16[1,272,128]{2,1,0:T(8,128)(2,1)S(1)} collective-permute-done((bf16[1,272,128]{2,1,0:T(8,128)(2,1)}, bf16[1,272,128]{2,1,0:T(8,128)(2,1)S(1)}, u32[]{:S(2)}, u32[]{:S(2)}) %collective-permute-start) | collective-permute-done | bytes 69664 | tf_op jit(solution)/shard_map/ppermute | solution.py:32
  4.7 3.3 %collective-permute-start.1 = (bf16[2,272,128]{2,1,0:T(8,128)(2,1)}, bf16[2,272,128]{2,1,0:T(8,128)(2,1)S(1)}, u32[]{:S(2)}, u32[]{:S(2)}) collective-permute-start(bf16[2,272,128]{2,1,0:T(8,128)(2,1)} %constant_dynamic-update-slice_fusion.2.refs_0_), channel_id=1, source_target_pairs={{0,32},{8,104},{16,48},{24,120},{32,64},{40,8},{48,80},{56,24},{64... | collective-permute-start | bytes 417800 | tf_op jit(solution)/shard_map/ppermute | solution.py:32
  8.0 3.1 %collective-permute-start.2 = (bf16[2,272,128]{2,1,0:T(8,128)(2,1)}, bf16[2,272,128]{2,1,0:T(8,128)(2,1)S(1)}, u32[]{:S(2)}, u32[]{:S(2)}) collective-permute-start(bf16[2,272,128]{2,1,0:T(8,128)(2,1)} %constant_dynamic-update-slice_fusion.2.refs_0_), channel_id=1, source_target_pairs={{0,16},{8,120},{16,32},{24,8},{32,48},{40,24},{48,64},{56,40},{64,... | collective-permute-start | bytes 417800 | tf_op jit(solution)/shard_map/ppermute | solution.py:32
  11.1 1.5 %collective-permute-start.3 = (bf16[2,272,128]{2,1,0:T(8,128)(2,1)}, bf16[2,272,128]{2,1,0:T(8,128)(2,1)S(1)}, u32[]{:S(2)}, u32[]{:S(2)}) collective-permute-start(bf16[2,272,128]{2,1,0:T(8,128)(2,1)} %constant_dynamic-update-slice_fusion.2.refs_0_), channel_id=1, source_target_pairs={{0,128},{8,136},{16,144},{24,152},{32,160},{40,168},{48,176},{56,1... | collective-permute-start | bytes 417800 | tf_op jit(solution)/shard_map/ppermute | solution.py:32
  12.6 0.8 copy.12
  13.5 2.2 %copy-done = bf16[1,1,64,2,128,128]{5,4,3,2,1,0:T(8,128)(2,1)S(1)} copy-done((bf16[1,1,64,2,128,128]{5,4,3,2,1,0:T(8,128)(2,1)S(1)}, bf16[1,1,64,2,128,128]{5,4,3,2,1,0:T(8,128)(2,1)}, u32[]{:S(2)}) %copy-start) | copy-done | bytes 4194328
  15.7 0.9 copy-done.4
  17.3 0.8 shard_map.104
  18.8 1.6 %collective-permute-start.4 = (bf16[3,272,128]{2,1,0:T(8,128)(2,1)S(1)}, bf16[3,272,128]{2,1,0:T(8,128)(2,1)S(1)}, u32[]{:S(2)}, u32[]{:S(2)}) collective-permute-start(bf16[3,272,128]{2,1,0:T(8,128)(2,1)S(1)} %slice.115), channel_id=1, source_target_pairs={{0,32},{8,104},{16,48},{24,120},{32,64},{40,8},{48,80},{56,24},{64... | collective-permute-start | bytes 626696 | tf_op jit(solution)/shard_map/ppermute | solution.py:32
  20.3 0.9 shard_map.105
  21.3 7.7 %collective-permute-done.4.refs_3_._ = bf16[3,272,128]{2,1,0:T(8,128)(2,1)S(1)} collective-permute-done((bf16[3,272,128]{2,1,0:T(8,128)(2,1)S(1)}, bf16[3,272,128]{2,1,0:T(8,128)(2,1)S(1)}, u32[]{:S(2)}, u32[]{:S(2)}) %collective-permute-start.4) | collective-permute-done | bytes 208928 | tf_op jit(solution)/shard_map/ppermute | solution.py:32
  29.6 1.1 collective-permute-start.8
  30.6 1.0 shard_map.106
  31.6 1.1 shard_map.108
  32.8 4.0 %collective-permute-done.8.refs_2_ = bf16[3,272,128]{2,1,0:T(8,128)(2,1)S(1)} collective-permute-done((bf16[3,272,128]{2,1,0:T(8,128)(2,1)S(1)}, bf16[3,272,128]{2,1,0:T(8,128)(2,1)S(1)}, u32[]{:S(2)}, u32[]{:S(2)}) %collective-permute-start.8) | collective-permute-done | bytes 208928 | tf_op jit(solution)/shard_map/ppermute | solution.py:32
  36.7 0.8 shard_map.109
  38.2 0.9 shard_map.110
  39.2 19.3 %all_to_all.15 = f16[8,272,128]{2,1,0:T(8,128)(2,1)S(1)} all-to-all(f16[8,272,128]{2,1,0:T(8,128)(2,1)S(1)} %convert_element_type.107), channel_id=1, replica_groups=mesh['blk'=32,'rep'=8] {'rep'}, dimensions={0} | all-to-all | bytes 1114112 | tf_op jit(solution)/shard_map/all_to_all | solution.py:419
  58.6 1.4 %shard_map.111 = (bf16[256,512]{1,0:T(8,128)(2,1)}, f32[128,256]{1,0:T(8,128)S(1)}, f32[4,64,256]{2,1,0:T(8,128)S(1)}, f32[2,8,128]{2,1,0:T(8,128)S(1)}) custom-call(f32[8,272,128]{2,1,0:T(8,128)S(1)} %convert_element_type.108.parts_ref, bf16[128,512]{1,0:T(8,128)(2,1)S(1)} %copy-done.5, f32[1,512]{1,0:T(1,128)S(1)} %bitcast.47, s32[2,128]{1,0:T(2,128)S(1)} %bitcast.45, ...), custom_call_target="tpu_custom_call" | custom-call | flops 134217728 | bytes 1048576 | tf_op jit(solution)/shard_map/pallas_call | solution.py:420
  60.4 16.4 %all_to_all.16 = f16[8,192,256]{2,1,0:T(8,128)(2,1)S(1)} all-to-all(f16[8,192,256]{2,1,0:T(8,128)(2,1)S(1)} %maximum_maximum_fusion), channel_id=1, replica_groups=mesh['blk'=32,'rep'=8] {'rep'}, dimensions={0} | all-to-all | bytes 1572864 | tf_op jit(solution)/shard_map/all_to_all | solution.py:433
  77.1 1.2 %shard_map.114 = f32[6,128,256]{2,1,0:T(8,128)S(1)} custom-call(s32[1]{0:T(128)} %bitcast.place_ref, s32[128]{0:T(128)S(1)} %reshape.59.rows_ref, s32[64]{0:T(128)S(1)} %bitcast.41, bf16[64,256,128]{2,1,0:T(8,128)(2,1)S(1)} %bitcast.32, f32[8,128,256]{2,1,0:T(8,128)S(1)} %slice.116.back_ref), custom_call_target="tpu_custom_call" | custom-call | flops 536870912 | bytes 1048576 | tf_op jit(solution)/shard_map/pallas_call | solution.py:407
  78.8 1.2 %shard_map.113 = f32[6,128,256]{2,1,0:T(8,128)S(1)} custom-call(s32[1]{0:T(128)} %bitcast.place_ref, s32[128]{0:T(128)S(1)} %reshape.59.rows_ref, s32[64]{0:T(128)S(1)} %bitcast.42, bf16[64,256,128]{2,1,0:T(8,128)(2,1)S(1)} %bitcast.33, f32[8,128,256]{2,1,0:T(8,128)S(1)} %slice.116.back_ref), custom_call_target="tpu_custom_call" | custom-call | flops 536870912 | bytes 1048576 | tf_op jit(solution)/shard_map/pallas_call | solution.py:407
  81.8 2.7 %collective-permute-start.14 = (f16[64,256]{1,0:T(8,128)(2,1)S(1)}, f16[64,256]{1,0:T(8,128)(2,1)S(1)}, u32[]{:S(2)}, u32[]{:S(2)}) collective-permute-start(f16[64,256]{1,0:T(8,128)(2,1)S(1)} %convert_element_type.119), channel_id=1, source_target_pairs={{0,16},{8,24},{16,0},{24,8},{32,48},{40,56},{48,32},{56,40},{64,80... | collective-permute-start | bytes 98312 | tf_op jit(solution)/shard_map/ppermute | solution.py:32
  84.6 2.2 %shard_map.112 = (f32[10,128,256]{2,1,0:T(8,128)S(1)}, f32[10,128,256]{2,1,0:T(8,128)S(1)}) custom-call(s32[1]{0:T(128)} %bitcast.place_ref, s32[128]{0:T(128)S(1)} %reshape.59.rows_ref, s32[64]{0:T(128)S(1)} %bitcast.43, bf16[64,256,128]{2,1,0:T(8,128)(2,1)S(1)} %bitcast.34, f32[8,128,256]{2,1,0:T(8,128)S(1)} %slice.116.back_ref), custom_call_target="tpu_custom_call" | custom-call | flops 536870912 | bytes 1048576 | tf_op jit(solution)/shard_map/pallas_call | solution.py:407
  87.0 2.3 %collective-permute-done.13 = f16[448,256]{1,0:T(8,128)(2,1)S(1)} collective-permute-done((f16[448,256]{1,0:T(8,128)(2,1)S(1)}, f16[448,256]{1,0:T(8,128)(2,1)S(1)}, u32[]{:S(2)}, u32[]{:S(2)}) %collective-permute-start.13) | collective-permute-done | bytes 229408 | tf_op jit(solution)/shard_map/ppermute | solution.py:32
  91.0 1.9 %collective-permute-start.20 = (f16[64,256]{1,0:T(8,128)(2,1)S(1)}, f16[64,256]{1,0:T(8,128)(2,1)S(1)}, u32[]{:S(2)}, u32[]{:S(2)}) collective-permute-start(f16[64,256]{1,0:T(8,128)(2,1)S(1)} %convert_element_type.132), channel_id=1, source_target_pairs={{0,64},{8,72},{16,80},{24,88},{32,96},{40,104},{48,112},{56,120},{... | collective-permute-start | bytes 98312 | tf_op jit(solution)/shard_map/ppermute | solution.py:32
  92.9 8.3 %collective-permute-done.16 = f16[448,256]{1,0:T(8,128)(2,1)S(1)} collective-permute-done((f16[448,256]{1,0:T(8,128)(2,1)S(1)}, f16[448,256]{1,0:T(8,128)(2,1)S(1)}, u32[]{:S(2)}, u32[]{:S(2)}) %collective-permute-start.16) | collective-permute-done | bytes 229408 | tf_op jit(solution)/shard_map/ppermute | solution.py:32
  101.7 3.2 %collective-permute-start.17 = (f16[2,128,256]{2,1,0:T(8,128)(2,1)S(1)}, f16[2,128,256]{2,1,0:T(8,128)(2,1)S(1)}, u32[]{:S(2)}, u32[]{:S(2)}) collective-permute-start(f16[2,128,256]{2,1,0:T(8,128)(2,1)S(1)} %pad_maximum_fusion.3), channel_id=1, source_target_pairs={{0,32},{8,104},{16,48},{24,120},{32,64},{40,8},{48,80},{56,24},{64... | collective-permute-start | bytes 393224 | tf_op jit(solution)/shard_map/ppermute | solution.py:32
  105.6 3.3 %all-to-all-start.2 = ((f16[4,64,256]{2,1,0:T(8,128)(2,1)}), f16[4,64,256]{2,1,0:T(8,128)(2,1)S(1)}, u32[]{:S(2)}, u32[]{:S(2)}) async-start(f16[4,64,256]{2,1,0:T(8,128)(2,1)} %broadcast_in_dim.5), calls=%async_computation.2 | async-start | bytes 262144 | tf_op jit(solution)/shard_map/all_to_all | solution.py:446
  109.2 5.7 %all-to-all-done.2 = f16[4,64,256]{2,1,0:T(8,128)(2,1)S(1)} async-done(((f16[4,64,256]{2,1,0:T(8,128)(2,1)}), f16[4,64,256]{2,1,0:T(8,128)(2,1)S(1)}, u32[]{:S(2)}, u32[]{:S(2)}) %all-to-all-start.2) | async-done | bytes 131104 | tf_op jit(solution)/shard_map/all_to_all | solution.py:446
  115.0 0.9 shard_map.118
  (105 shorter events, 9.5 us)
Async XLA Ops:
  2.5 1.6 %collective-permute-start = (bf16[1,272,128]{2,1,0:T(8,128)(2,1)}, bf16[1,272,128]{2,1,0:T(8,128)(2,1)S(1)}, u32[]{:S(2)}, u32[]{:S(2)}) collective-permute-start(bf16[1,272,128]{2,1,0:T(8,128)(2,1)} %get-tuple-element.47), channel_id=1, source_target_pairs={{0,8},{8,0},{16,24},{24,16},{32,40},{40,32},{48,56},{56,48},{64,72... | collective-permute-start | bytes 208904 | tf_op jit(solution)/shard_map/ppermute | solution.py:32
  4.7 13.3 %collective-permute-start.1 = (bf16[2,272,128]{2,1,0:T(8,128)(2,1)}, bf16[2,272,128]{2,1,0:T(8,128)(2,1)S(1)}, u32[]{:S(2)}, u32[]{:S(2)}) collective-permute-start(bf16[2,272,128]{2,1,0:T(8,128)(2,1)} %constant_dynamic-update-slice_fusion.2.refs_0_), channel_id=1, source_target_pairs={{0,32},{8,104},{16,48},{24,120},{32,64},{40,8},{48,80},{56,24},{64... | collective-permute-start | bytes 417800 | tf_op jit(solution)/shard_map/ppermute | solution.py:32
  8.0 10.1 %collective-permute-start.2 = (bf16[2,272,128]{2,1,0:T(8,128)(2,1)}, bf16[2,272,128]{2,1,0:T(8,128)(2,1)S(1)}, u32[]{:S(2)}, u32[]{:S(2)}) collective-permute-start(bf16[2,272,128]{2,1,0:T(8,128)(2,1)} %constant_dynamic-update-slice_fusion.2.refs_0_), channel_id=1, source_target_pairs={{0,16},{8,120},{16,32},{24,8},{32,48},{40,24},{48,64},{56,40},{64,... | collective-permute-start | bytes 417800 | tf_op jit(solution)/shard_map/ppermute | solution.py:32
  11.1 7.0 %collective-permute-start.3 = (bf16[2,272,128]{2,1,0:T(8,128)(2,1)}, bf16[2,272,128]{2,1,0:T(8,128)(2,1)S(1)}, u32[]{:S(2)}, u32[]{:S(2)}) collective-permute-start(bf16[2,272,128]{2,1,0:T(8,128)(2,1)} %constant_dynamic-update-slice_fusion.2.refs_0_), channel_id=1, source_target_pairs={{0,128},{8,136},{16,144},{24,152},{32,160},{40,168},{48,176},{56,1... | collective-permute-start | bytes 417800 | tf_op jit(solution)/shard_map/ppermute | solution.py:32
  13.5 2.2 %copy-start = (bf16[1,1,64,2,128,128]{5,4,3,2,1,0:T(8,128)(2,1)S(1)}, bf16[1,1,64,2,128,128]{5,4,3,2,1,0:T(8,128)(2,1)}, u32[]{:S(2)}) copy-start(bf16[1,1,64,2,128,128]{5,4,3,2,1,0:T(8,128)(2,1)} %param.12) | copy-start | bytes 12582916
  15.7 0.9 copy-start.4
  17.3 3.1 %copy-start.1 = (bf16[1,1,64,2,128,128]{5,4,3,2,1,0:T(8,128)(2,1)S(1)}, bf16[1,1,64,2,128,128]{5,4,3,2,1,0:T(8,128)(2,1)}, u32[]{:S(2)}) copy-start(bf16[1,1,64,2,128,128]{5,4,3,2,1,0:T(8,128)(2,1)} %param.12) | copy-start | bytes 12582916
  17.3 3.1 %copy-start.7 = (s32[1,1,64]{2,1,0:T(1,128)S(1)}, s32[1,1,64]{2,1,0:T(1,128)}, u32[]{:S(2)}) copy-start(s32[1,1,64]{2,1,0:T(1,128)} %param.14) | copy-start | bytes 772
  18.1 10.8 %collective-permute-start.5 = (bf16[4,272,128]{2,1,0:T(8,128)(2,1)S(1)}, bf16[4,272,128]{2,1,0:T(8,128)(2,1)S(1)}, u32[]{:S(2)}, u32[]{:S(2)}) collective-permute-start(bf16[4,272,128]{2,1,0:T(8,128)(2,1)S(1)} %constant_dynamic-update-slice_fusion.refs_3_.first_ref), channel_id=1, source_target_pairs={{0,128},{8,136},{16,144},{24,152},{32,160},{40,168},{48,176},{56,1... | collective-permute-start | bytes 835592 | tf_op jit(solution)/shard_map/ppermute | solution.py:32
  18.8 10.2 %collective-permute-start.4 = (bf16[3,272,128]{2,1,0:T(8,128)(2,1)S(1)}, bf16[3,272,128]{2,1,0:T(8,128)(2,1)S(1)}, u32[]{:S(2)}, u32[]{:S(2)}) collective-permute-start(bf16[3,272,128]{2,1,0:T(8,128)(2,1)S(1)} %slice.115), channel_id=1, source_target_pairs={{0,32},{8,104},{16,48},{24,120},{32,64},{40,8},{48,80},{56,24},{64... | collective-permute-start | bytes 626696 | tf_op jit(solution)/shard_map/ppermute | solution.py:32
  29.0 2.7 %collective-permute-start.7 = (bf16[8,272,128]{2,1,0:T(8,128)(2,1)S(1)}, bf16[8,272,128]{2,1,0:T(8,128)(2,1)S(1)}, u32[]{:S(2)}, u32[]{:S(2)}) collective-permute-start(bf16[8,272,128]{2,1,0:T(8,128)(2,1)S(1)} %shard_map.107), channel_id=1, source_target_pairs={{0,8},{8,0},{16,24},{24,16},{32,40},{40,32},{48,56},{56,48},{64,72... | collective-permute-start | bytes 1671176 | tf_op jit(solution)/shard_map/ppermute | solution.py:32
  29.1 2.5 %collective-permute-start.6 = (bf16[3,272,128]{2,1,0:T(8,128)(2,1)S(1)}, bf16[3,272,128]{2,1,0:T(8,128)(2,1)S(1)}, u32[]{:S(2)}, u32[]{:S(2)}) collective-permute-start(bf16[3,272,128]{2,1,0:T(8,128)(2,1)S(1)} %collective-permute-done.4.refs_3_._), channel_id=1, source_target_pairs={{0,8},{8,0},{16,24},{24,16},{32,40},{40,32},{48,56},{56,48},{64,72... | collective-permute-start | bytes 626696 | tf_op jit(solution)/shard_map/ppermute | solution.py:32
  29.6 7.2 %collective-permute-start.8 = (bf16[3,272,128]{2,1,0:T(8,128)(2,1)S(1)}, bf16[3,272,128]{2,1,0:T(8,128)(2,1)S(1)}, u32[]{:S(2)}, u32[]{:S(2)}) collective-permute-start(bf16[3,272,128]{2,1,0:T(8,128)(2,1)S(1)} %collective-permute-done.4.refs_3_._), channel_id=1, source_target_pairs={{0,128},{8,136},{16,144},{24,152},{32,160},{40,168},{48,176},{56,1... | collective-permute-start | bytes 626696 | tf_op jit(solution)/shard_map/ppermute | solution.py:32
  36.7 1.5 %collective-permute-start.9 = (bf16[3,272,128]{2,1,0:T(8,128)(2,1)S(1)}, bf16[3,272,128]{2,1,0:T(8,128)(2,1)S(1)}, u32[]{:S(2)}, u32[]{:S(2)}) collective-permute-start(bf16[3,272,128]{2,1,0:T(8,128)(2,1)S(1)} %collective-permute-done.8.refs_2_), channel_id=1, source_target_pairs={{0,8},{8,0},{16,24},{24,16},{32,40},{40,32},{48,56},{56,48},{64,72... | collective-permute-start | bytes 626696 | tf_op jit(solution)/shard_map/ppermute | solution.py:32
  39.2 19.4 %copy-start.2 = (bf16[256,512]{1,0:T(8,128)(2,1)S(1)}, bf16[256,512]{1,0:T(8,128)(2,1)}, u32[]{:S(2)}) copy-start(bf16[256,512]{1,0:T(8,128)(2,1)} %cot_ref.1) | copy-start | bytes 786436
  39.2 19.4 %copy-start.3 = (bf16[256,128]{1,0:T(8,128)(2,1)S(1)}, bf16[256,128]{1,0:T(8,128)(2,1)}, u32[]{:S(2)}) copy-start(bf16[256,128]{1,0:T(8,128)(2,1)} %features_ref.1) | copy-start | bytes 196612
  39.2 19.4 %copy-start.5 = (bf16[128,512]{1,0:T(8,128)(2,1)S(1)}, bf16[128,512]{1,0:T(8,128)(2,1)}, u32[]{:S(2)}) copy-start(bf16[128,512]{1,0:T(8,128)(2,1)} %weight_ref.1) | copy-start | bytes 393220
  39.2 19.4 %copy-start.8 = (s32[256]{0:T(256)S(1)}, s32[256]{0:T(256)}, u32[]{:S(2)}) copy-start(s32[256]{0:T(256)} %param.11) | copy-start | bytes 3076
  39.2 19.4 %copy-start.9 = (f32[512]{0:T(512)S(1)}, f32[512]{0:T(512)}, u32[]{:S(2)}) copy-start(f32[512]{0:T(512)} %param.10) | copy-start | bytes 6148
  78.5 2.0 %collective-permute-start.12 = (f16[832,256]{1,0:T(8,128)(2,1)S(1)}, f16[832,256]{1,0:T(8,128)(2,1)S(1)}, u32[]{:S(2)}, u32[]{:S(2)}) collective-permute-start(f16[832,256]{1,0:T(8,128)(2,1)S(1)} %pad_maximum_fusion), channel_id=1, source_target_pairs={{0,8},{8,0},{16,24},{24,16},{32,40},{40,32},{48,56},{56,48},{64,72... | collective-permute-start | bytes 1277960 | tf_op jit(solution)/shard_map/ppermute | solution.py:32
  80.9 8.4 %collective-permute-start.13 = (f16[448,256]{1,0:T(8,128)(2,1)S(1)}, f16[448,256]{1,0:T(8,128)(2,1)S(1)}, u32[]{:S(2)}, u32[]{:S(2)}) collective-permute-start(f16[448,256]{1,0:T(8,128)(2,1)S(1)} %pad_maximum_fusion.1), channel_id=1, source_target_pairs={{0,128},{8,136},{16,144},{24,152},{32,160},{40,168},{48,176},{56,1... | collective-permute-start | bytes 688136 | tf_op jit(solution)/shard_map/ppermute | solution.py:32
  81.5 7.9 %collective-permute-start.15 = (f16[64,256]{1,0:T(8,128)(2,1)S(1)}, f16[64,256]{1,0:T(8,128)(2,1)S(1)}, u32[]{:S(2)}, u32[]{:S(2)}) collective-permute-start(f16[64,256]{1,0:T(8,128)(2,1)S(1)} %convert_element_type.119), channel_id=1, source_target_pairs={{0,144},{8,152},{16,128},{24,136},{32,176},{40,184},{48,160},{56,1... | collective-permute-start | bytes 98312 | tf_op jit(solution)/shard_map/ppermute | solution.py:32
  81.8 7.6 %collective-permute-start.14 = (f16[64,256]{1,0:T(8,128)(2,1)S(1)}, f16[64,256]{1,0:T(8,128)(2,1)S(1)}, u32[]{:S(2)}, u32[]{:S(2)}) collective-permute-start(f16[64,256]{1,0:T(8,128)(2,1)S(1)} %convert_element_type.119), channel_id=1, source_target_pairs={{0,16},{8,24},{16,0},{24,8},{32,48},{40,56},{48,32},{56,40},{64,80... | collective-permute-start | bytes 98312 | tf_op jit(solution)/shard_map/ppermute | solution.py:32
  86.9 3.1 %collective-permute-start.10 = (f16[10,128,256]{2,1,0:T(8,128)(2,1)S(1)}, f16[10,128,256]{2,1,0:T(8,128)(2,1)S(1)}, u32[]{:S(2)}, u32[]{:S(2)}) collective-permute-start(f16[10,128,256]{2,1,0:T(8,128)(2,1)S(1)} %convert_element_type.110), channel_id=1, source_target_pairs={{0,8},{8,0},{16,24},{24,16},{32,40},{40,32},{48,56},{56,48},{64,72... | collective-permute-start | bytes 1966088 | tf_op jit(solution)/shard_map/ppermute | solution.py:32
  89.6 11.6 %collective-permute-start.16 = (f16[448,256]{1,0:T(8,128)(2,1)S(1)}, f16[448,256]{1,0:T(8,128)(2,1)S(1)}, u32[]{:S(2)}, u32[]{:S(2)}) collective-permute-start(f16[448,256]{1,0:T(8,128)(2,1)S(1)} %pad_maximum_fusion.2), channel_id=1, source_target_pairs={{0,32},{8,104},{16,48},{24,120},{32,64},{40,8},{48,80},{56,24},{64... | collective-permute-start | bytes 688136 | tf_op jit(solution)/shard_map/ppermute | solution.py:32
  90.2 11.0 %collective-permute-start.11 = (f16[5,128,256]{2,1,0:T(8,128)(2,1)S(1)}, f16[5,128,256]{2,1,0:T(8,128)(2,1)S(1)}, u32[]{:S(2)}, u32[]{:S(2)}) collective-permute-start(f16[5,128,256]{2,1,0:T(8,128)(2,1)S(1)} %slice_convert_fusion), channel_id=1, source_target_pairs={{0,128},{8,136},{16,144},{24,152},{32,160},{40,168},{48,176},{56,1... | collective-permute-start | bytes 983048 | tf_op jit(solution)/shard_map/ppermute | solution.py:32
  91.0 14.0 %collective-permute-start.20 = (f16[64,256]{1,0:T(8,128)(2,1)S(1)}, f16[64,256]{1,0:T(8,128)(2,1)S(1)}, u32[]{:S(2)}, u32[]{:S(2)}) collective-permute-start(f16[64,256]{1,0:T(8,128)(2,1)S(1)} %convert_element_type.132), channel_id=1, source_target_pairs={{0,64},{8,72},{16,80},{24,88},{32,96},{40,104},{48,112},{56,120},{... | collective-permute-start | bytes 98312 | tf_op jit(solution)/shard_map/ppermute | solution.py:32
  101.5 3.4 %collective-permute-start.21 = (f16[64,256]{1,0:T(8,128)(2,1)S(1)}, f16[64,256]{1,0:T(8,128)(2,1)S(1)}, u32[]{:S(2)}, u32[]{:S(2)}) collective-permute-start(f16[64,256]{1,0:T(8,128)(2,1)S(1)} %convert_element_type.136), channel_id=1, source_target_pairs={{0,8},{8,0},{16,24},{24,16},{32,40},{40,32},{48,56},{56,48},{64,72... | collective-permute-start | bytes 98312 | tf_op jit(solution)/shard_map/ppermute | solution.py:32
  101.6 7.4 %collective-permute-start.18 = (f16[2,128,256]{2,1,0:T(8,128)(2,1)S(1)}, f16[2,128,256]{2,1,0:T(8,128)(2,1)S(1)}, u32[]{:S(2)}, u32[]{:S(2)}) collective-permute-start(f16[2,128,256]{2,1,0:T(8,128)(2,1)S(1)} %fusion.1), channel_id=1, source_target_pairs={{0,16},{8,120},{16,32},{24,8},{32,48},{40,24},{48,64},{56,40},{64,... | collective-permute-start | bytes 393224 | tf_op jit(solution)/shard_map/ppermute | solution.py:32
  101.7 7.3 %collective-permute-start.17 = (f16[2,128,256]{2,1,0:T(8,128)(2,1)S(1)}, f16[2,128,256]{2,1,0:T(8,128)(2,1)S(1)}, u32[]{:S(2)}, u32[]{:S(2)}) collective-permute-start(f16[2,128,256]{2,1,0:T(8,128)(2,1)S(1)} %pad_maximum_fusion.3), channel_id=1, source_target_pairs={{0,32},{8,104},{16,48},{24,120},{32,64},{40,8},{48,80},{56,24},{64... | collective-permute-start | bytes 393224 | tf_op jit(solution)/shard_map/ppermute | solution.py:32
  105.6 9.3 %all-to-all-start.2 = ((f16[4,64,256]{2,1,0:T(8,128)(2,1)}), f16[4,64,256]{2,1,0:T(8,128)(2,1)S(1)}, u32[]{:S(2)}, u32[]{:S(2)}) async-start(f16[4,64,256]{2,1,0:T(8,128)(2,1)} %broadcast_in_dim.5), calls=%async_computation.2 | async-start | bytes 262144 | tf_op jit(solution)/shard_map/all_to_all | solution.py:446
  109.1 5.9 %collective-permute-start.19 = (f16[128,256]{1,0:T(8,128)(2,1)S(1)}, f16[128,256]{1,0:T(8,128)(2,1)S(1)}, u32[]{:S(2)}, u32[]{:S(2)}) collective-permute-start(f16[128,256]{1,0:T(8,128)(2,1)S(1)} %get-tuple-element.97), channel_id=1, source_target_pairs={{0,8},{8,0},{16,24},{24,16},{32,40},{40,32},{48,56},{56,48},{64,72... | collective-permute-start | bytes 196616 | tf_op jit(solution)/shard_map/ppermute | solution.py:32
  (1 other events, 0.7 us)

commit v6 on v4

--- a/solution.py
+++ b/solution.py
@@ -155,11 +155,10 @@
     [[(1, -1, 0), (1, -1, 1), (1, -2, 0), (1, -2, 1)], [(0, -3, 0), (0, -3, 1), (0, 4, 0)]],
     [
         [(dx, i, dc) for dx in (0, 1) for i in (1, 2) for dc in (1, 0)],
-        [(0, 3, 1), (0, 3, 0), (0, 4, 1)],
     ],
     [[(1, -3, 0), (1, -3, 1), (1, 4, 0)]],
 ]
-LAST_ORDER = [[(1, 3, 1), (1, 3, 0), (1, 4, 1)]]
+LAST_ORDER = [[(dx, *rest) for dx in (0, 1) for rest in ((3, 1), (3, 0), (4, 1))]]
 
 
 def middle_kernel(
@@ -310,13 +309,12 @@
     all_near = call(join_kernel, shape((8, BLOCK, TILE), bf16), [VMEM] * 3, cost=1 << 31)(
         near, near_x, far
     )
-    *begun, far_core, near_core = together(
-        *forward(2, *begun, near_x, far),
-        permute_blk(far, to_core),
-        permute_blk(all_near, to_core),
-    )
-    *begun, far_x = together(*forward(3, *begun, near_core, far_core), far_x)
-    return together(*forward(4, *begun, far_x), permute_blk(far_x, to_core))
+    *begun, near_core = together(
+        *forward(2, *begun, near_x, far), permute_blk(all_near, to_core)
+    )
+    *begun, far_x = together(*forward(3, *begun, near_core), far_x)
+    far_core = permute_blk(jnp.concatenate([far, far_x]), to_core)
+    return together(*forward(4, *begun, far_x), far_core)
 
 
 def behind(value, *others):

time: 115 us -> 116 us (level)
    ppermute x22 -> x21, waiting for transfers between devices: 22.9 us -> 23.7 us  [permute_blk(): return lax.ppermute(value, 'blk', pairs)]
    ppermute x22 -> x21, starting transfers between devices: 22.7 us -> 22.4 us  [permute_blk(): return lax.ppermute(value, 'blk', pairs)]
  transfers between devices with their start and end apart: 23 -> 22, of which waited for: 8 -> 8; matrix products, arithmetic and copies ran while one was open for 2% -> 2% of each run, Pallas kernels for 7% -> 7%
where the time goes in v6:
time: 116 us; the launch traced here: 115 us
  blocking collectives  34.4 us (30%)
  waiting for transfers between devices  31.5 us (27%)
  starting transfers between devices  25.8 us (22%)
  Pallas kernels  14.4 us (12%)
  local copies, waits for them, and re-layouts  6.26 us (5%)
  other arithmetic  1.76 us (2%)
  between operations  1.29 us (1%)
    ppermute x21, waiting for transfers between devices, permute_blk(): return lax.ppermute(value, 'blk', pairs)  23.7 us
    ppermute x21, starting transfers between devices, permute_blk(): return lax.ppermute(value, 'blk', pairs)  22.4 us
    all_to_all x1, blocking collectives, per_device(): parts = lax.all_to_all(partial.astype(f16), 'rep', 0, 0).astype(f32)  19.3 us
    all_to_all x1, blocking collectives, per_device(): got = lax.all_to_all(sent, 'rep', 0, 0).astype(f32)  15.1 us
    pallas_call x9, Pallas kernels, products(): call(kernel, outs, ins, scratch, 1 << 29)(place, *smem, tiles, *pieces)  10.2 us
    all_to_all x1, waiting for transfers between devices, per_device(): slices = lax.all_to_all(grad, 'rep', 0, 0).astype(f32)  7.83 us
    unnamed x22, local copies, waits for them, and re-layouts  4.56 us
    all_to_all x1, starting transfers between devices, per_device(): slices = lax.all_to_all(grad, 'rep', 0, 0).astype(f32)  3.37 us
  transfers between devices with their start and end apart: 22, of which 8 were waited for; matrix products, arithmetic and copies ran while one was open for 2% of the time, Pallas kernels for 7%

profile of v6, /device:TPU:32, one launch (start us, length us, event | category | flops | bytes accessed | tf_op | source)
XLA Modules:
  0.0 115.4 jit_solution(8281053097480067782)
XLA Ops:
  0.6 1.9 %shard_map.103 = (bf16[1,272,128]{2,1,0:T(8,128)(2,1)}, bf16[2,272,128]{2,1,0:T(8,128)(2,1)}) custom-call(bf16[256,128]{1,0:T(8,128)(2,1)} %features_ref.1, s32[2,128]{1,0:T(2,128)} %bitcast.44, bf16[256,512]{1,0:T(8,128)(2,1)} %cot_ref.1), custom_call_target="tpu_custom_call" | custom-call | bytes 1048576 | tf_op jit(solution)/shard_map/pallas_call | solution.py:384
  2.6 1.5 %collective-permute-done = bf16[1,272,128]{2,1,0:T(8,128)(2,1)S(1)} collective-permute-done((bf16[1,272,128]{2,1,0:T(8,128)(2,1)}, bf16[1,272,128]{2,1,0:T(8,128)(2,1)S(1)}, u32[]{:S(2)}, u32[]{:S(2)}) %collective-permute-start) | collective-permute-done | bytes 69664 | tf_op jit(solution)/shard_map/ppermute | solution.py:32
  4.7 3.3 %collective-permute-start.1 = (bf16[2,272,128]{2,1,0:T(8,128)(2,1)}, bf16[2,272,128]{2,1,0:T(8,128)(2,1)S(1)}, u32[]{:S(2)}, u32[]{:S(2)}) collective-permute-start(bf16[2,272,128]{2,1,0:T(8,128)(2,1)} %constant_dynamic-update-slice_fusion.2.refs_0_), channel_id=1, source_target_pairs={{0,32},{8,104},{16,48},{24,120},{32,64},{40,8},{48,80},{56,24},{64... | collective-permute-start | bytes 417800 | tf_op jit(solution)/shard_map/ppermute | solution.py:32
  8.0 3.1 %collective-permute-start.2 = (bf16[2,272,128]{2,1,0:T(8,128)(2,1)}, bf16[2,272,128]{2,1,0:T(8,128)(2,1)S(1)}, u32[]{:S(2)}, u32[]{:S(2)}) collective-permute-start(bf16[2,272,128]{2,1,0:T(8,128)(2,1)} %constant_dynamic-update-slice_fusion.2.refs_0_), channel_id=1, source_target_pairs={{0,16},{8,120},{16,32},{24,8},{32,48},{40,24},{48,64},{56,40},{64,... | collective-permute-start | bytes 417800 | tf_op jit(solution)/shard_map/ppermute | solution.py:32
  11.1 1.5 %collective-permute-start.3 = (bf16[2,272,128]{2,1,0:T(8,128)(2,1)}, bf16[2,272,128]{2,1,0:T(8,128)(2,1)S(1)}, u32[]{:S(2)}, u32[]{:S(2)}) collective-permute-start(bf16[2,272,128]{2,1,0:T(8,128)(2,1)} %constant_dynamic-update-slice_fusion.2.refs_0_), channel_id=1, source_target_pairs={{0,128},{8,136},{16,144},{24,152},{32,160},{40,168},{48,176},{56,1... | collective-permute-start | bytes 417800 | tf_op jit(solution)/shard_map/ppermute | solution.py:32
  13.5 2.2 %copy-done = bf16[1,1,64,2,128,128]{5,4,3,2,1,0:T(8,128)(2,1)S(1)} copy-done((bf16[1,1,64,2,128,128]{5,4,3,2,1,0:T(8,128)(2,1)S(1)}, bf16[1,1,64,2,128,128]{5,4,3,2,1,0:T(8,128)(2,1)}, u32[]{:S(2)}) %copy-start) | copy-done | bytes 4194328
  15.7 0.9 copy-done.4
  17.3 0.8 shard_map.104
  18.8 1.6 %collective-permute-start.4 = (bf16[3,272,128]{2,1,0:T(8,128)(2,1)S(1)}, bf16[3,272,128]{2,1,0:T(8,128)(2,1)S(1)}, u32[]{:S(2)}, u32[]{:S(2)}) collective-permute-start(bf16[3,272,128]{2,1,0:T(8,128)(2,1)S(1)} %slice.115), channel_id=1, source_target_pairs={{0,32},{8,104},{16,48},{24,120},{32,64},{40,8},{48,80},{56,24},{64... | collective-permute-start | bytes 626696 | tf_op jit(solution)/shard_map/ppermute | solution.py:32
  20.3 0.9 shard_map.105
  21.3 7.7 %collective-permute-done.4.refs_3_._ = bf16[3,272,128]{2,1,0:T(8,128)(2,1)S(1)} collective-permute-done((bf16[3,272,128]{2,1,0:T(8,128)(2,1)S(1)}, bf16[3,272,128]{2,1,0:T(8,128)(2,1)S(1)}, u32[]{:S(2)}, u32[]{:S(2)}) %collective-permute-start.4) | collective-permute-done | bytes 208928 | tf_op jit(solution)/shard_map/ppermute | solution.py:32
  29.1 1.2 %collective-permute-start.7 = (bf16[3,272,128]{2,1,0:T(8,128)(2,1)S(1)}, bf16[3,272,128]{2,1,0:T(8,128)(2,1)S(1)}, u32[]{:S(2)}, u32[]{:S(2)}) collective-permute-start(bf16[3,272,128]{2,1,0:T(8,128)(2,1)S(1)} %collective-permute-done.4.refs_3_._), channel_id=1, source_target_pairs={{0,128},{8,136},{16,144},{24,152},{32,160},{40,168},{48,176},{56,1... | collective-permute-start | bytes 626696 | tf_op jit(solution)/shard_map/ppermute | solution.py:32
  30.2 1.0 shard_map.106
  31.2 1.0 shard_map.108
  32.2 4.4 %collective-permute-done.7.refs_2_ = bf16[3,272,128]{2,1,0:T(8,128)(2,1)S(1)} collective-permute-done((bf16[3,272,128]{2,1,0:T(8,128)(2,1)S(1)}, bf16[3,272,128]{2,1,0:T(8,128)(2,1)S(1)}, u32[]{:S(2)}, u32[]{:S(2)}) %collective-permute-start.7) | collective-permute-done | bytes 208928 | tf_op jit(solution)/shard_map/ppermute | solution.py:32
  36.8 0.8 shard_map.109
  37.6 0.9 collective-permute-done.8.refs_0_
  38.5 1.0 shard_map.110
  39.7 19.3 %all_to_all.15 = f16[8,272,128]{2,1,0:T(8,128)(2,1)S(1)} all-to-all(f16[8,272,128]{2,1,0:T(8,128)(2,1)S(1)} %convert_element_type.107), channel_id=1, replica_groups=mesh['blk'=32,'rep'=8] {'rep'}, dimensions={0} | all-to-all | bytes 1114112 | tf_op jit(solution)/shard_map/all_to_all | solution.py:415
  59.1 1.4 %shard_map.111 = (bf16[256,512]{1,0:T(8,128)(2,1)}, f32[128,256]{1,0:T(8,128)S(1)}, f32[8,32,256]{2,1,0:T(8,128)S(1)}, f32[2,8,128]{2,1,0:T(8,128)S(1)}) custom-call(f32[8,272,128]{2,1,0:T(8,128)S(1)} %convert_element_type.108.parts_ref, bf16[128,512]{1,0:T(8,128)(2,1)S(1)} %copy-done.5, f32[1,512]{1,0:T(1,128)S(1)} %bitcast.47, s32[2,128]{1,0:T(2,128)S(1)} %bitcast.45, ...), custom_call_target="tpu_custom_call" | custom-call | flops 134217728 | bytes 1048576 | tf_op jit(solution)/shard_map/pallas_call | solution.py:416
  60.8 15.1 %all_to_all.16 = f16[8,160,256]{2,1,0:T(8,128)(2,1)S(1)} all-to-all(f16[8,160,256]{2,1,0:T(8,128)(2,1)S(1)} %pad_maximum_fusion), channel_id=1, replica_groups=mesh['blk'=32,'rep'=8] {'rep'}, dimensions={0} | all-to-all | bytes 1310720 | tf_op jit(solution)/shard_map/all_to_all | solution.py:429
  76.1 1.2 %shard_map.114 = f32[6,128,256]{2,1,0:T(8,128)S(1)} custom-call(s32[1]{0:T(128)} %bitcast.place_ref, s32[128]{0:T(128)S(1)} %reshape.59.rows_ref, s32[64]{0:T(128)S(1)} %bitcast.41, bf16[64,256,128]{2,1,0:T(8,128)(2,1)S(1)} %bitcast.32, f32[8,128,256]{2,1,0:T(8,128)S(1)} %slice.116.back_ref), custom_call_target="tpu_custom_call" | custom-call | flops 536870912 | bytes 1048576 | tf_op jit(solution)/shard_map/pallas_call | solution.py:403
  77.8 1.2 %shard_map.113 = f32[6,128,256]{2,1,0:T(8,128)S(1)} custom-call(s32[1]{0:T(128)} %bitcast.place_ref, s32[128]{0:T(128)S(1)} %reshape.59.rows_ref, s32[64]{0:T(128)S(1)} %bitcast.42, bf16[64,256,128]{2,1,0:T(8,128)(2,1)S(1)} %bitcast.33, f32[8,128,256]{2,1,0:T(8,128)S(1)} %slice.116.back_ref), custom_call_target="tpu_custom_call" | custom-call | flops 536870912 | bytes 1048576 | tf_op jit(solution)/shard_map/pallas_call | solution.py:403
  80.8 2.7 %collective-permute-start.13 = (f16[32,256]{1,0:T(8,128)(2,1)S(1)}, f16[32,256]{1,0:T(8,128)(2,1)S(1)}, u32[]{:S(2)}, u32[]{:S(2)}) collective-permute-start(f16[32,256]{1,0:T(8,128)(2,1)S(1)} %convert_element_type.119), channel_id=1, source_target_pairs={{0,16},{8,24},{16,0},{24,8},{32,48},{40,56},{48,32},{56,40},{64,80... | collective-permute-start | bytes 49160 | tf_op jit(solution)/shard_map/ppermute | solution.py:32
  83.5 2.2 %shard_map.112 = (f32[10,128,256]{2,1,0:T(8,128)S(1)}, f32[10,128,256]{2,1,0:T(8,128)S(1)}) custom-call(s32[1]{0:T(128)} %bitcast.place_ref, s32[128]{0:T(128)S(1)} %reshape.59.rows_ref, s32[64]{0:T(128)S(1)} %bitcast.43, bf16[64,256,128]{2,1,0:T(8,128)(2,1)S(1)} %bitcast.34, f32[8,128,256]{2,1,0:T(8,128)S(1)} %slice.116.back_ref), custom_call_target="tpu_custom_call" | custom-call | flops 536870912 | bytes 1048576 | tf_op jit(solution)/shard_map/pallas_call | solution.py:403
  86.0 1.6 %collective-permute-done.12 = f16[416,256]{1,0:T(8,128)(2,1)S(1)} collective-permute-done((f16[416,256]{1,0:T(8,128)(2,1)S(1)}, f16[416,256]{1,0:T(8,128)(2,1)S(1)}, u32[]{:S(2)}, u32[]{:S(2)}) %collective-permute-start.12) | collective-permute-done | bytes 213024 | tf_op jit(solution)/shard_map/ppermute | solution.py:32
  89.3 2.0 %collective-permute-start.19 = (f16[32,256]{1,0:T(8,128)(2,1)S(1)}, f16[32,256]{1,0:T(8,128)(2,1)S(1)}, u32[]{:S(2)}, u32[]{:S(2)}) collective-permute-start(f16[32,256]{1,0:T(8,128)(2,1)S(1)} %convert_element_type.132), channel_id=1, source_target_pairs={{0,64},{8,72},{16,80},{24,88},{32,96},{40,104},{48,112},{56,120},{... | collective-permute-start | bytes 49160 | tf_op jit(solution)/shard_map/ppermute | solution.py:32
  91.3 7.1 %collective-permute-done.15 = f16[416,256]{1,0:T(8,128)(2,1)S(1)} collective-permute-done((f16[416,256]{1,0:T(8,128)(2,1)S(1)}, f16[416,256]{1,0:T(8,128)(2,1)S(1)}, u32[]{:S(2)}, u32[]{:S(2)}) %collective-permute-start.15) | collective-permute-done | bytes 213024 | tf_op jit(solution)/shard_map/ppermute | solution.py:32
  99.0 3.3 %collective-permute-start.16 = (f16[2,128,256]{2,1,0:T(8,128)(2,1)S(1)}, f16[2,128,256]{2,1,0:T(8,128)(2,1)S(1)}, u32[]{:S(2)}, u32[]{:S(2)}) collective-permute-start(f16[2,128,256]{2,1,0:T(8,128)(2,1)S(1)} %pad_maximum_fusion.5), channel_id=1, source_target_pairs={{0,32},{8,104},{16,48},{24,120},{32,64},{40,8},{48,80},{56,24},{64... | collective-permute-start | bytes 393224 | tf_op jit(solution)/shard_map/ppermute | solution.py:32
  103.0 3.4 %all-to-all-start.2 = ((f16[8,32,256]{2,1,0:T(8,128)(2,1)}), f16[8,32,256]{2,1,0:T(8,128)(2,1)S(1)}, u32[]{:S(2)}, u32[]{:S(2)}) async-start(f16[8,32,256]{2,1,0:T(8,128)(2,1)} %broadcast_in_dim.5), calls=%async_computation.2 | async-start | bytes 262144 | tf_op jit(solution)/shard_map/all_to_all | solution.py:441
  106.6 7.8 %all-to-all-done.2 = f16[8,32,256]{2,1,0:T(8,128)(2,1)S(1)} async-done(((f16[8,32,256]{2,1,0:T(8,128)(2,1)}), f16[8,32,256]{2,1,0:T(8,128)(2,1)S(1)}, u32[]{:S(2)}, u32[]{:S(2)}) %all-to-all-start.2) | async-done | bytes 131104 | tf_op jit(solution)/shard_map/all_to_all | solution.py:441
  114.5 0.9 shard_map.118
  (104 shorter events, 9.2 us)
Async XLA Ops:
  2.5 1.6 %collective-permute-start = (bf16[1,272,128]{2,1,0:T(8,128)(2,1)}, bf16[1,272,128]{2,1,0:T(8,128)(2,1)S(1)}, u32[]{:S(2)}, u32[]{:S(2)}) collective-permute-start(bf16[1,272,128]{2,1,0:T(8,128)(2,1)} %get-tuple-element.46), channel_id=1, source_target_pairs={{0,8},{8,0},{16,24},{24,16},{32,40},{40,32},{48,56},{56,48},{64,72... | collective-permute-start | bytes 208904 | tf_op jit(solution)/shard_map/ppermute | solution.py:32
  4.7 13.3 %collective-permute-start.1 = (bf16[2,272,128]{2,1,0:T(8,128)(2,1)}, bf16[2,272,128]{2,1,0:T(8,128)(2,1)S(1)}, u32[]{:S(2)}, u32[]{:S(2)}) collective-permute-start(bf16[2,272,128]{2,1,0:T(8,128)(2,1)} %constant_dynamic-update-slice_fusion.2.refs_0_), channel_id=1, source_target_pairs={{0,32},{8,104},{16,48},{24,120},{32,64},{40,8},{48,80},{56,24},{64... | collective-permute-start | bytes 417800 | tf_op jit(solution)/shard_map/ppermute | solution.py:32
  8.0 10.1 %collective-permute-start.2 = (bf16[2,272,128]{2,1,0:T(8,128)(2,1)}, bf16[2,272,128]{2,1,0:T(8,128)(2,1)S(1)}, u32[]{:S(2)}, u32[]{:S(2)}) collective-permute-start(bf16[2,272,128]{2,1,0:T(8,128)(2,1)} %constant_dynamic-update-slice_fusion.2.refs_0_), channel_id=1, source_target_pairs={{0,16},{8,120},{16,32},{24,8},{32,48},{40,24},{48,64},{56,40},{64,... | collective-permute-start | bytes 417800 | tf_op jit(solution)/shard_map/ppermute | solution.py:32
  11.1 7.0 %collective-permute-start.3 = (bf16[2,272,128]{2,1,0:T(8,128)(2,1)}, bf16[2,272,128]{2,1,0:T(8,128)(2,1)S(1)}, u32[]{:S(2)}, u32[]{:S(2)}) collective-permute-start(bf16[2,272,128]{2,1,0:T(8,128)(2,1)} %constant_dynamic-update-slice_fusion.2.refs_0_), channel_id=1, source_target_pairs={{0,128},{8,136},{16,144},{24,152},{32,160},{40,168},{48,176},{56,1... | collective-permute-start | bytes 417800 | tf_op jit(solution)/shard_map/ppermute | solution.py:32
  13.5 2.2 %copy-start = (bf16[1,1,64,2,128,128]{5,4,3,2,1,0:T(8,128)(2,1)S(1)}, bf16[1,1,64,2,128,128]{5,4,3,2,1,0:T(8,128)(2,1)}, u32[]{:S(2)}) copy-start(bf16[1,1,64,2,128,128]{5,4,3,2,1,0:T(8,128)(2,1)} %param.12) | copy-start | bytes 12582916
  15.7 0.9 copy-start.4
  16.6 0.7 copy-start.6
  17.3 3.1 %copy-start.1 = (bf16[1,1,64,2,128,128]{5,4,3,2,1,0:T(8,128)(2,1)S(1)}, bf16[1,1,64,2,128,128]{5,4,3,2,1,0:T(8,128)(2,1)}, u32[]{:S(2)}) copy-start(bf16[1,1,64,2,128,128]{5,4,3,2,1,0:T(8,128)(2,1)} %param.12) | copy-start | bytes 12582916
  17.3 3.1 %copy-start.7 = (s32[1,1,64]{2,1,0:T(1,128)S(1)}, s32[1,1,64]{2,1,0:T(1,128)}, u32[]{:S(2)}) copy-start(s32[1,1,64]{2,1,0:T(1,128)} %param.14) | copy-start | bytes 772
  18.1 10.8 %collective-permute-start.5 = (bf16[4,272,128]{2,1,0:T(8,128)(2,1)S(1)}, bf16[4,272,128]{2,1,0:T(8,128)(2,1)S(1)}, u32[]{:S(2)}, u32[]{:S(2)}) collective-permute-start(bf16[4,272,128]{2,1,0:T(8,128)(2,1)S(1)} %constant_dynamic-update-slice_fusion.refs_3_.first_ref), channel_id=1, source_target_pairs={{0,128},{8,136},{16,144},{24,152},{32,160},{40,168},{48,176},{56,1... | collective-permute-start | bytes 835592 | tf_op jit(solution)/shard_map/ppermute | solution.py:32
  18.8 10.2 %collective-permute-start.4 = (bf16[3,272,128]{2,1,0:T(8,128)(2,1)S(1)}, bf16[3,272,128]{2,1,0:T(8,128)(2,1)S(1)}, u32[]{:S(2)}, u32[]{:S(2)}) collective-permute-start(bf16[3,272,128]{2,1,0:T(8,128)(2,1)S(1)} %slice.115), channel_id=1, source_target_pairs={{0,32},{8,104},{16,48},{24,120},{32,64},{40,8},{48,80},{56,24},{64... | collective-permute-start | bytes 626696 | tf_op jit(solution)/shard_map/ppermute | solution.py:32
  29.0 2.2 %collective-permute-start.6 = (bf16[8,272,128]{2,1,0:T(8,128)(2,1)S(1)}, bf16[8,272,128]{2,1,0:T(8,128)(2,1)S(1)}, u32[]{:S(2)}, u32[]{:S(2)}) collective-permute-start(bf16[8,272,128]{2,1,0:T(8,128)(2,1)S(1)} %shard_map.107), channel_id=1, source_target_pairs={{0,8},{8,0},{16,24},{24,16},{32,40},{40,32},{48,56},{56,48},{64,72... | collective-permute-start | bytes 1671176 | tf_op jit(solution)/shard_map/ppermute | solution.py:32
  29.1 7.6 %collective-permute-start.7 = (bf16[3,272,128]{2,1,0:T(8,128)(2,1)S(1)}, bf16[3,272,128]{2,1,0:T(8,128)(2,1)S(1)}, u32[]{:S(2)}, u32[]{:S(2)}) collective-permute-start(bf16[3,272,128]{2,1,0:T(8,128)(2,1)S(1)} %collective-permute-done.4.refs_3_._), channel_id=1, source_target_pairs={{0,128},{8,136},{16,144},{24,152},{32,160},{40,168},{48,176},{56,1... | collective-permute-start | bytes 626696 | tf_op jit(solution)/shard_map/ppermute | solution.py:32
  36.7 1.8 %collective-permute-start.8 = (bf16[6,272,128]{2,1,0:T(8,128)(2,1)S(1)}, bf16[6,272,128]{2,1,0:T(8,128)(2,1)S(1)}, u32[]{:S(2)}, u32[]{:S(2)}) collective-permute-start(bf16[6,272,128]{2,1,0:T(8,128)(2,1)S(1)} %pad_maximum_fusion.1), channel_id=1, source_target_pairs={{0,8},{8,0},{16,24},{24,16},{32,40},{40,32},{48,56},{56,48},{64,72... | collective-permute-start | bytes 1253384 | tf_op jit(solution)/shard_map/ppermute | solution.py:32
  39.6 19.4 %copy-start.2 = (bf16[256,512]{1,0:T(8,128)(2,1)S(1)}, bf16[256,512]{1,0:T(8,128)(2,1)}, u32[]{:S(2)}) copy-start(bf16[256,512]{1,0:T(8,128)(2,1)} %cot_ref.1) | copy-start | bytes 786436
  39.6 19.4 %copy-start.3 = (bf16[256,128]{1,0:T(8,128)(2,1)S(1)}, bf16[256,128]{1,0:T(8,128)(2,1)}, u32[]{:S(2)}) copy-start(bf16[256,128]{1,0:T(8,128)(2,1)} %features_ref.1) | copy-start | bytes 196612
  39.6 19.4 %copy-start.5 = (bf16[128,512]{1,0:T(8,128)(2,1)S(1)}, bf16[128,512]{1,0:T(8,128)(2,1)}, u32[]{:S(2)}) copy-start(bf16[128,512]{1,0:T(8,128)(2,1)} %weight_ref.1) | copy-start | bytes 393220
  39.7 19.4 %copy-start.8 = (s32[256]{0:T(256)S(1)}, s32[256]{0:T(256)}, u32[]{:S(2)}) copy-start(s32[256]{0:T(256)} %param.11) | copy-start | bytes 3076
  39.7 19.4 %copy-start.9 = (f32[512]{0:T(512)S(1)}, f32[512]{0:T(512)}, u32[]{:S(2)}) copy-start(f32[512]{0:T(512)} %param.10) | copy-start | bytes 6148
  77.5 2.0 %collective-permute-start.11 = (f16[800,256]{1,0:T(8,128)(2,1)S(1)}, f16[800,256]{1,0:T(8,128)(2,1)S(1)}, u32[]{:S(2)}, u32[]{:S(2)}) collective-permute-start(f16[800,256]{1,0:T(8,128)(2,1)S(1)} %pad_maximum_fusion.2), channel_id=1, source_target_pairs={{0,8},{8,0},{16,24},{24,16},{32,40},{40,32},{48,56},{56,48},{64,72... | collective-permute-start | bytes 1228808 | tf_op jit(solution)/shard_map/ppermute | solution.py:32
  79.9 7.7 %collective-permute-start.12 = (f16[416,256]{1,0:T(8,128)(2,1)S(1)}, f16[416,256]{1,0:T(8,128)(2,1)S(1)}, u32[]{:S(2)}, u32[]{:S(2)}) collective-permute-start(f16[416,256]{1,0:T(8,128)(2,1)S(1)} %pad_maximum_fusion.3), channel_id=1, source_target_pairs={{0,128},{8,136},{16,144},{24,152},{32,160},{40,168},{48,176},{56,1... | collective-permute-start | bytes 638984 | tf_op jit(solution)/shard_map/ppermute | solution.py:32
  80.5 7.1 %collective-permute-start.14 = (f16[32,256]{1,0:T(8,128)(2,1)S(1)}, f16[32,256]{1,0:T(8,128)(2,1)S(1)}, u32[]{:S(2)}, u32[]{:S(2)}) collective-permute-start(f16[32,256]{1,0:T(8,128)(2,1)S(1)} %convert_element_type.119), channel_id=1, source_target_pairs={{0,144},{8,152},{16,128},{24,136},{32,176},{40,184},{48,160},{56,1... | collective-permute-start | bytes 49160 | tf_op jit(solution)/shard_map/ppermute | solution.py:32
  80.8 6.8 %collective-permute-start.13 = (f16[32,256]{1,0:T(8,128)(2,1)S(1)}, f16[32,256]{1,0:T(8,128)(2,1)S(1)}, u32[]{:S(2)}, u32[]{:S(2)}) collective-permute-start(f16[32,256]{1,0:T(8,128)(2,1)S(1)} %convert_element_type.119), channel_id=1, source_target_pairs={{0,16},{8,24},{16,0},{24,8},{32,48},{40,56},{48,32},{56,40},{64,80... | collective-permute-start | bytes 49160 | tf_op jit(solution)/shard_map/ppermute | solution.py:32
  85.9 2.4 %collective-permute-start.9 = (f16[10,128,256]{2,1,0:T(8,128)(2,1)S(1)}, f16[10,128,256]{2,1,0:T(8,128)(2,1)S(1)}, u32[]{:S(2)}, u32[]{:S(2)}) collective-permute-start(f16[10,128,256]{2,1,0:T(8,128)(2,1)S(1)} %convert_element_type.110), channel_id=1, source_target_pairs={{0,8},{8,0},{16,24},{24,16},{32,40},{40,32},{48,56},{56,48},{64,72... | collective-permute-start | bytes 1966088 | tf_op jit(solution)/shard_map/ppermute | solution.py:32
  87.8 10.5 %collective-permute-start.15 = (f16[416,256]{1,0:T(8,128)(2,1)S(1)}, f16[416,256]{1,0:T(8,128)(2,1)S(1)}, u32[]{:S(2)}, u32[]{:S(2)}) collective-permute-start(f16[416,256]{1,0:T(8,128)(2,1)S(1)} %pad_maximum_fusion.4), channel_id=1, source_target_pairs={{0,32},{8,104},{16,48},{24,120},{32,64},{40,8},{48,80},{56,24},{64... | collective-permute-start | bytes 638984 | tf_op jit(solution)/shard_map/ppermute | solution.py:32
  88.5 9.9 %collective-permute-start.10 = (f16[5,128,256]{2,1,0:T(8,128)(2,1)S(1)}, f16[5,128,256]{2,1,0:T(8,128)(2,1)S(1)}, u32[]{:S(2)}, u32[]{:S(2)}) collective-permute-start(f16[5,128,256]{2,1,0:T(8,128)(2,1)S(1)} %slice_convert_fusion), channel_id=1, source_target_pairs={{0,128},{8,136},{16,144},{24,152},{32,160},{40,168},{48,176},{56,1... | collective-permute-start | bytes 983048 | tf_op jit(solution)/shard_map/ppermute | solution.py:32
  89.3 13.0 %collective-permute-start.19 = (f16[32,256]{1,0:T(8,128)(2,1)S(1)}, f16[32,256]{1,0:T(8,128)(2,1)S(1)}, u32[]{:S(2)}, u32[]{:S(2)}) collective-permute-start(f16[32,256]{1,0:T(8,128)(2,1)S(1)} %convert_element_type.132), channel_id=1, source_target_pairs={{0,64},{8,72},{16,80},{24,88},{32,96},{40,104},{48,112},{56,120},{... | collective-permute-start | bytes 49160 | tf_op jit(solution)/shard_map/ppermute | solution.py:32
  98.7 3.6 %collective-permute-start.20 = (f16[32,256]{1,0:T(8,128)(2,1)S(1)}, f16[32,256]{1,0:T(8,128)(2,1)S(1)}, u32[]{:S(2)}, u32[]{:S(2)}) collective-permute-start(f16[32,256]{1,0:T(8,128)(2,1)S(1)} %convert_element_type.136), channel_id=1, source_target_pairs={{0,8},{8,0},{16,24},{24,16},{32,40},{40,32},{48,56},{56,48},{64,72... | collective-permute-start | bytes 49160 | tf_op jit(solution)/shard_map/ppermute | solution.py:32
  98.8 7.6 %collective-permute-start.17 = (f16[2,128,256]{2,1,0:T(8,128)(2,1)S(1)}, f16[2,128,256]{2,1,0:T(8,128)(2,1)S(1)}, u32[]{:S(2)}, u32[]{:S(2)}) collective-permute-start(f16[2,128,256]{2,1,0:T(8,128)(2,1)S(1)} %fusion.1), channel_id=1, source_target_pairs={{0,16},{8,120},{16,32},{24,8},{32,48},{40,24},{48,64},{56,40},{64,... | collective-permute-start | bytes 393224 | tf_op jit(solution)/shard_map/ppermute | solution.py:32
  99.0 7.4 %collective-permute-start.16 = (f16[2,128,256]{2,1,0:T(8,128)(2,1)S(1)}, f16[2,128,256]{2,1,0:T(8,128)(2,1)S(1)}, u32[]{:S(2)}, u32[]{:S(2)}) collective-permute-start(f16[2,128,256]{2,1,0:T(8,128)(2,1)S(1)} %pad_maximum_fusion.5), channel_id=1, source_target_pairs={{0,32},{8,104},{16,48},{24,120},{32,64},{40,8},{48,80},{56,24},{64... | collective-permute-start | bytes 393224 | tf_op jit(solution)/shard_map/ppermute | solution.py:32
  103.0 11.4 %all-to-all-start.2 = ((f16[8,32,256]{2,1,0:T(8,128)(2,1)}), f16[8,32,256]{2,1,0:T(8,128)(2,1)S(1)}, u32[]{:S(2)}, u32[]{:S(2)}) async-start(f16[8,32,256]{2,1,0:T(8,128)(2,1)} %broadcast_in_dim.5), calls=%async_computation.2 | async-start | bytes 262144 | tf_op jit(solution)/shard_map/all_to_all | solution.py:441
  106.5 8.0 %collective-permute-start.18 = (f16[128,256]{1,0:T(8,128)(2,1)S(1)}, f16[128,256]{1,0:T(8,128)(2,1)S(1)}, u32[]{:S(2)}, u32[]{:S(2)}) collective-permute-start(f16[128,256]{1,0:T(8,128)(2,1)S(1)} %get-tuple-element.95), channel_id=1, source_target_pairs={{0,8},{8,0},{16,24},{24,16},{32,40},{40,32},{48,56},{56,48},{64,72... | collective-permute-start | bytes 196616 | tf_op jit(solution)/shard_map/ppermute | solution.py:32
